TPU v7x, 1024 devices: a whole 4x8x16 slice. The times are simulated.
1024 devices in a mesh: pipe: 4 (over y_hi), dp: 256 (over y_lo, z, x, core).
Axes of the slice: x: 4, y: 8 (y_hi: 4, y_lo: 2; y = y_hi * 2 + y_lo), z: 16, core: 2. Of those that a mesh axis runs over, the one named last changes fastest.
Arguments:
- top_grad: bfloat16 [32768, 8192], P('dp'), may hold values from -6 to 6
- slab_inputs: bfloat16 [4, 32768, 128], P('pipe', 'dp'), may hold values from -24 to 24
- weights: bfloat16 [4, 128, 8192], P('pipe'), may hold values from -0.0625 to 0.0625
- master: float32 [4, 8192, 128], P('pipe', 'dp'), may hold values from -0.01953125 to 0.01953125
- moment1: float32 [4, 8192, 128], P('pipe', 'dp'), may hold values from -0.00048828125 to 0.00048828125
- moment2: float32 [4, 8192, 128], P('pipe', 'dp'), may hold values from 1.1920929e-09 to 3.576279e-08
- grad_accum: float32 [4, 8192, 128], P('pipe', 'dp'), may hold values from -0.078125 to 0.078125
- layer_counts: int32 [4], replicated, may hold values from 4 to 36
Outputs:
- new_weights: bfloat16 [4, 128, 8192], P('pipe')
- adam_step: float32 [4, 8192, 128], P('pipe', 'dp')
- new_master: float32 [4, 8192, 128], P('pipe', 'dp')
- section_grads: bfloat16 [4, 32768, 128], P('pipe', 'dp')
All inputs are finite; a program needn't handle non-finite values.
Results may differ from a plain program's by a relative error of at most 0.0027.
Values may be sent and summed in bfloat16 or wider, within the bound.
No kernel may reach another device: no remote copies, remote signals or barrier semaphores. Data moves between devices by JAX's collectives and lax.ppermute only.
A program may use at most 32 MiB of HBM per device.

v0:
```python
import jax
import jax.numpy as jnp
from jax import lax
from jax.sharding import PartitionSpec as P

beta_one = 0.9
beta_two = 0.95
bias_one = 1.0 - 0.9**20
bias_two = 1.0 - 0.95**20
epsilon = 1e-08
decay_rate = 0.1
learn_rate = 0.0003
clip_norm = 1.0


def shifted(x, axis, by):
    size = lax.axis_size(axis)
    pairs = [(i, i + by) for i in range(size) if 0 <= i + by < size]
    return lax.ppermute(x, axis, pairs)


def local(top_grad, slab_inputs, weights, master, moment1, moment2, grad_accum, layer_counts):
    sections = lax.axis_size("pipe")
    section = lax.axis_index("pipe")
    token_rows = top_grad.shape[0]
    model_width = top_grad.shape[1]
    tokens_all = token_rows * lax.axis_size("dp")
    slab_rows = slab_inputs.shape[2]
    span_cols = sections * slab_rows
    inputs_here = slab_inputs[0]
    weight_here = weights[0]
    shard_rows = master.shape[1]
    lanes_count = master.shape[2]
    top_head = top_grad[:, :span_cols].astype(jnp.float32)
    weight_head = weight_here[:, :span_cols]
    tail_part = lax.dot_general(
        top_grad[:, span_cols:],
        weight_here[:, span_cols:],
        (((1,), (1,)), ((), ())),
        preferred_element_type=jnp.float32,
    )

    def head_of(placed):
        return (top_head + placed.astype(jnp.float32)).astype(jnp.bfloat16)

    def branch_of(head_cols):
        product = lax.dot_general(
            head_cols, weight_head, (((1,), (1,)), ((), ())), preferred_element_type=jnp.float32
        )
        return (product + tail_part).astype(jnp.bfloat16)

    placed = jnp.zeros((token_rows, span_cols), jnp.bfloat16)
    for turn_index in range(sections - 1):
        sent_stack = lax.dynamic_update_slice(
            placed, branch_of(head_of(placed)), (0, section * slab_rows)
        )
        placed = shifted(sent_stack, "pipe", -1)
    head_final = head_of(placed)
    section_grad = branch_of(head_final)
    residual = jnp.concatenate([head_final, top_grad[:, span_cols:]], axis=1)
    per_row = model_width // lanes_count
    cover_rows = min(slab_rows, (shard_rows * lax.axis_size("dp") + per_row - 1) // per_row + 1)
    product = lax.dot_general(
        inputs_here, residual, (((0,), (0,)), ((), ())), preferred_element_type=jnp.float32
    )
    product = product.reshape(cover_rows * per_row, lanes_count)
    summed = lax.psum_scatter(product, "dp", scatter_dimension=0, tiled=True)
    total_grad = grad_accum[0] + summed / tokens_all
    local_square = layer_counts.astype(jnp.float32)[section] * jnp.sum(total_grad * total_grad)
    square_norm = lax.psum(local_square, ("pipe", "dp"))
    clip_factor = jnp.minimum(1.0, clip_norm / jnp.sqrt(square_norm))
    clipped = clip_factor * total_grad
    moment_one = beta_one * moment1[0] + (1.0 - beta_one) * clipped
    moment_two = beta_two * moment2[0] + (1.0 - beta_two) * clipped * clipped
    adam_step = (
        moment_one / bias_one / (jnp.sqrt(moment_two / bias_two) + epsilon) + decay_rate * master[0]
    )
    new_master = master[0] - learn_rate * adam_step
    gathered = lax.all_gather(new_master.astype(jnp.bfloat16)[None], "dp", axis=1, tiled=True)
    new_weights = gathered.reshape(1, slab_rows, model_width)
    return (new_weights, adam_step[None], new_master[None], section_grad[None])


def solution(mesh):
    return jax.shard_map(
        local,
        mesh=mesh,
        in_specs=(
            P("dp", None),
            P("pipe", "dp", None),
            P("pipe", None, None),
            P("pipe", "dp", None),
            P("pipe", "dp", None),
            P("pipe", "dp", None),
            P("pipe", "dp", None),
            P(),
        ),
        out_specs=(
            P("pipe", None, None),
            P("pipe", "dp", None),
            P("pipe", "dp", None),
            P("pipe", "dp", None),
        ),
        check_vma=False,
    )
```

profile of v0, /device:TPU:1, one launch (start us, length us, event | category | flops | bytes accessed | tf_op | source)
XLA Modules:
  0.0 1736.5 jit_solution(3799831611965219031)
XLA Ops:
  7.2 0.0 copy-start
  7.2 0.0 reduce-scatter.2.cloned.1.call-start
  7.2 0.0 copy-start.1
  7.2 3.0 fusion.3
  10.2 0.0 copy-done.1
  10.2 1.1 fusion.6
  11.3 1.3 collective-permute-start
  12.6 8.4 collective-permute-done
  21.0 1.1 fusion.8
  22.2 1.3 collective-permute-start.1
  23.5 10.4 collective-permute-done.1
  33.9 1.1 fusion.10
  35.0 0.0 slice-start
  35.1 1.4 collective-permute-start.2
  36.5 6.0 collective-permute-done.2
  42.5 0.0 copy-done
  42.5 0.0 slice-done
  42.6 2.7 convolution_bitcast_fusion
  45.3 5.6 copy.12
  50.9 4.9 reshape.18
  55.8 0.0 copy-start.7
  55.8 0.0 copy-start.2
  55.8 0.0 copy-start.3
  55.8 0.0 copy-start.5
  55.8 0.0 copy-start.6
  55.8 0.0 reduce-scatter.2.cloned.1.call-update
  55.9 0.0 all-gather.3.cloned.1.call-start
  55.9 0.6 copy-done.7
  56.5 0.6 dynamic_slice.3
  57.1 1132.8 %reduce-scatter.2.cloned.1.call-done = f32[32,128]{1,0:T(8,128)} async-done(((f32[8192,128]{1,0:T(8,128)}), f32[32,128]{1,0:T(8,128)}) %reduce-scatter.2.cloned.1.call-update) | async-done | bytes 16400 | tf_op jit(solution)/shard_map/reduce_scatter | solution.py:67
  1189.8 0.0 copy-done.2
  1189.8 1.3 multiply_reduce_fusion
  1192.5 122.5 %psum.7 = f32[]{:T(128)} all-reduce(f32[]{:T(128)S(6)} %mul.61), channel_id=1, replica_groups=mesh['pipe'=4,'dp'=256] {'pipe','dp'}, use_global_device_ids=true, to_apply=%region_2.0 | all-reduce | flops 1 | bytes 8 | tf_op jit(solution)/shard_map/psum | solution.py:70
  1315.7 0.0 copy-done.3
  1315.7 0.0 copy-done.5
  1315.7 0.0 copy-done.6
  1315.7 1.4 fusion.29
  1317.1 0.0 copy-start.4
  1317.1 0.6 fusion.30
  1317.7 0.0 all-gather.3.cloned.1.call-update
  1317.7 1.7 fusion.12
  1319.4 406.1 %all-gather.3.cloned.1.call-done = bf16[8192,128]{1,0:T(8,128)(2,1)} async-done(((bf16[32,128]{1,0:T(8,128)(2,1)}), bf16[8192,128]{1,0:T(8,128)(2,1)}) %all-gather.3.cloned.1.call-update) | async-done | bytes 2097168 | tf_op jit(solution)/shard_map/all_gather | solution.py:79
  1725.5 4.2 reshape.19
  1729.7 0.0 copy-done.4
  (5 shorter events, 0.1 us)
Async XLA Ops:
  7.2 35.4 %copy-start = (bf16[1,128,128]{2,1,0:T(8,128)(2,1)S(1)}, bf16[1,128,128]{2,1,0:T(8,128)(2,1)}, u32[]{:S(2)}) copy-start(bf16[1,128,128]{2,1,0:T(8,128)(2,1)} %param.9) | copy-start | bytes 98308
  7.2 1182.7 %reduce-scatter.2.cloned.1.call-start = ((), (), s32[]{:S(2)}) async-start(), calls=%async_computation.1 | async-start | bytes 4210688 | tf_op jit(solution)/shard_map/reduce_scatter | solution.py:67
  7.2 3.0 copy-start.1
  11.3 9.7 collective-permute-start
  22.2 11.7 collective-permute-start.1
  35.0 7.5 slice-start
  35.1 7.4 collective-permute-start.2
  55.8 0.7 copy-start.7
  55.8 1134.0 %copy-start.2 = (f32[1,32,128]{2,1,0:T(8,128)S(1)}, f32[1,32,128]{2,1,0:T(8,128)}, u32[]{:S(2)}) copy-start(f32[1,32,128]{2,1,0:T(8,128)} %param.14) | copy-start | bytes 49156
  55.8 1259.9 %copy-start.3 = (f32[1,32,128]{2,1,0:T(8,128)S(1)}, f32[1,32,128]{2,1,0:T(8,128)}, u32[]{:S(2)}) copy-start(f32[1,32,128]{2,1,0:T(8,128)} %param.11) | copy-start | bytes 49156
  55.8 1259.9 %copy-start.5 = (f32[1,32,128]{2,1,0:T(8,128)S(1)}, f32[1,32,128]{2,1,0:T(8,128)}, u32[]{:S(2)}) copy-start(f32[1,32,128]{2,1,0:T(8,128)} %param.13) | copy-start | bytes 49156
  55.8 1259.9 %copy-start.6 = (f32[1,32,128]{2,1,0:T(8,128)S(1)}, f32[1,32,128]{2,1,0:T(8,128)}, u32[]{:S(2)}) copy-start(f32[1,32,128]{2,1,0:T(8,128)} %param.12) | copy-start | bytes 49156
  55.9 1669.7 %all-gather.3.cloned.1.call-start = ((), (), s32[]{:S(2)}) async-start(), calls=%async_computation.2 | async-start | bytes 2105344 | tf_op jit(solution)/shard_map/all_gather | solution.py:79
  1317.1 412.6 %copy-start.4 = (f32[32,128]{1,0:T(8,128)}, f32[32,128]{1,0:T(8,128)S(1)}, u32[]{:S(2)}) copy-start(f32[32,128]{1,0:T(8,128)S(1)} %get-tuple-element.5) | copy-start | bytes 49156
Sparse Core Ops, SparseCore 0:
  56.0 1133.8 reduce-scatter.1
  1317.8 407.6 all-gather.2
where the time goes:
time: 1740 us
  waiting for transfers between devices  1560 us (90%)
  blocking collectives  123 us (7%)
    reduce_scatter x1, waiting for transfers between devices, local(): summed = lax.psum_scatter(product, 'dp', scatter_dimension=0, tiled=True)  1130 us
    all_gather x1, waiting for transfers between devices, local(): lax.all_gather(new_master.astype(jnp.bfloat16)[None], 'dp', axis=1, tiled...  406 us
    psum x1, blocking collectives, local(): square_norm = lax.psum(local_square, ('pipe', 'dp'))  123 us
  transfers between devices with their start and end apart: 5, of which 5 were waited for; matrix products, arithmetic and copies ran while one was open for 0% of the time, Pallas kernels for 0%

commit v1 on v0

v1 whole, which is shorter than its diff:
```python
import functools
import jax
import jax.numpy as jnp
from jax import lax
from jax.experimental import pallas as pl
from jax.experimental.pallas import tpu as pltpu
from jax.sharding import Mesh, PartitionSpec as P

beta_one = 0.9
beta_two = 0.95
bias_one = 1.0 - 0.9**20
bias_two = 1.0 - 0.95**20
epsilon = 1e-08
decay_rate = 0.1
learn_rate = 0.0003
clip_norm = 1.0

bf16 = jnp.bfloat16
f32 = jnp.float32
DP_AXES = ("y", "z", "x", "core")
DP_SIZES = (2, 16, 4, 2)


def dot(a, b, dims):
    return lax.dot_general(a, b, (dims, ((), ())), preferred_element_type=f32)


def vmem_spec():
    return pl.BlockSpec(memory_space=pltpu.VMEM)


def known_kernel(section_ref, top_ref, weight_ref, out_ref, *, slab, span):
    step = pl.program_id(0)

    @pl.when(step == 0)
    def _():
        column = lax.broadcasted_iota(jnp.int32, top_ref.shape, 1)
        later = (column >= (section_ref[0] + 1) * slab) & (column < span)
        known = jnp.where(later, 0.0, top_ref[...].astype(f32)).astype(bf16)
        out_ref[...] = dot(known, weight_ref[...], ((1,), (1,)))

    @pl.when(step != 0)
    def _():
        out_ref[...] += dot(top_ref[...], weight_ref[...], ((1,), (1,)))


def known_part(section, top_grad, weight, slab, span, steps):
    rows, width = top_grad.shape
    block = width // steps
    return pl.pallas_call(
        functools.partial(known_kernel, slab=slab, span=span),
        grid_spec=pltpu.PrefetchScalarGridSpec(
            num_scalar_prefetch=1,
            grid=(steps,),
            in_specs=[
                pl.BlockSpec((rows, block), lambda i, s: (0, i)),
                pl.BlockSpec((slab, block), lambda i, s: (0, i)),
            ],
            out_specs=pl.BlockSpec((rows, slab), lambda i, s: (0, 0)),
        ),
        out_shape=jax.ShapeDtypeStruct((rows, slab), f32),
        name="known_part",
    )(section, top_grad, weight)


def relay_kernel(section_ref, top_ref, own_ref, one_ref, two_ref, three_ref, w_own_ref, w_one_ref, w_two_ref, head_ref, grad_ref, *, slab):
    section = section_ref[0]
    known = (own_ref, one_ref, two_ref, three_ref)
    for u in range(3, -1, -1):
        @pl.when(section <= u)
        def _(u=u):
            offset = u - section
            total = known[3][...]
            for k in (2, 1, 0):
                total = jnp.where(offset == k, known[k][...], total)
            for v in range(u + 1, 4):
                block = slice(v * slab, (v + 1) * slab)
                weight = w_own_ref[:, block].astype(f32)
                if v >= 2:
                    narrow = slice((v - 2) * slab, (v - 1) * slab)
                    weight = jnp.where(offset == 1, w_one_ref[:, narrow].astype(f32), weight)
                    weight = jnp.where(offset == 2, w_two_ref[:, narrow].astype(f32), weight)
                total = total + dot(head_ref[:, block], weight.astype(bf16), ((1,), (1,)))
            branch = total.astype(bf16)
            here = slice(u * slab, (u + 1) * slab)
            top = top_ref[:, here]
            placed = (top.astype(f32) + branch.astype(f32)).astype(bf16)
            head_ref[:, here] = jnp.where(offset == 0, top.astype(f32), placed.astype(f32)).astype(bf16)
            grad_ref[...] = branch

        @pl.when(section > u)
        def _(u=u):
            here = slice(u * slab, (u + 1) * slab)
            head_ref[:, here] = top_ref[:, here]


def relay(section, top_head, known, weights, slab):
    rows, span = top_head.shape
    return pl.pallas_call(
        functools.partial(relay_kernel, slab=slab),
        in_specs=[pl.BlockSpec(memory_space=pltpu.SMEM)] + [vmem_spec()] * 8,
        out_specs=[vmem_spec()] * 2,
        out_shape=[
            jax.ShapeDtypeStruct((rows, span), bf16),
            jax.ShapeDtypeStruct((rows, slab), bf16),
        ],
        name="relay",
    )(section, top_head, *known, *weights)


def product_kernel(core_ref, order_ref, slab_a_ref, slab_b_ref, head_a_ref, head_b_ref, top_ref, other_ref, out_ref, a_ref, b_ref, *, span):
    step = pl.program_id(0)

    @pl.when(step == 0)
    def _():
        a_ref[...] = dot(order_ref[...], slab_a_ref[...], ((1,), (1,))).astype(bf16)
        b_ref[...] = dot(order_ref[...], slab_b_ref[...], ((1,), (1,))).astype(bf16)

    out_ref[...] = (
        dot(a_ref[...], top_ref[...], ((1,), (0,))) + dot(b_ref[...], other_ref[...], ((1,), (0,)))
    ).astype(bf16)

    @pl.when((step == 0) & (core_ref[0] == 0))
    def _():
        out_ref[:, :span] = (
            dot(a_ref[...], head_a_ref[...], ((1,), (0,))) + dot(b_ref[...], head_b_ref[...], ((1,), (0,)))
        ).astype(bf16)


def slab_product(core, order, slab_a, slab_b, head_a, head_b, top_grad, other, steps):
    rows = top_grad.shape[0]
    slab = slab_a.shape[1]
    half = top_grad.shape[1] // 2
    span = head_a.shape[1]
    block = half // steps
    whole = lambda shape: pl.BlockSpec(shape, lambda i, c: (0, 0))
    return pl.pallas_call(
        functools.partial(product_kernel, span=span),
        grid_spec=pltpu.PrefetchScalarGridSpec(
            num_scalar_prefetch=1,
            grid=(steps,),
            in_specs=[
                whole((slab, slab)),
                whole((rows, slab)),
                whole((rows, slab)),
                whole((rows, span)),
                whole((rows, span)),
                pl.BlockSpec((rows, block), lambda i, c: (0, c[0] * steps + i)),
                pl.BlockSpec((rows, block), lambda i, c: (0, i)),
            ],
            out_specs=pl.BlockSpec((slab, block), lambda i, c: (0, i)),
            scratch_shapes=[pltpu.VMEM((slab, rows), bf16), pltpu.VMEM((slab, rows), bf16)],
        ),
        out_shape=jax.ShapeDtypeStruct((slab, half), bf16),
        name="slab_product",
    )(core, order, slab_a, slab_b, head_a, head_b, top_grad, other)


def fold_kernel(parts_ref, out_ref, *, count):
    total = parts_ref[0].astype(f32)
    for i in range(1, count):
        total = total + parts_ref[i].astype(f32)
    out_ref[...] = total.astype(out_ref.dtype)


def fold(parts, dtype):
    return pl.pallas_call(
        functools.partial(fold_kernel, count=parts.shape[0]),
        in_specs=[vmem_spec()],
        out_specs=vmem_spec(),
        out_shape=jax.ShapeDtypeStruct(parts.shape[1:], dtype),
        name="fold",
    )(parts)


def fold_chunks_kernel(parts_ref, out_ref, *, count, chunks):
    width = out_ref.shape[2]
    for j in range(chunks):
        cols = slice(j * width, (j + 1) * width)
        total = parts_ref[0, :, cols].astype(f32)
        for i in range(1, count):
            total = total + parts_ref[i, :, cols].astype(f32)
        out_ref[j] = total.astype(out_ref.dtype)


def fold_chunks(parts, chunks):
    count, rows, width = parts.shape
    return pl.pallas_call(
        functools.partial(fold_chunks_kernel, count=count, chunks=chunks),
        in_specs=[vmem_spec()],
        out_specs=vmem_spec(),
        out_shape=jax.ShapeDtypeStruct((chunks, rows, width // chunks), bf16),
        name="fold_chunks",
    )(parts)


def total_kernel(sums_ref, accum_ref, total_ref, square_ref, *, chunks, tokens):
    width = sums_ref.shape[2]
    square = jnp.zeros((accum_ref.shape[0], width), f32)
    for j in range(chunks):
        cols = slice(j * width, (j + 1) * width)
        total = accum_ref[:, cols] + sums_ref[j] * (1.0 / tokens)
        total_ref[:, cols] = total
        square = square + total * total
    square_ref[0, 0] = jnp.sum(square)


def total_of(sums, accum, tokens):
    return pl.pallas_call(
        functools.partial(total_kernel, chunks=sums.shape[0], tokens=tokens),
        in_specs=[vmem_spec()] * 2,
        out_specs=[vmem_spec(), pl.BlockSpec(memory_space=pltpu.SMEM)],
        out_shape=[
            jax.ShapeDtypeStruct(accum.shape, f32),
            jax.ShapeDtypeStruct((1, 1), f32),
        ],
        name="total_of",
    )(sums, accum)


def adam(total_grad, master, moment1, moment2, clip_factor):
    clipped = clip_factor * total_grad
    moment_one = beta_one * moment1 + (1.0 - beta_one) * clipped
    moment_two = beta_two * moment2 + (1.0 - beta_two) * clipped * clipped
    step = moment_one / bias_one / (jnp.sqrt(moment_two / bias_two) + epsilon) + decay_rate * master
    return step, master - learn_rate * step


def place_kernel(core_ref, order_ref, own_ref, other_ref, out_ref):
    side = pl.program_id(0)

    @pl.when(side == 0)
    def _():
        out_ref[...] = dot(order_ref[...], own_ref[...], ((1,), (0,))).astype(bf16)

    @pl.when(side == 1)
    def _():
        out_ref[...] = dot(order_ref[...], other_ref[...], ((1,), (0,))).astype(bf16)


def place(core, order, own, other, steps):
    slab, half = own.shape
    block = half // steps
    return pl.pallas_call(
        place_kernel,
        grid_spec=pltpu.PrefetchScalarGridSpec(
            num_scalar_prefetch=1,
            grid=(2, steps),
            in_specs=[
                pl.BlockSpec((slab, slab), lambda g, j, c: (0, 0)),
                pl.BlockSpec((slab, block), lambda g, j, c: (0, jnp.where(g == 0, j, steps - 1))),
                pl.BlockSpec((slab, block), lambda g, j, c: (0, jnp.where(g == 1, j, 0))),
            ],
            out_specs=pl.BlockSpec(
                (slab, block), lambda g, j, c: (0, jnp.where(g == 0, c[0], 1 - c[0]) * steps + j)
            ),
        ),
        out_shape=jax.ShapeDtypeStruct((slab, 2 * half), bf16),
        name="place",
    )(core, order, own, other)


def down(x, by):
    return lax.ppermute(x, "pipe", [(i, i - by) for i in range(by, 4)])


def swap(x, axis):
    return lax.ppermute(x, axis, [(0, 1), (1, 0)])


def local(top_grad, slab_inputs, weights, master, moment1, moment2, grad_accum, layer_counts):
    sizes = [lax.axis_size(axis) for axis in DP_AXES]
    n_y, n_z, n_x, n_core = sizes
    section = lax.axis_index("pipe").astype(jnp.int32)
    core = lax.axis_index("core").astype(jnp.int32)
    rows, width = top_grad.shape
    slab = slab_inputs.shape[2]
    span = 4 * slab
    half = width // 2
    tokens = rows * n_y * n_z * n_x * n_core
    slab_own, weight = slab_inputs[0], weights[0]
    shard = master.shape[1:]

    state = jnp.stack([master[0], moment1[0], moment2[0], grad_accum[0]])
    state = lax.all_gather(state, "z", axis=0, tiled=False)

    sent = lax.dynamic_slice(top_grad, (0, (1 - core) * half), (rows, half))
    other = swap(jnp.concatenate([sent, slab_own], axis=1), "core")
    slab_other = other[:, half:]

    w_sent = weight[:, 2 * slab : span]
    w_one = lax.ppermute(w_sent, "pipe", [(2, 1), (1, 0)])
    w_two = lax.ppermute(w_sent, "pipe", [(2, 0)])
    known = known_part(section[None], top_grad, weight, slab, span, 4)
    known_all = [known, down(known, 1), down(known, 2), down(known, 3)]
    top_head = top_grad[:, :span]
    head, section_grad = relay(
        section[None], top_head, known_all, [weight[:, :span], w_one, w_two], slab
    )
    head_other = swap(head, "core")

    here = jnp.arange(slab)
    source = (here % (n_y * n_z)) * n_x + here // (n_y * n_z)
    order = (jnp.arange(slab)[None, :] == source[:, None]).astype(bf16)
    product = slab_product(
        core[None], order, slab_own, slab_other, head, head_other, top_grad, other, 4
    )
    parts = lax.all_to_all(product, "x", split_axis=0, concat_axis=0, tiled=True)
    parts = fold(parts.reshape(n_x, slab // n_x, half), bf16)
    parts = lax.all_to_all(parts, "y", split_axis=0, concat_axis=0, tiled=True)
    parts = fold_chunks(parts.reshape(n_y, n_z, half), n_z)
    parts = lax.all_to_all(parts, "z", split_axis=0, concat_axis=0, tiled=True)
    sums = lax.all_gather(fold(parts, f32), "z", axis=0, tiled=False)

    state = state.transpose(1, 0, 2, 3).reshape(4, n_z, half)
    total_grad, square = total_of(sums, state[3], tokens)
    weighted = layer_counts.astype(f32)[section] * square[0, 0]
    weighted = lax.psum(weighted, "core")
    weighted = lax.psum(weighted, "x")
    square_norm = lax.psum(weighted, ("pipe", "y"))
    clip_factor = jnp.minimum(1.0, clip_norm / jnp.sqrt(square_norm))

    fresh = adam(total_grad, state[0], state[1], state[2], clip_factor)[1].astype(bf16)
    fresh = lax.all_gather(fresh, "y", axis=0, tiled=False)
    fresh = jnp.broadcast_to(fresh[None], (n_x, n_y, n_z, half))
    fresh = lax.all_to_all(fresh, "x", split_axis=0, concat_axis=0, tiled=True)
    fresh = fresh.reshape(slab, half)
    new_weights = place(core[None], order.T, fresh, swap(fresh, "core"), 4)

    own = lax.dynamic_slice(total_grad, (lax.axis_index("z"), 0), (1, half)).reshape(shard)
    adam_step, new_master = adam(own, master[0], moment1[0], moment2[0], clip_factor)
    return (new_weights[None], adam_step[None], new_master[None], section_grad[None])


def solution(mesh):
    devices = mesh.devices
    split = Mesh(devices.reshape((devices.shape[0],) + DP_SIZES), ("pipe",) + DP_AXES)
    return jax.shard_map(
        local,
        mesh=split,
        in_specs=(
            P(DP_AXES, None),
            P("pipe", DP_AXES, None),
            P("pipe", None, None),
            P("pipe", DP_AXES, None),
            P("pipe", DP_AXES, None),
            P("pipe", DP_AXES, None),
            P("pipe", DP_AXES, None),
            P(),
        ),
        out_specs=(
            P("pipe", None, None),
            P("pipe", DP_AXES, None),
            P("pipe", DP_AXES, None),
            P("pipe", DP_AXES, None),
        ),
        check_vma=False,
    )
```

time: 1740 us -> 220 us (0.13)
  waiting for transfers between devices: 1560 us -> 15.2 us
  starting transfers between devices: 4.09 us -> 43.8 us
  Pallas kernels: 0 us -> 24.2 us
  blocking collectives: 123 us -> 103 us
    reduce_scatter x1 -> x0, waiting for transfers between devices: 1130 us -> none  [local(): summed = lax.psum_scatter(product, 'dp', scatter_dimension=0, tiled=True)]
    all_gather x1, waiting for transfers between devices: 406 us -> 0.01 us  [local(): state = lax.all_gather(state, 'z', axis=0, tiled=False)]
    psum x1 -> x3, blocking collectives: 123 us -> 32.8 us  [the longest x1 12.9 us: local(): weighted = lax.psum(weighted, 'core')]
    all_to_all x0 -> x3, blocking collectives: none -> 39.9 us  [the longest x1 19.3 us: local(): lax.all_to_all(product, 'x', split_axis=0, concat_axis=0, tiled=True)]
    ppermute x3 -> x8, starting transfers between devices: 4.01 us -> 35.5 us  [the longest x3 29.1 us: swap(): return lax.ppermute(x, axis, [(0, 1), (1, 0)])]
    all_gather x0 -> x2, blocking collectives: none -> 30.3 us  [the longest x1 25.8 us: local(): sums = lax.all_gather(fold(parts, f32), 'z', axis=0, tiled=False)]
    pallas_call x0 -> x8, Pallas kernels: none -> 24.2 us  [the longest x1 6.42 us: place(): pl.pallas_call(place_kernel, grid_spec=pltpu.PrefetchScalarGridSpec(num_s...]
    ppermute x3 -> x8, waiting for transfers between devices: 24.8 us -> 6.08 us  [the longest x3 5.38 us: down(): return lax.ppermute(x, 'pipe', [(i, i - by) for i in range(by, 4)])]
  transfers between devices with their start and end apart: 5 -> 10, of which waited for: 5 -> 5; matrix products, arithmetic and copies ran while one was open for 0% -> 5% of each run, Pallas kernels for 0% -> 7%
where the time goes in v1:
time: 220 us; the launch traced here: 219 us
  blocking collectives  103 us (47%)
  starting transfers between devices  43.8 us (20%)
  Pallas kernels  24.2 us (11%)
  between operations  16.3 us (7%)
  waiting for transfers between devices  15.2 us (7%)
  local copies, waits for them, and re-layouts  11.7 us (5%)
  other arithmetic  4.59 us (2%)
    ppermute x3, starting transfers between devices, swap(): return lax.ppermute(x, axis, [(0, 1), (1, 0)])  29.1 us
    all_gather x1, blocking collectives, local(): sums = lax.all_gather(fold(parts, f32), 'z', axis=0, tiled=False)  25.8 us
    all_to_all x1, blocking collectives, local(): lax.all_to_all(product, 'x', split_axis=0, concat_axis=0, tiled=True)  19.3 us
    psum x1, blocking collectives, local(): weighted = lax.psum(weighted, 'core')  12.9 us
    psum x1, blocking collectives, local(): square_norm = lax.psum(weighted, ('pipe', 'y'))  12.4 us
    all_to_all x1, blocking collectives, local(): fresh = lax.all_to_all(fresh, 'x', split_axis=0, concat_axis=0, tiled=True)  12.2 us
    all_to_all x1, waiting for transfers between devices, local(): parts = lax.all_to_all(parts, 'z', split_axis=0, concat_axis=0, tiled=True)  9.08 us
    all_to_all x1, blocking collectives, local(): parts = lax.all_to_all(parts, 'y', split_axis=0, concat_axis=0, tiled=True)  8.42 us
  transfers between devices with their start and end apart: 10, of which 5 were waited for; matrix products, arithmetic and copies ran while one was open for 5% of the time, Pallas kernels for 7%

profile of v1, /device:TPU:1, one launch (start us, length us, event | category | flops | bytes accessed | tf_op | source)
XLA Modules:
  0.0 218.8 jit_solution(89450163469722094)
XLA Ops:
  7.2 0.0 copy-start.4
  7.2 0.0 all-gather.5.cloned.1.call-start
  7.2 0.0 copy-start.11
  7.2 0.0 copy-start.12
  7.2 0.0 copy-start.13
  7.3 0.0 copy-start.14
  7.3 1.3 constant_dynamic-slice_fusion
  8.6 0.0 copy-done.4
  8.6 0.1 pad_maximum_fusion
  8.7 16.1 %collective-permute-start = (bf16[128,4224]{1,0:T(8,128)(2,1)S(1)}, bf16[128,4224]{1,0:T(8,128)(2,1)S(1)}, u32[]{:S(2)}, u32[]{:S(2)}) collective-permute-start(bf16[128,4224]{1,0:T(8,128)(2,1)S(1)} %pad_maximum_fusion), channel_id=1, source_target_pairs={{0,1},{1,0},{2,3},{3,2},{4,5},{5,4},{6,7},{7,6},{8,9},{9,8},{10,11... | collective-permute-start | bytes 3244040 | tf_op jit(solution)/shard_map/ppermute | solution.py:268
  24.8 0.6 pad_maximum_fusion.1
  25.4 0.0 all-gather.5.cloned.1.call-update
  25.4 0.8 slice.40
  26.3 1.3 collective-permute-start.5
  27.6 1.3 collective-permute-start.4
  28.9 4.0 %known_part.1.own_ref = f32[128,128]{1,0:T(8,128)} custom-call(s32[1]{0:T(128)} %bitcast.5.section_ref, bf16[128,8192]{1,0:T(8,128)(2,1)} %top_ref.3, bf16[128,8192]{1,0:T(8,128)(2,1)} %bitcast.55), custom_call_target="tpu_custom_call" | custom-call | tf_op jit(solution)/shard_map/known_part/pallas_call | solution.py:50
  32.9 1.3 collective-permute-start.3
  34.2 1.3 collective-permute-start.2
  35.5 1.6 slice.39.w_own_ref
  37.1 1.6 slice.31.top_ref
  38.7 0.0 collective-permute-done.5.w_two_ref
  38.7 1.3 collective-permute-start.1
  40.0 0.0 collective-permute-done.4.w_one_ref
  40.0 0.9 collective-permute-done.3.three_ref
  40.9 3.1 %collective-permute-done.2.two_ref = f32[128,128]{1,0:T(8,128)S(1)} collective-permute-done((f32[128,128]{1,0:T(8,128)}, f32[128,128]{1,0:T(8,128)S(1)}, u32[]{:S(2)}, u32[]{:S(2)}) %collective-permute-start.2) | collective-permute-done | bytes 65568 | tf_op jit(solution)/shard_map/ppermute | solution.py:264
  44.0 1.4 collective-permute-done.1.one_ref
  45.4 0.0 copy-done.6
  45.4 0.6 copy-done.10
  46.0 2.4 %relay.1 = (bf16[128,512]{1,0:T(8,128)(2,1)}, bf16[128,128]{1,0:T(8,128)(2,1)}) custom-call(s32[1]{0:T(128)} %bitcast.5.section_ref, bf16[128,512]{1,0:T(8,128)(2,1)} %slice.31.top_ref, f32[128,128]{1,0:T(8,128)} %known_part.1.own_ref, f32[128,128]{1,0:T(8,128)} %copy-done.10, f32[128,128]{1,0:T(8,128)} %copy-done.9, f32[128,128]{1,0:T(8,128)} %copy-done.8, ...), custom_call_target="tpu_custom_call" | custom-call | tf_op jit(solution)/shard_map/relay/pallas_call | solution.py:99
  48.4 2.7 %collective-permute-start.6 = (bf16[128,512]{1,0:T(8,128)(2,1)}, bf16[128,512]{1,0:T(8,128)(2,1)S(1)}, u32[]{:S(2)}, u32[]{:S(2)}) collective-permute-start(bf16[128,512]{1,0:T(8,128)(2,1)} %get-tuple-element.8.head_a_ref), channel_id=1, source_target_pairs={{0,1},{1,0},{2,3},{3,2},{4,5},{5,4},{6,7},{7,6},{8,9},{9,8},{10,11... | collective-permute-start | bytes 393224 | tf_op jit(solution)/shard_map/ppermute | solution.py:268
  51.1 0.7 fusion.9
  51.8 0.0 collective-permute-done.other_ref
  51.8 0.7 slice.38.slab_b_ref
  52.4 0.0 collective-permute-done.6.head_b_ref
  52.4 0.3 copy-done.1
  52.8 0.3 copy-done.5
  53.1 4.4 %slab_product.1 = bf16[128,4096]{1,0:T(8,128)(2,1)} custom-call(s32[1]{0:T(128)} %bitcast.core_ref, bf16[128,128]{1,0:T(8,128)(2,1)} %get-tuple-element.18.order_ref, bf16[128,128]{1,0:T(8,128)(2,1)} %bitcast.67, bf16[128,128]{1,0:T(8,128)(2,1)} %slice.38.slab_b_ref, bf16[128,512]{1,0:T(8,128)(2,1)} %get-tuple-element.8.head_a_ref, ...), custom_call_target="tpu_custom_call" | custom-call | tf_op jit(solution)/shard_map/slab_product/pallas_call | solution.py:137
  57.5 19.3 %all_to_all.28.parts_ref = bf16[4,32,4096]{2,1,0:T(8,128)(2,1)} all-to-all(bf16[4,32,4096]{2,1,0:T(8,128)(2,1)} %bitcast.52), channel_id=1, replica_groups=mesh['pipe'=4,'y'=2,'z'=16,'x'=4,'core'=2] {'x'}, dimensions={0} | all-to-all | bytes 2097152 | tf_op jit(solution)/shard_map/all_to_all | solution.py:308
  76.8 2.1 fold.2
  78.8 8.4 %all_to_all.29.parts_ref = bf16[2,16,4096]{2,1,0:T(8,128)(2,1)} all-to-all(bf16[2,16,4096]{2,1,0:T(8,128)(2,1)} %bitcast.58), channel_id=1, replica_groups=mesh['pipe'=4,'y'=2,'z'=16,'x'=4,'core'=2] {'y'}, dimensions={0} | all-to-all | bytes 524288 | tf_op jit(solution)/shard_map/all_to_all | solution.py:310
  87.2 1.6 fold_chunks.1
  88.9 8.3 %all-to-all-start.2 = ((bf16[16,16,256]{2,1,0:T(8,128)(2,1)}), bf16[16,16,256]{2,1,0:T(8,128)(2,1)S(1)}, u32[]{:S(2)}, u32[]{:S(2)}) async-start(bf16[16,16,256]{2,1,0:T(8,128)(2,1)} %fold_chunks.1), calls=%async_computation.2 | async-start | bytes 262144 | tf_op jit(solution)/shard_map/all_to_all | solution.py:312
  97.2 0.6 dynamic_slice.9
  97.8 1.3 copy.27
  99.1 0.1 fusion.19
  99.3 0.9 copy.28
  100.1 9.1 %all-to-all-done.2.parts_ref = bf16[16,16,256]{2,1,0:T(8,128)(2,1)S(1)} async-done(((bf16[16,16,256]{2,1,0:T(8,128)(2,1)}), bf16[16,16,256]{2,1,0:T(8,128)(2,1)S(1)}, u32[]{:S(2)}, u32[]{:S(2)}) %all-to-all-start.2) | async-done | bytes 131104 | tf_op jit(solution)/shard_map/all_to_all | solution.py:312
  109.2 0.6 copy-done.3
  109.8 1.5 fold.3
  111.4 25.8 %all-gather.1 = f32[256,256]{1,0:T(8,128)} all-gather(f32[16,256]{1,0:T(8,128)} %fold.3), channel_id=3, replica_groups=mesh['pipe'=4,'y'=2,'z'=16,'x'=4,'core'=2] {'z'}, dimensions={0}, use_global_device_ids=true | all-gather | bytes 278528 | tf_op jit(solution)/shard_map/all_gather | solution.py:313
  137.2 1.8 total_of.1
  140.2 12.9 %psum.21 = f32[]{:T(128)} all-reduce(f32[]{:T(128)S(6)} %mul.153), channel_id=1, replica_groups=mesh['pipe'=4,'y'=2,'z'=16,'x'=4,'core'=2] {'core'}, use_global_device_ids=true, to_apply=%region_0.1 | all-reduce | flops 1 | bytes 8 | tf_op jit(solution)/shard_map/psum | solution.py:318
  153.2 7.5 %psum.22 = f32[]{:T(128)} all-reduce(f32[]{:T(128)} %psum.21), channel_id=1, replica_groups=mesh['pipe'=4,'y'=2,'z'=16,'x'=4,'core'=2] {'x'}, use_global_device_ids=true, to_apply=%region_1.2 | all-reduce | flops 1 | bytes 8 | tf_op jit(solution)/shard_map/psum | solution.py:319
  160.6 12.4 %psum.23 = f32[]{:T(128)} all-reduce(f32[]{:T(128)} %psum.22), channel_id=1, replica_groups=mesh['pipe'=4,'y'=2,'z'=16,'x'=4,'core'=2] {'pipe','y'}, use_global_device_ids=true, to_apply=%region_2.3 | all-reduce | flops 1 | bytes 8 | tf_op jit(solution)/shard_map/psum | solution.py:320
  173.8 1.5 fusion.7
  175.3 4.5 %all-gather.2 = bf16[32,4096]{1,0:T(8,128)(2,1)S(1)} all-gather(bf16[16,4096]{1,0:T(8,128)(2,1)S(1)} %fusion.7), channel_id=4, replica_groups=mesh['pipe'=4,'y'=2,'z'=16,'x'=4,'core'=2] {'y'}, dimensions={0}, use_global_device_ids=true | all-gather | bytes 393216 | tf_op jit(solution)/shard_map/all_gather | solution.py:324
  179.8 0.1 broadcast_in_dim.12
  179.9 12.2 %all_to_all.30 = bf16[4,2,16,4096]{3,2,1,0:T(8,128)(2,1)S(1)} all-to-all(bf16[4,2,16,4096]{3,2,1,0:T(8,128)(2,1)S(1)} %broadcast_in_dim.12), channel_id=1, replica_groups=mesh['pipe'=4,'y'=2,'z'=16,'x'=4,'core'=2] {'x'}, dimensions={0} | all-to-all | bytes 2097152 | tf_op jit(solution)/shard_map/all_to_all | solution.py:326
  192.0 10.3 %collective-permute-start.7 = (bf16[128,4096]{1,0:T(8,128)(2,1)S(1)}, bf16[128,4096]{1,0:T(8,128)(2,1)S(1)}, u32[]{:S(2)}, u32[]{:S(2)}) collective-permute-start(bf16[128,4096]{1,0:T(8,128)(2,1)S(1)} %bitcast.50), channel_id=1, source_target_pairs={{0,1},{1,0},{2,3},{3,2},{4,5},{5,4},{6,7},{7,6},{8,9},{9,8},{10,11... | collective-permute-start | bytes 3145736 | tf_op jit(solution)/shard_map/ppermute | solution.py:268
  202.4 0.9 dynamic-slice_multiply_fusion
  203.3 0.6 multiply_subtract_fusion
  203.9 0.7 collective-permute-done.7.other_ref
  204.6 1.0 copy-done.2
  205.6 6.4 %place.1 = bf16[128,8192]{1,0:T(8,128)(2,1)} custom-call(s32[1]{0:T(128)} %bitcast.core_ref, bf16[128,128]{1,0:T(8,128)(2,1)} %get-tuple-element.19.order_ref, bf16[128,4096]{1,0:T(8,128)(2,1)} %bitcast.51, bf16[128,4096]{1,0:T(8,128)(2,1)} %copy-done.2), custom_call_target="tpu_custom_call" | custom-call | tf_op jit(solution)/shard_map/place/pallas_call | solution.py:244
  (23 shorter events, 0.0 us)
Async XLA Ops:
  7.2 1.4 copy-start.4
  7.2 90.6 %all-gather.5.cloned.1.call-start = ((), (), s32[]{:S(2)}) async-start(), calls=%async_computation.4 | async-start | bytes 1114112 | tf_op jit(solution)/shard_map/all_gather | solution.py:285
  7.2 17.5 %copy-start.11 = (f32[1,32,128]{2,1,0:T(8,128)S(1)}, f32[1,32,128]{2,1,0:T(8,128)}, u32[]{:S(2)}) copy-start(f32[1,32,128]{2,1,0:T(8,128)} %param.13) | copy-start | bytes 49156
  7.2 17.5 %copy-start.12 = (f32[1,32,128]{2,1,0:T(8,128)S(1)}, f32[1,32,128]{2,1,0:T(8,128)}, u32[]{:S(2)}) copy-start(f32[1,32,128]{2,1,0:T(8,128)} %param.12) | copy-start | bytes 49156
  7.2 17.5 %copy-start.13 = (f32[1,32,128]{2,1,0:T(8,128)S(1)}, f32[1,32,128]{2,1,0:T(8,128)}, u32[]{:S(2)}) copy-start(f32[1,32,128]{2,1,0:T(8,128)} %param.11) | copy-start | bytes 49156
  7.3 17.5 %copy-start.14 = (f32[1,32,128]{2,1,0:T(8,128)S(1)}, f32[1,32,128]{2,1,0:T(8,128)}, u32[]{:S(2)}) copy-start(f32[1,32,128]{2,1,0:T(8,128)} %param.14) | copy-start | bytes 49156
  8.7 43.1 %collective-permute-start = (bf16[128,4224]{1,0:T(8,128)(2,1)S(1)}, bf16[128,4224]{1,0:T(8,128)(2,1)S(1)}, u32[]{:S(2)}, u32[]{:S(2)}) collective-permute-start(bf16[128,4224]{1,0:T(8,128)(2,1)S(1)} %pad_maximum_fusion), channel_id=1, source_target_pairs={{0,1},{1,0},{2,3},{3,2},{4,5},{5,4},{6,7},{7,6},{8,9},{9,8},{10,11... | collective-permute-start | bytes 3244040 | tf_op jit(solution)/shard_map/ppermute | solution.py:268
  26.3 12.4 %collective-permute-start.5 = (bf16[128,256]{1,0:T(8,128)(2,1)S(1)}, bf16[128,256]{1,0:T(8,128)(2,1)S(1)}, u32[]{:S(2)}, u32[]{:S(2)}) collective-permute-start(bf16[128,256]{1,0:T(8,128)(2,1)S(1)} %slice.40), channel_id=1, source_target_pairs={{512,0},{513,1},{514,2},{515,3},{516,4},{517,5},{518,6},{519,7},{5... | collective-permute-start | bytes 196616 | tf_op jit(solution)/shard_map/ppermute | solution.py:293
  27.6 12.4 %collective-permute-start.4 = (bf16[128,256]{1,0:T(8,128)(2,1)S(1)}, bf16[128,256]{1,0:T(8,128)(2,1)S(1)}, u32[]{:S(2)}, u32[]{:S(2)}) collective-permute-start(bf16[128,256]{1,0:T(8,128)(2,1)S(1)} %slice.40), channel_id=1, source_target_pairs={{512,256},{256,0},{513,257},{257,1},{514,258},{258,2},{515,259},{2... | collective-permute-start | bytes 196616 | tf_op jit(solution)/shard_map/ppermute | solution.py:292
  32.9 7.9 %collective-permute-start.3 = (f32[128,128]{1,0:T(8,128)}, f32[128,128]{1,0:T(8,128)S(1)}, u32[]{:S(2)}, u32[]{:S(2)}) collective-permute-start(f32[128,128]{1,0:T(8,128)} %known_part.1.own_ref), channel_id=1, source_target_pairs={{768,0},{769,1},{770,2},{771,3},{772,4},{773,5},{774,6},{775,7},{7... | collective-permute-start | bytes 196616 | tf_op jit(solution)/shard_map/ppermute | solution.py:264
  34.2 9.7 %collective-permute-start.2 = (f32[128,128]{1,0:T(8,128)}, f32[128,128]{1,0:T(8,128)S(1)}, u32[]{:S(2)}, u32[]{:S(2)}) collective-permute-start(f32[128,128]{1,0:T(8,128)} %known_part.1.own_ref), channel_id=1, source_target_pairs={{512,0},{768,256},{513,1},{769,257},{514,2},{770,258},{515,3},{771... | collective-permute-start | bytes 196616 | tf_op jit(solution)/shard_map/ppermute | solution.py:264
  38.7 6.7 %copy-start.6 = (bf16[128,256]{1,0:T(8,128)(2,1)}, bf16[128,256]{1,0:T(8,128)(2,1)S(1)}, u32[]{:S(2)}) copy-start(bf16[128,256]{1,0:T(8,128)(2,1)S(1)} %collective-permute-done.5.w_two_ref) | copy-start | bytes 196612
  38.7 6.7 %collective-permute-start.1 = (f32[128,128]{1,0:T(8,128)}, f32[128,128]{1,0:T(8,128)S(1)}, u32[]{:S(2)}, u32[]{:S(2)}) collective-permute-start(f32[128,128]{1,0:T(8,128)} %known_part.1.own_ref), channel_id=1, source_target_pairs={{256,0},{512,256},{768,512},{257,1},{513,257},{769,513},{258,2},{5... | collective-permute-start | bytes 196616 | tf_op jit(solution)/shard_map/ppermute | solution.py:264
  40.0 5.4 %copy-start.7 = (bf16[128,256]{1,0:T(8,128)(2,1)}, bf16[128,256]{1,0:T(8,128)(2,1)S(1)}, u32[]{:S(2)}) copy-start(bf16[128,256]{1,0:T(8,128)(2,1)S(1)} %collective-permute-done.4.w_one_ref) | copy-start | bytes 196612
  40.9 4.5 %copy-start.8 = (f32[128,128]{1,0:T(8,128)}, f32[128,128]{1,0:T(8,128)S(1)}, u32[]{:S(2)}) copy-start(f32[128,128]{1,0:T(8,128)S(1)} %collective-permute-done.3.three_ref) | copy-start | bytes 196612
  43.9 1.4 copy-start.9
  45.4 0.6 copy-start.10
  48.4 4.1 %collective-permute-start.6 = (bf16[128,512]{1,0:T(8,128)(2,1)}, bf16[128,512]{1,0:T(8,128)(2,1)S(1)}, u32[]{:S(2)}, u32[]{:S(2)}) collective-permute-start(bf16[128,512]{1,0:T(8,128)(2,1)} %get-tuple-element.8.head_a_ref), channel_id=1, source_target_pairs={{0,1},{1,0},{2,3},{3,2},{4,5},{5,4},{6,7},{7,6},{8,9},{9,8},{10,11... | collective-permute-start | bytes 393224 | tf_op jit(solution)/shard_map/ppermute | solution.py:268
  51.8 1.0 copy-start.1
  52.4 0.6 copy-start.5
  57.5 39.7 %copy-start.15 = (s32[4]{0:T(128)S(1)}, s32[4]{0:T(128)}, u32[]{:S(2)}) copy-start(s32[4]{0:T(128)} %param.15) | copy-start | bytes 52
  88.9 20.3 %all-to-all-start.2 = ((bf16[16,16,256]{2,1,0:T(8,128)(2,1)}), bf16[16,16,256]{2,1,0:T(8,128)(2,1)S(1)}, u32[]{:S(2)}, u32[]{:S(2)}) async-start(bf16[16,16,256]{2,1,0:T(8,128)(2,1)} %fold_chunks.1), calls=%async_computation.2 | async-start | bytes 262144 | tf_op jit(solution)/shard_map/all_to_all | solution.py:312
  109.2 0.6 copy-start.3
  192.0 12.6 %copy-start = (bf16[4,2,16,4096]{3,2,1,0:T(8,128)(2,1)}, bf16[4,2,16,4096]{3,2,1,0:T(8,128)(2,1)S(1)}, u32[]{:S(2)}) copy-start(bf16[4,2,16,4096]{3,2,1,0:T(8,128)(2,1)S(1)} %all_to_all.30) | copy-start | bytes 3145732
  192.0 12.6 %collective-permute-start.7 = (bf16[128,4096]{1,0:T(8,128)(2,1)S(1)}, bf16[128,4096]{1,0:T(8,128)(2,1)S(1)}, u32[]{:S(2)}, u32[]{:S(2)}) collective-permute-start(bf16[128,4096]{1,0:T(8,128)(2,1)S(1)} %bitcast.50), channel_id=1, source_target_pairs={{0,1},{1,0},{2,3},{3,2},{4,5},{5,4},{6,7},{7,6},{8,9},{9,8},{10,11... | collective-permute-start | bytes 3145736 | tf_op jit(solution)/shard_map/ppermute | solution.py:268
  204.6 1.0 copy-start.2
Sparse Core Ops, SparseCore 0:
  25.6 60.4 all-gather.4

commit v2 on v1

--- a/solution.py
+++ b/solution.py
@@ -94,18 +94,23 @@
             head_ref[:, here] = top_ref[:, here]
 
 
-def relay(section, top_head, known, weights, slab):
-    rows, span = top_head.shape
+def relay(section, top_grad, known, weights, slab, span):
+    rows = top_grad.shape[0]
+    first = pl.BlockSpec((rows, span), lambda i: (0, 0))
     return pl.pallas_call(
         functools.partial(relay_kernel, slab=slab),
-        in_specs=[pl.BlockSpec(memory_space=pltpu.SMEM)] + [vmem_spec()] * 8,
-        out_specs=[vmem_spec()] * 2,
+        grid=(1,),
+        in_specs=[pl.BlockSpec(memory_space=pltpu.SMEM), first]
+        + [pl.BlockSpec((rows, slab), lambda i: (0, 0))] * 4
+        + [pl.BlockSpec((slab, span), lambda i: (0, 0))]
+        + [pl.BlockSpec((slab, span // 2), lambda i: (0, 0))] * 2,
+        out_specs=[first, pl.BlockSpec((rows, slab), lambda i: (0, 0))],
         out_shape=[
             jax.ShapeDtypeStruct((rows, span), bf16),
             jax.ShapeDtypeStruct((rows, slab), bf16),
         ],
         name="relay",
-    )(section, top_head, *known, *weights)
+    )(section, top_grad, *known, *weights)
 
 
 def product_kernel(core_ref, order_ref, slab_a_ref, slab_b_ref, head_a_ref, head_b_ref, top_ref, other_ref, out_ref, a_ref, b_ref, *, span):
@@ -160,15 +165,16 @@
     total = parts_ref[0].astype(f32)
     for i in range(1, count):
         total = total + parts_ref[i].astype(f32)
-    out_ref[...] = total.astype(out_ref.dtype)
-
-
-def fold(parts, dtype):
+    for i in range(count):
+        out_ref[i] = total
+
+
+def fold(parts):
     return pl.pallas_call(
         functools.partial(fold_kernel, count=parts.shape[0]),
         in_specs=[vmem_spec()],
         out_specs=vmem_spec(),
-        out_shape=jax.ShapeDtypeStruct(parts.shape[1:], dtype),
+        out_shape=jax.ShapeDtypeStruct(parts.shape, f32),
         name="fold",
     )(parts)
 
@@ -194,7 +200,7 @@
     )(parts)
 
 
-def total_kernel(sums_ref, accum_ref, total_ref, square_ref, *, chunks, tokens):
+def total_kernel(count_ref, sums_ref, accum_ref, total_ref, square_ref, *, chunks, tokens):
     width = sums_ref.shape[2]
     square = jnp.zeros((accum_ref.shape[0], width), f32)
     for j in range(chunks):
@@ -202,20 +208,20 @@
         total = accum_ref[:, cols] + sums_ref[j] * (1.0 / tokens)
         total_ref[:, cols] = total
         square = square + total * total
-    square_ref[0, 0] = jnp.sum(square)
-
-
-def total_of(sums, accum, tokens):
+    square_ref[...] = jnp.full(square_ref.shape, jnp.sum(square) * count_ref[0].astype(f32), f32)
+
+
+def total_of(count, sums, accum, tokens, peers):
     return pl.pallas_call(
         functools.partial(total_kernel, chunks=sums.shape[0], tokens=tokens),
-        in_specs=[vmem_spec()] * 2,
-        out_specs=[vmem_spec(), pl.BlockSpec(memory_space=pltpu.SMEM)],
+        in_specs=[pl.BlockSpec(memory_space=pltpu.SMEM)] + [vmem_spec()] * 2,
+        out_specs=[vmem_spec()] * 2,
         out_shape=[
             jax.ShapeDtypeStruct(accum.shape, f32),
-            jax.ShapeDtypeStruct((1, 1), f32),
+            jax.ShapeDtypeStruct((peers, 8, 128), f32),
         ],
         name="total_of",
-    )(sums, accum)
+    )(count, sums, accum)
 
 
 def adam(total_grad, master, moment1, moment2, clip_factor):
@@ -226,38 +232,59 @@
     return step, master - learn_rate * step
 
 
-def place_kernel(core_ref, order_ref, own_ref, other_ref, out_ref):
-    side = pl.program_id(0)
-
-    @pl.when(side == 0)
-    def _():
-        out_ref[...] = dot(order_ref[...], own_ref[...], ((1,), (0,))).astype(bf16)
-
-    @pl.when(side == 1)
-    def _():
-        out_ref[...] = dot(order_ref[...], other_ref[...], ((1,), (0,))).astype(bf16)
-
-
-def place(core, order, own, other, steps):
-    slab, half = own.shape
+def fresh_kernel(squares_ref, total_ref, state_ref, out_ref, factor_ref):
+    square_norm = jnp.sum(squares_ref[...], axis=0)[:1]
+    clip_factor = jnp.minimum(1.0, clip_norm / jnp.sqrt(square_norm))
+    factor_ref[...] = jnp.broadcast_to(clip_factor, factor_ref.shape)
+    lanes = factor_ref.shape[1]
+    for j in range(total_ref.shape[1] // lanes):
+        cols = slice(j * lanes, (j + 1) * lanes)
+        out_ref[:, cols] = adam(
+            total_ref[:, cols], state_ref[0, :, cols], state_ref[1, :, cols], state_ref[2, :, cols], clip_factor
+        )[1].astype(bf16)
+
+
+def fresh_weights(squares, total_grad, state):
+    return pl.pallas_call(
+        fresh_kernel,
+        in_specs=[vmem_spec()] * 3,
+        out_specs=[vmem_spec()] * 2,
+        out_shape=[
+            jax.ShapeDtypeStruct(total_grad.shape, bf16),
+            jax.ShapeDtypeStruct((8, 128), f32),
+        ],
+        name="fresh_weights",
+    )(squares, total_grad, state)
+
+
+def place_kernel(side_ref, order_ref, half_ref, *refs):
+    out_ref = refs[-1]
+    out_ref[...] = dot(order_ref[...], half_ref[...], ((1,), (0,))).astype(bf16)
+
+
+def place(side, order, values, steps, into=None):
+    slab, half = values.shape
     block = half // steps
+    rest = [] if into is None else [into]
     return pl.pallas_call(
         place_kernel,
         grid_spec=pltpu.PrefetchScalarGridSpec(
             num_scalar_prefetch=1,
-            grid=(2, steps),
+            grid=(steps,),
             in_specs=[
-                pl.BlockSpec((slab, slab), lambda g, j, c: (0, 0)),
-                pl.BlockSpec((slab, block), lambda g, j, c: (0, jnp.where(g == 0, j, steps - 1))),
-                pl.BlockSpec((slab, block), lambda g, j, c: (0, jnp.where(g == 1, j, 0))),
-            ],
-            out_specs=pl.BlockSpec(
-                (slab, block), lambda g, j, c: (0, jnp.where(g == 0, c[0], 1 - c[0]) * steps + j)
-            ),
+                pl.BlockSpec((slab, slab), lambda j, c: (0, 0)),
+                pl.BlockSpec((slab, block), lambda j, c: (0, j)),
+            ]
+            + [pl.BlockSpec(memory_space=pl.ANY)] * len(rest),
+            out_specs=pl.BlockSpec((slab, block), lambda j, c: (0, c[0] * steps + j)),
         ),
         out_shape=jax.ShapeDtypeStruct((slab, 2 * half), bf16),
+        input_output_aliases={3: 0} if rest else {},
+        cost_estimate=pl.CostEstimate(
+            flops=2 * slab * slab * half, bytes_accessed=4 * slab * half, transcendentals=0
+        ),
         name="place",
-    )(core, order, own, other)
+    )(side, order, values, *rest)
 
 
 def down(x, by):
@@ -293,42 +320,41 @@
     w_two = lax.ppermute(w_sent, "pipe", [(2, 0)])
     known = known_part(section[None], top_grad, weight, slab, span, 4)
     known_all = [known, down(known, 1), down(known, 2), down(known, 3)]
-    top_head = top_grad[:, :span]
     head, section_grad = relay(
-        section[None], top_head, known_all, [weight[:, :span], w_one, w_two], slab
+        section[None], top_grad, known_all, [weight, w_one, w_two], slab, span
     )
     head_other = swap(head, "core")
 
     here = jnp.arange(slab)
-    source = (here % (n_y * n_z)) * n_x + here // (n_y * n_z)
-    order = (jnp.arange(slab)[None, :] == source[:, None]).astype(bf16)
+    source = here // (n_x * n_z) * (n_x * n_z) + here % n_z * n_x + here // n_z % n_x
+    order = (here[None, :] == source[:, None]).astype(bf16)
     product = slab_product(
         core[None], order, slab_own, slab_other, head, head_other, top_grad, other, 4
     )
-    parts = lax.all_to_all(product, "x", split_axis=0, concat_axis=0, tiled=True)
-    parts = fold(parts.reshape(n_x, slab // n_x, half), bf16)
-    parts = lax.all_to_all(parts, "y", split_axis=0, concat_axis=0, tiled=True)
-    parts = fold_chunks(parts.reshape(n_y, n_z, half), n_z)
+    parts = lax.all_to_all(product, ("y", "x"), split_axis=0, concat_axis=0, tiled=True)
+    parts = fold_chunks(parts.reshape(n_y * n_x, n_z, half), n_z)
     parts = lax.all_to_all(parts, "z", split_axis=0, concat_axis=0, tiled=True)
-    sums = lax.all_gather(fold(parts, f32), "z", axis=0, tiled=False)
+    sums = lax.all_to_all(fold(parts), "z", split_axis=0, concat_axis=0, tiled=True)
 
     state = state.transpose(1, 0, 2, 3).reshape(4, n_z, half)
-    total_grad, square = total_of(sums, state[3], tokens)
-    weighted = layer_counts.astype(f32)[section] * square[0, 0]
-    weighted = lax.psum(weighted, "core")
-    weighted = lax.psum(weighted, "x")
-    square_norm = lax.psum(weighted, ("pipe", "y"))
-    clip_factor = jnp.minimum(1.0, clip_norm / jnp.sqrt(square_norm))
-
-    fresh = adam(total_grad, state[0], state[1], state[2], clip_factor)[1].astype(bf16)
+    group = ("pipe", "y", "x", "core")
+    count = lax.dynamic_slice(layer_counts, (section,), (1,))
+    total_grad, squares = total_of(count, sums, state[3], tokens, lax.axis_size(group))
+    squares = lax.all_to_all(squares, group, split_axis=0, concat_axis=0, tiled=True)
+
+    fresh, factor = fresh_weights(squares, total_grad, state[:3])
     fresh = lax.all_gather(fresh, "y", axis=0, tiled=False)
     fresh = jnp.broadcast_to(fresh[None], (n_x, n_y, n_z, half))
     fresh = lax.all_to_all(fresh, "x", split_axis=0, concat_axis=0, tiled=True)
     fresh = fresh.reshape(slab, half)
-    new_weights = place(core[None], order.T, fresh, swap(fresh, "core"), 4)
+    source = here % n_x * (n_y * n_z) + here // n_x
+    order = (here[None, :] == source[:, None]).astype(bf16)
+    fresh_other = swap(fresh, "core")
+    new_weights = place(core[None], order, fresh, 2)
+    new_weights = place(1 - core[None], order, fresh_other, 2, new_weights)
 
     own = lax.dynamic_slice(total_grad, (lax.axis_index("z"), 0), (1, half)).reshape(shard)
-    adam_step, new_master = adam(own, master[0], moment1[0], moment2[0], clip_factor)
+    adam_step, new_master = adam(own, master[0], moment1[0], moment2[0], factor[0, 0])
     return (new_weights[None], adam_step[None], new_master[None], section_grad[None])
 
 

time: 220 us -> 216 us (0.982)
  blocking collectives: 103 us -> 41.7 us
  waiting for transfers between devices: 15.2 us -> 58 us
  starting transfers between devices: 43.8 us -> 58.9 us
    psum x3 -> x0, blocking collectives: 32.8 us -> none  [the longest x1 12.9 us: local(): weighted = lax.psum(weighted, 'core')]
    all_gather x1 -> x0, blocking collectives: 25.8 us -> none  [local(): sums = lax.all_gather(fold(parts, f32), 'z', axis=0, tiled=False)]
    all_gather x1, waiting for transfers between devices: 0.01 us -> 24.7 us  [local(): state = lax.all_gather(state, 'z', axis=0, tiled=False)]
    all_to_all x1 -> x3, starting transfers between devices: 8.3 us -> 29.1 us  [the longest x1 17.8 us: local(): lax.all_to_all(squares, group, split_axis=0, concat_axis=0, tiled=True)]
    all_to_all x1 -> x3, waiting for transfers between devices: 9.08 us -> 26.2 us  [the longest x1 14.2 us: local(): lax.all_to_all(product, ('y', 'x'), split_axis=0, concat_axis=0, tiled=True)]
    all_to_all x2 -> x1, blocking collectives: 27.7 us -> 20.1 us  [local(): parts = lax.all_to_all(parts, 'z', split_axis=0, concat_axis=0, tiled=True)]
    ppermute x3, starting transfers between devices: 29.1 us -> 23.4 us  [swap(): return lax.ppermute(x, axis, [(0, 1), (1, 0)])]
    all_to_all x1, blocking collectives: 12.2 us -> 15.8 us  [local(): fresh = lax.all_to_all(fresh, 'x', split_axis=0, concat_axis=0, tiled=True)]
  transfers between devices with their start and end apart: 10 -> 12, of which waited for: 5 -> 6; matrix products, arithmetic and copies ran while one was open for 5% -> 5% of each run, Pallas kernels for 7% -> 6%
where the time goes in v2:
time: 216 us; the launch traced here: 215 us
  starting transfers between devices  58.9 us (27%)
  waiting for transfers between devices  58 us (27%)
  blocking collectives  41.7 us (19%)
  Pallas kernels  24.2 us (11%)
  between operations  14.3 us (7%)
  local copies, waits for them, and re-layouts  13.2 us (6%)
  other arithmetic  4.32 us (2%)
    all_gather x1, waiting for transfers between devices, local(): state = lax.all_gather(state, 'z', axis=0, tiled=False)  24.7 us
    ppermute x3, starting transfers between devices, swap(): return lax.ppermute(x, axis, [(0, 1), (1, 0)])  23.4 us
    all_to_all x1, blocking collectives, local(): parts = lax.all_to_all(parts, 'z', split_axis=0, concat_axis=0, tiled=True)  20.1 us
    all_to_all x1, starting transfers between devices, local(): lax.all_to_all(squares, group, split_axis=0, concat_axis=0, tiled=True)  17.8 us
    all_to_all x1, blocking collectives, local(): fresh = lax.all_to_all(fresh, 'x', split_axis=0, concat_axis=0, tiled=True)  15.8 us
    all_to_all x1, waiting for transfers between devices, local(): lax.all_to_all(product, ('y', 'x'), split_axis=0, concat_axis=0, tiled=True)  14.2 us
    all_to_all x1, waiting for transfers between devices, local(): lax.all_to_all(squares, group, split_axis=0, concat_axis=0, tiled=True)  12.1 us
    all_to_all x1, starting transfers between devices, local(): lax.all_to_all(fold(parts), 'z', split_axis=0, concat_axis=0, tiled=True)  7.59 us
  transfers between devices with their start and end apart: 12, of which 6 were waited for; matrix products, arithmetic and copies ran while one was open for 5% of the time, Pallas kernels for 6%

profile of v2, /device:TPU:1, one launch (start us, length us, event | category | flops | bytes accessed | tf_op | source)
XLA Modules:
  0.0 214.7 jit_solution(16874616750134459450)
XLA Ops:
  7.2 0.0 copy-start.6
  7.2 1.3 constant_dynamic-slice_fusion
  8.5 0.1 pad_maximum_fusion
  8.6 16.1 %collective-permute-start = (bf16[128,4224]{1,0:T(8,128)(2,1)S(1)}, bf16[128,4224]{1,0:T(8,128)(2,1)S(1)}, u32[]{:S(2)}, u32[]{:S(2)}) collective-permute-start(bf16[128,4224]{1,0:T(8,128)(2,1)S(1)} %pad_maximum_fusion), channel_id=1, source_target_pairs={{0,1},{1,0},{2,3},{3,2},{4,5},{5,4},{6,7},{7,6},{8,9},{9,8},{10,11... | collective-permute-start | bytes 3244040 | tf_op jit(solution)/shard_map/ppermute | solution.py:295
  24.7 0.8 slice.26
  25.5 1.3 collective-permute-start.5
  26.8 1.3 collective-permute-start.4
  28.1 4.1 %known_part.1.own_ref = f32[128,128]{1,0:T(8,128)} custom-call(s32[1]{0:T(128)} %bitcast.2.section_ref, bf16[128,8192]{1,0:T(8,128)(2,1)} %top_ref.5, bf16[128,8192]{1,0:T(8,128)(2,1)} %bitcast.23), custom_call_target="tpu_custom_call" | custom-call | tf_op jit(solution)/shard_map/known_part/pallas_call | solution.py:50
  32.2 1.3 collective-permute-start.3
  33.5 1.3 collective-permute-start.2
  34.8 0.3 collective-permute-done.5.w_two_ref
  35.0 1.3 collective-permute-start.1
  36.3 0.0 collective-permute-done.4.w_one_ref
  36.3 3.7 %collective-permute-done.3.three_ref = f32[128,128]{1,0:T(8,128)S(1)} collective-permute-done((f32[128,128]{1,0:T(8,128)}, f32[128,128]{1,0:T(8,128)S(1)}, u32[]{:S(2)}, u32[]{:S(2)}) %collective-permute-start.3) | collective-permute-done | bytes 65568 | tf_op jit(solution)/shard_map/ppermute | solution.py:291
  40.1 3.1 %collective-permute-done.2.two_ref = f32[128,128]{1,0:T(8,128)S(1)} collective-permute-done((f32[128,128]{1,0:T(8,128)}, f32[128,128]{1,0:T(8,128)S(1)}, u32[]{:S(2)}, u32[]{:S(2)}) %collective-permute-start.2) | collective-permute-done | bytes 65568 | tf_op jit(solution)/shard_map/ppermute | solution.py:291
  43.2 0.0 collective-permute-done.1.one_ref
  43.2 0.6 copy-done.11
  43.8 0.6 copy-done.12
  44.4 2.4 %relay.1 = (bf16[128,512]{1,0:T(8,128)(2,1)}, bf16[128,128]{1,0:T(8,128)(2,1)}) custom-call(s32[1]{0:T(128)} %bitcast.2.section_ref, bf16[128,8192]{1,0:T(8,128)(2,1)} %top_ref.5, f32[128,128]{1,0:T(8,128)} %known_part.1.own_ref, f32[128,128]{1,0:T(8,128)} %copy-done.12, f32[128,128]{1,0:T(8,128)} %copy-done.11, f32[128,128]{1,0:T(8,128)} %copy-done.10, ...), custom_call_target="tpu_custom_call" | custom-call | tf_op jit(solution)/shard_map/relay/pallas_call | solution.py:100
  46.8 2.8 %collective-permute-start.6 = (bf16[128,512]{1,0:T(8,128)(2,1)}, bf16[128,512]{1,0:T(8,128)(2,1)S(1)}, u32[]{:S(2)}, u32[]{:S(2)}) collective-permute-start(bf16[128,512]{1,0:T(8,128)(2,1)} %get-tuple-element.10.head_a_ref), channel_id=1, source_target_pairs={{0,1},{1,0},{2,3},{3,2},{4,5},{5,4},{6,7},{7,6},{8,9},{9,8},{10,11... | collective-permute-start | bytes 393224 | tf_op jit(solution)/shard_map/ppermute | solution.py:295
  49.6 0.7 fusion.1.order_ref
  50.3 0.0 collective-permute-done.other_ref
  50.3 0.6 slice.25.slab_b_ref
  51.0 0.0 collective-permute-done.6.head_b_ref
  51.0 0.3 copy-done.2
  51.3 0.3 copy-done.7
  51.6 4.4 %slab_product.1 = bf16[128,4096]{1,0:T(8,128)(2,1)} custom-call(s32[1]{0:T(128)} %bitcast.core_ref.side_ref, bf16[128,128]{1,0:T(8,128)(2,1)} %fusion.1.order_ref, bf16[128,128]{1,0:T(8,128)(2,1)} %bitcast.35, bf16[128,128]{1,0:T(8,128)(2,1)} %slice.25.slab_b_ref, bf16[128,512]{1,0:T(8,128)(2,1)} %get-tuple-element.10.head_a_ref, ...), custom_call_target="tpu_custom_call" | custom-call | tf_op jit(solution)/shard_map/slab_product/pallas_call | solution.py:142
  56.0 0.0 copy-start.15
  56.1 0.0 copy-start.16
  56.1 0.0 copy-start.17
  56.1 3.7 %all-to-all-start = ((bf16[8,16,4096]{2,1,0:T(8,128)(2,1)}), bf16[8,16,4096]{2,1,0:T(8,128)(2,1)S(1)}, u32[]{:S(2)}, u32[]{:S(2)}) async-start(bf16[8,16,4096]{2,1,0:T(8,128)(2,1)} %bitcast.26), calls=%async_computation | async-start | bytes 2097152 | tf_op jit(solution)/shard_map/all_to_all | solution.py:334
  59.8 0.0 all-gather.4.cloned.1.call-start
  59.9 0.6 pad_maximum_fusion.1
  60.5 0.0 all-gather.4.cloned.1.call-update
  60.5 14.2 %all-to-all-done.parts_ref = bf16[8,16,4096]{2,1,0:T(8,128)(2,1)S(1)} async-done(((bf16[8,16,4096]{2,1,0:T(8,128)(2,1)}), bf16[8,16,4096]{2,1,0:T(8,128)(2,1)S(1)}, u32[]{:S(2)}, u32[]{:S(2)}) %all-to-all-start) | async-done | bytes 1048608 | tf_op jit(solution)/shard_map/all_to_all | solution.py:334
  74.7 1.0 copy-done.1
  75.7 2.0 fold_chunks.1
  77.7 20.1 %all_to_all.29.parts_ref = bf16[16,16,256]{2,1,0:T(8,128)(2,1)} all-to-all(bf16[16,16,256]{2,1,0:T(8,128)(2,1)} %fold_chunks.1), channel_id=1, replica_groups=mesh['pipe'=4,'y'=2,'z'=16,'x'=4,'core'=2] {'z'}, dimensions={0} | all-to-all | bytes 262144 | tf_op jit(solution)/shard_map/all_to_all | solution.py:336
  97.8 1.7 fold.1
  99.4 7.6 %all-to-all-start.2 = ((f32[16,16,256]{2,1,0:T(8,128)}), f32[16,16,256]{2,1,0:T(8,128)S(1)}, u32[]{:S(2)}, u32[]{:S(2)}) async-start(f32[16,16,256]{2,1,0:T(8,128)} %fold.1), calls=%async_computation.2 | async-start | bytes 524288 | tf_op jit(solution)/shard_map/all_to_all | solution.py:337
  107.1 0.6 dynamic_slice.9.count_ref
  107.6 24.7 %all-gather.4.cloned.1.call-done = f32[64,32,128]{2,1,0:T(8,128)} async-done(((f32[4,32,128]{2,1,0:T(8,128)}), f32[64,32,128]{2,1,0:T(8,128)}) %all-gather.4.cloned.1.call-update) | async-done | bytes 1048592 | tf_op jit(solution)/shard_map/all_gather | solution.py:312
  132.3 1.3 copy.18
  133.6 0.9 copy.19
  134.5 0.0 all-to-all-done.2.sums_ref
  134.5 0.7 copy-done.4
  135.2 2.5 %total_of.1 = (f32[16,4096]{1,0:T(8,128)}, f32[64,8,128]{2,1,0:T(8,128)}) custom-call(s32[1]{0:T(128)} %dynamic_slice.9.count_ref, f32[16,16,256]{2,1,0:T(8,128)} %copy-done.4, f32[16,4096]{1,0:T(8,128)} %bitcast.32), custom_call_target="tpu_custom_call" | custom-call | tf_op jit(solution)/shard_map/total_of/pallas_call | solution.py:215
  137.7 17.8 %all-to-all-start.3 = ((f32[64,8,128]{2,1,0:T(8,128)}), f32[64,8,128]{2,1,0:T(8,128)S(1)}, u32[]{:S(2)}, u32[]{:S(2)}) async-start(f32[64,8,128]{2,1,0:T(8,128)} %get-tuple-element.11), calls=%async_computation.3 | async-start | bytes 524288 | tf_op jit(solution)/shard_map/all_to_all | solution.py:343
  155.5 0.1 slice.28
  155.6 1.0 slice.23.state_ref
  156.6 12.1 %all-to-all-done.3.squares_ref = f32[64,8,128]{2,1,0:T(8,128)S(1)} async-done(((f32[64,8,128]{2,1,0:T(8,128)}), f32[64,8,128]{2,1,0:T(8,128)S(1)}, u32[]{:S(2)}, u32[]{:S(2)}) %all-to-all-start.3) | async-done | bytes 262176 | tf_op jit(solution)/shard_map/all_to_all | solution.py:343
  168.7 0.7 copy-done.3
  169.4 2.3 %fresh_weights.1 = (bf16[16,4096]{1,0:T(8,128)(2,1)}, f32[8,128]{1,0:T(8,128)}) custom-call(f32[64,8,128]{2,1,0:T(8,128)} %copy-done.3, f32[16,4096]{1,0:T(8,128)} %get-tuple-element.12.total_ref, f32[3,16,4096]{2,1,0:T(8,128)} %slice.23.state_ref), custom_call_target="tpu_custom_call" | custom-call | tf_op jit(solution)/shard_map/fresh_weights/pallas_call | solution.py:248
  171.7 5.7 %all-gather.1 = bf16[32,4096]{1,0:T(8,128)(2,1)S(1)} all-gather(bf16[16,4096]{1,0:T(8,128)(2,1)} %get-tuple-element.13), channel_id=3, replica_groups=mesh['pipe'=4,'y'=2,'z'=16,'x'=4,'core'=2] {'y'}, dimensions={0}, use_global_device_ids=true | all-gather | bytes 393216 | tf_op jit(solution)/shard_map/all_gather | solution.py:346
  177.4 0.1 broadcast_in_dim.12
  177.5 15.8 %all_to_all.30 = bf16[4,2,16,4096]{3,2,1,0:T(8,128)(2,1)S(1)} all-to-all(bf16[4,2,16,4096]{3,2,1,0:T(8,128)(2,1)S(1)} %broadcast_in_dim.12), channel_id=1, replica_groups=mesh['pipe'=4,'y'=2,'z'=16,'x'=4,'core'=2] {'x'}, dimensions={0} | all-to-all | bytes 2097152 | tf_op jit(solution)/shard_map/all_to_all | solution.py:348
  193.3 4.5 %collective-permute-start.7 = (bf16[128,4096]{1,0:T(8,128)(2,1)S(1)}, bf16[128,4096]{1,0:T(8,128)(2,1)S(1)}, u32[]{:S(2)}, u32[]{:S(2)}) collective-permute-start(bf16[128,4096]{1,0:T(8,128)(2,1)S(1)} %bitcast.29), channel_id=1, source_target_pairs={{0,1},{1,0},{2,3},{3,2},{4,5},{5,4},{6,7},{7,6},{8,9},{9,8},{10,11... | collective-permute-start | bytes 3145736 | tf_op jit(solution)/shard_map/ppermute | solution.py:295
  197.9 0.7 fusion.order_ref
  198.6 1.2 slice.24
  199.8 1.6 dynamic-slice_multiply_fusion
  201.3 0.6 multiply_subtract_fusion
  202.0 2.4 %place.2.refs_0_ = bf16[128,8192]{1,0:T(8,128)(2,1)} custom-call(s32[1]{0:T(128)} %bitcast.core_ref.side_ref, bf16[128,128]{1,0:T(8,128)(2,1)} %fusion.order_ref, bf16[128,4096]{1,0:T(8,128)(2,1)} %bitcast.30), custom_call_target="tpu_custom_call" | custom-call | flops 134217728 | bytes 2097152 | tf_op jit(solution)/shard_map/place/pallas_call | solution.py:269
  204.4 1.0 copy-done.5
  205.4 2.4 %place.3 = bf16[128,8192]{1,0:T(8,128)(2,1)} custom-call(s32[1]{0:T(128)S(6)} %sub.26.side_ref, bf16[128,128]{1,0:T(8,128)(2,1)} %fusion.order_ref, bf16[128,4096]{1,0:T(8,128)(2,1)} %copy-done.5, bf16[128,8192]{1,0:T(8,128)(2,1)} %place.2.refs_0_), custom_call_target="tpu_custom_call", output_to_operand_aliasing={{}: (3, {})} | custom-call | flops 134217728 | bytes 2097152 | tf_op jit(solution)/shard_map/place/pallas_call | solution.py:269
  (28 shorter events, 0.1 us)
Async XLA Ops:
  7.2 1.3 copy-start.6
  8.6 41.7 %collective-permute-start = (bf16[128,4224]{1,0:T(8,128)(2,1)S(1)}, bf16[128,4224]{1,0:T(8,128)(2,1)S(1)}, u32[]{:S(2)}, u32[]{:S(2)}) collective-permute-start(bf16[128,4224]{1,0:T(8,128)(2,1)S(1)} %pad_maximum_fusion), channel_id=1, source_target_pairs={{0,1},{1,0},{2,3},{3,2},{4,5},{5,4},{6,7},{7,6},{8,9},{9,8},{10,11... | collective-permute-start | bytes 3244040 | tf_op jit(solution)/shard_map/ppermute | solution.py:295
  25.5 9.5 %collective-permute-start.5 = (bf16[128,256]{1,0:T(8,128)(2,1)S(1)}, bf16[128,256]{1,0:T(8,128)(2,1)S(1)}, u32[]{:S(2)}, u32[]{:S(2)}) collective-permute-start(bf16[128,256]{1,0:T(8,128)(2,1)S(1)} %slice.26), channel_id=1, source_target_pairs={{512,0},{513,1},{514,2},{515,3},{516,4},{517,5},{518,6},{519,7},{5... | collective-permute-start | bytes 196616 | tf_op jit(solution)/shard_map/ppermute | solution.py:320
  26.8 9.5 %collective-permute-start.4 = (bf16[128,256]{1,0:T(8,128)(2,1)S(1)}, bf16[128,256]{1,0:T(8,128)(2,1)S(1)}, u32[]{:S(2)}, u32[]{:S(2)}) collective-permute-start(bf16[128,256]{1,0:T(8,128)(2,1)S(1)} %slice.26), channel_id=1, source_target_pairs={{512,256},{256,0},{513,257},{257,1},{514,258},{258,2},{515,259},{2... | collective-permute-start | bytes 196616 | tf_op jit(solution)/shard_map/ppermute | solution.py:319
  32.2 7.9 %collective-permute-start.3 = (f32[128,128]{1,0:T(8,128)}, f32[128,128]{1,0:T(8,128)S(1)}, u32[]{:S(2)}, u32[]{:S(2)}) collective-permute-start(f32[128,128]{1,0:T(8,128)} %known_part.1.own_ref), channel_id=1, source_target_pairs={{768,0},{769,1},{770,2},{771,3},{772,4},{773,5},{774,6},{775,7},{7... | collective-permute-start | bytes 196616 | tf_op jit(solution)/shard_map/ppermute | solution.py:291
  33.5 9.7 %collective-permute-start.2 = (f32[128,128]{1,0:T(8,128)}, f32[128,128]{1,0:T(8,128)S(1)}, u32[]{:S(2)}, u32[]{:S(2)}) collective-permute-start(f32[128,128]{1,0:T(8,128)} %known_part.1.own_ref), channel_id=1, source_target_pairs={{512,0},{768,256},{513,1},{769,257},{514,2},{770,258},{515,3},{771... | collective-permute-start | bytes 196616 | tf_op jit(solution)/shard_map/ppermute | solution.py:291
  35.0 8.2 %copy-start.8 = (bf16[128,256]{1,0:T(8,128)(2,1)}, bf16[128,256]{1,0:T(8,128)(2,1)S(1)}, u32[]{:S(2)}) copy-start(bf16[128,256]{1,0:T(8,128)(2,1)S(1)} %collective-permute-done.5.w_two_ref) | copy-start | bytes 196612
  35.0 8.1 %collective-permute-start.1 = (f32[128,128]{1,0:T(8,128)}, f32[128,128]{1,0:T(8,128)S(1)}, u32[]{:S(2)}, u32[]{:S(2)}) collective-permute-start(f32[128,128]{1,0:T(8,128)} %known_part.1.own_ref), channel_id=1, source_target_pairs={{256,0},{512,256},{768,512},{257,1},{513,257},{769,513},{258,2},{5... | collective-permute-start | bytes 196616 | tf_op jit(solution)/shard_map/ppermute | solution.py:291
  36.3 6.8 %copy-start.9 = (bf16[128,256]{1,0:T(8,128)(2,1)}, bf16[128,256]{1,0:T(8,128)(2,1)S(1)}, u32[]{:S(2)}) copy-start(bf16[128,256]{1,0:T(8,128)(2,1)S(1)} %collective-permute-done.4.w_one_ref) | copy-start | bytes 196612
  40.1 3.1 %copy-start.10 = (f32[128,128]{1,0:T(8,128)}, f32[128,128]{1,0:T(8,128)S(1)}, u32[]{:S(2)}) copy-start(f32[128,128]{1,0:T(8,128)S(1)} %collective-permute-done.3.three_ref) | copy-start | bytes 196612
  43.2 0.6 copy-start.11
  43.8 0.6 copy-start.12
  46.8 4.2 %collective-permute-start.6 = (bf16[128,512]{1,0:T(8,128)(2,1)}, bf16[128,512]{1,0:T(8,128)(2,1)S(1)}, u32[]{:S(2)}, u32[]{:S(2)}) collective-permute-start(bf16[128,512]{1,0:T(8,128)(2,1)} %get-tuple-element.10.head_a_ref), channel_id=1, source_target_pairs={{0,1},{1,0},{2,3},{3,2},{4,5},{5,4},{6,7},{7,6},{8,9},{9,8},{10,11... | collective-permute-start | bytes 393224 | tf_op jit(solution)/shard_map/ppermute | solution.py:295
  50.3 1.0 copy-start.2
  51.0 0.7 copy-start.7
  56.0 3.8 %copy-start.13 = (f32[1,32,128]{2,1,0:T(8,128)S(1)}, f32[1,32,128]{2,1,0:T(8,128)}, u32[]{:S(2)}) copy-start(f32[1,32,128]{2,1,0:T(8,128)} %param.13) | copy-start | bytes 49156
  56.0 3.8 %copy-start.14 = (f32[1,32,128]{2,1,0:T(8,128)S(1)}, f32[1,32,128]{2,1,0:T(8,128)}, u32[]{:S(2)}) copy-start(f32[1,32,128]{2,1,0:T(8,128)} %param.12) | copy-start | bytes 49156
  56.0 3.8 %copy-start.15 = (f32[1,32,128]{2,1,0:T(8,128)S(1)}, f32[1,32,128]{2,1,0:T(8,128)}, u32[]{:S(2)}) copy-start(f32[1,32,128]{2,1,0:T(8,128)} %param.11) | copy-start | bytes 49156
  56.1 3.8 %copy-start.16 = (f32[1,32,128]{2,1,0:T(8,128)S(1)}, f32[1,32,128]{2,1,0:T(8,128)}, u32[]{:S(2)}) copy-start(f32[1,32,128]{2,1,0:T(8,128)} %param.14) | copy-start | bytes 49156
  56.1 51.0 %copy-start.17 = (s32[4]{0:T(128)S(1)}, s32[4]{0:T(128)}, u32[]{:S(2)}) copy-start(s32[4]{0:T(128)} %param.15) | copy-start | bytes 52
  56.1 18.6 %all-to-all-start = ((bf16[8,16,4096]{2,1,0:T(8,128)(2,1)}), bf16[8,16,4096]{2,1,0:T(8,128)(2,1)S(1)}, u32[]{:S(2)}, u32[]{:S(2)}) async-start(bf16[8,16,4096]{2,1,0:T(8,128)(2,1)} %bitcast.26), calls=%async_computation | async-start | bytes 2097152 | tf_op jit(solution)/shard_map/all_to_all | solution.py:334
  59.8 72.5 %all-gather.4.cloned.1.call-start = ((), (), s32[]{:S(2)}) async-start(), calls=%async_computation.5 | async-start | bytes 1114112 | tf_op jit(solution)/shard_map/all_gather | solution.py:312
  74.7 1.0 copy-start.1
  99.4 35.1 %all-to-all-start.2 = ((f32[16,16,256]{2,1,0:T(8,128)}), f32[16,16,256]{2,1,0:T(8,128)S(1)}, u32[]{:S(2)}, u32[]{:S(2)}) async-start(f32[16,16,256]{2,1,0:T(8,128)} %fold.1), calls=%async_computation.2 | async-start | bytes 524288 | tf_op jit(solution)/shard_map/all_to_all | solution.py:337
  134.5 0.7 copy-start.4
  137.7 30.9 %all-to-all-start.3 = ((f32[64,8,128]{2,1,0:T(8,128)}), f32[64,8,128]{2,1,0:T(8,128)S(1)}, u32[]{:S(2)}, u32[]{:S(2)}) async-start(f32[64,8,128]{2,1,0:T(8,128)} %get-tuple-element.11), calls=%async_computation.3 | async-start | bytes 524288 | tf_op jit(solution)/shard_map/all_to_all | solution.py:343
  168.7 0.7 copy-start.3
  193.3 8.7 %copy-start = (bf16[4,2,16,4096]{3,2,1,0:T(8,128)(2,1)}, bf16[4,2,16,4096]{3,2,1,0:T(8,128)(2,1)S(1)}, u32[]{:S(2)}) copy-start(bf16[4,2,16,4096]{3,2,1,0:T(8,128)(2,1)S(1)} %all_to_all.30) | copy-start | bytes 3145732
  193.3 11.1 %collective-permute-start.7 = (bf16[128,4096]{1,0:T(8,128)(2,1)S(1)}, bf16[128,4096]{1,0:T(8,128)(2,1)S(1)}, u32[]{:S(2)}, u32[]{:S(2)}) collective-permute-start(bf16[128,4096]{1,0:T(8,128)(2,1)S(1)} %bitcast.29), channel_id=1, source_target_pairs={{0,1},{1,0},{2,3},{3,2},{4,5},{5,4},{6,7},{7,6},{8,9},{9,8},{10,11... | collective-permute-start | bytes 3145736 | tf_op jit(solution)/shard_map/ppermute | solution.py:295
  204.4 1.0 copy-start.5
Sparse Core Ops, SparseCore 0:
  63.3 68.9 all-gather.3

commit v3 on v2

--- a/solution.py
+++ b/solution.py
@@ -113,52 +113,82 @@
     )(section, top_grad, *known, *weights)
 
 
-def product_kernel(core_ref, order_ref, slab_a_ref, slab_b_ref, head_a_ref, head_b_ref, top_ref, other_ref, out_ref, a_ref, b_ref, *, span):
-    step = pl.program_id(0)
-
-    @pl.when(step == 0)
+def turn_kernel(order_ref, a_in_ref, b_in_ref, a_ref, b_ref):
+    a_ref[...] = dot(order_ref[...], a_in_ref[...], ((1,), (1,))).astype(bf16)
+    b_ref[...] = dot(order_ref[...], b_in_ref[...], ((1,), (1,))).astype(bf16)
+
+
+def tail_kernel(core_ref, order_ref, slab_a_ref, slab_b_ref, top_ref, other_ref, out_ref, a_ref, b_ref):
+    @pl.when(pl.program_id(0) == 0)
     def _():
-        a_ref[...] = dot(order_ref[...], slab_a_ref[...], ((1,), (1,))).astype(bf16)
-        b_ref[...] = dot(order_ref[...], slab_b_ref[...], ((1,), (1,))).astype(bf16)
+        turn_kernel(order_ref, slab_a_ref, slab_b_ref, a_ref, b_ref)
 
     out_ref[...] = (
         dot(a_ref[...], top_ref[...], ((1,), (0,))) + dot(b_ref[...], other_ref[...], ((1,), (0,)))
     ).astype(bf16)
 
-    @pl.when((step == 0) & (core_ref[0] == 0))
+
+def tail_product(core, order, slab_a, top_grad, other, span):
+    rows, width = top_grad.shape
+    slab = slab_a.shape[1]
+    half = width // 2
+    blocks = half // span
+    whole = pl.BlockSpec((rows, slab), lambda i, c: (0, 0))
+    turned = pl.BlockSpec((slab, rows), lambda i, c: (0, 0))
+    return pl.pallas_call(
+        tail_kernel,
+        grid_spec=pltpu.PrefetchScalarGridSpec(
+            num_scalar_prefetch=1,
+            grid=(blocks - 1,),
+            in_specs=[
+                turned,
+                whole,
+                pl.BlockSpec((rows, slab), lambda i, c: (0, half // slab)),
+                pl.BlockSpec((rows, span), lambda i, c: (0, c[0] * blocks + i + 1)),
+                pl.BlockSpec((rows, span), lambda i, c: (0, i + 1)),
+            ],
+            out_specs=[pl.BlockSpec((slab, span), lambda i, c: (0, i)), turned, turned],
+        ),
+        out_shape=[
+            jax.ShapeDtypeStruct((slab, half - span), bf16),
+            jax.ShapeDtypeStruct((slab, rows), bf16),
+            jax.ShapeDtypeStruct((slab, rows), bf16),
+        ],
+        name="tail_product",
+    )(core, order, slab_a, other, top_grad, other)
+
+
+def head_kernel(core_ref, a_ref, b_ref, head_a_ref, head_b_ref, top_ref, other_ref, out_ref):
+    @pl.when(core_ref[0] == 0)
     def _():
-        out_ref[:, :span] = (
+        out_ref[...] = (
             dot(a_ref[...], head_a_ref[...], ((1,), (0,))) + dot(b_ref[...], head_b_ref[...], ((1,), (0,)))
         ).astype(bf16)
 
-
-def slab_product(core, order, slab_a, slab_b, head_a, head_b, top_grad, other, steps):
-    rows = top_grad.shape[0]
-    slab = slab_a.shape[1]
-    half = top_grad.shape[1] // 2
-    span = head_a.shape[1]
-    block = half // steps
-    whole = lambda shape: pl.BlockSpec(shape, lambda i, c: (0, 0))
-    return pl.pallas_call(
-        functools.partial(product_kernel, span=span),
+    @pl.when(core_ref[0] != 0)
+    def _():
+        out_ref[...] = (
+            dot(a_ref[...], top_ref[...], ((1,), (0,))) + dot(b_ref[...], other_ref[...], ((1,), (0,)))
+        ).astype(bf16)
+
+
+def head_product(core, a, b, head_a, head_b, top_grad, other):
+    rows, span = head_a.shape
+    slab = a.shape[0]
+    blocks = top_grad.shape[1] // 2 // span
+    turned = pl.BlockSpec((slab, rows), lambda i, c: (0, 0))
+    first = pl.BlockSpec((rows, span), lambda i, c: (0, 0))
+    return pl.pallas_call(
+        head_kernel,
         grid_spec=pltpu.PrefetchScalarGridSpec(
             num_scalar_prefetch=1,
-            grid=(steps,),
-            in_specs=[
-                whole((slab, slab)),
-                whole((rows, slab)),
-                whole((rows, slab)),
-                whole((rows, span)),
-                whole((rows, span)),
-                pl.BlockSpec((rows, block), lambda i, c: (0, c[0] * steps + i)),
-                pl.BlockSpec((rows, block), lambda i, c: (0, i)),
-            ],
-            out_specs=pl.BlockSpec((slab, block), lambda i, c: (0, i)),
-            scratch_shapes=[pltpu.VMEM((slab, rows), bf16), pltpu.VMEM((slab, rows), bf16)],
-        ),
-        out_shape=jax.ShapeDtypeStruct((slab, half), bf16),
-        name="slab_product",
-    )(core, order, slab_a, slab_b, head_a, head_b, top_grad, other)
+            grid=(1,),
+            in_specs=[turned, turned, first, first, pl.BlockSpec((rows, span), lambda i, c: (0, c[0] * blocks)), first],
+            out_specs=pl.BlockSpec((slab, span), lambda i, c: (0, 0)),
+        ),
+        out_shape=jax.ShapeDtypeStruct((slab, span), bf16),
+        name="head_product",
+    )(core, a, b, head_a, head_b, top_grad, other)
 
 
 def fold_kernel(parts_ref, out_ref, *, count):
@@ -179,49 +209,55 @@
     )(parts)
 
 
-def fold_chunks_kernel(parts_ref, out_ref, *, count, chunks):
-    width = out_ref.shape[2]
+def fold_chunks_kernel(row_ref, accum_ref, head_ref, tail_ref, out_ref, *, tokens):
+    count, rows, span = head_ref.shape
+    chunks, _, width = out_ref.shape
+    own = lax.broadcasted_iota(jnp.int32, (rows, width), 0) == row_ref[0]
     for j in range(chunks):
-        cols = slice(j * width, (j + 1) * width)
-        total = parts_ref[0, :, cols].astype(f32)
-        for i in range(1, count):
-            total = total + parts_ref[i, :, cols].astype(f32)
-        out_ref[j] = total.astype(out_ref.dtype)
-
-
-def fold_chunks(parts, chunks):
-    count, rows, width = parts.shape
-    return pl.pallas_call(
-        functools.partial(fold_chunks_kernel, count=count, chunks=chunks),
-        in_specs=[vmem_spec()],
+        at = j * width
+        ref, start = (head_ref, at) if at < span else (tail_ref, at - span)
+        cols = slice(start, start + width)
+        total = jnp.where(own, accum_ref[:, at : at + width] * tokens, 0.0)
+        for i in range(count):
+            total = total + ref[i, :, cols].astype(f32)
+        out_ref[j] = total.astype(bf16)
+
+
+def fold_chunks(row, accum, head, tail, chunks, tokens):
+    rows = head.shape[1]
+    width = accum.shape[1]
+    return pl.pallas_call(
+        functools.partial(fold_chunks_kernel, tokens=float(tokens)),
+        in_specs=[pl.BlockSpec(memory_space=pltpu.SMEM)] + [vmem_spec()] * 3,
         out_specs=vmem_spec(),
         out_shape=jax.ShapeDtypeStruct((chunks, rows, width // chunks), bf16),
         name="fold_chunks",
-    )(parts)
-
-
-def total_kernel(count_ref, sums_ref, accum_ref, total_ref, square_ref, *, chunks, tokens):
-    width = sums_ref.shape[2]
-    square = jnp.zeros((accum_ref.shape[0], width), f32)
+    )(row, accum, head, tail)
+
+
+def total_kernel(count_ref, sums_ref, total_ref, square_ref, *, chunks, tokens):
+    rows, width = sums_ref.shape[1:]
+    square = jnp.zeros((rows, width), f32)
     for j in range(chunks):
         cols = slice(j * width, (j + 1) * width)
-        total = accum_ref[:, cols] + sums_ref[j] * (1.0 / tokens)
+        total = sums_ref[j] * (1.0 / tokens)
         total_ref[:, cols] = total
         square = square + total * total
     square_ref[...] = jnp.full(square_ref.shape, jnp.sum(square) * count_ref[0].astype(f32), f32)
 
 
-def total_of(count, sums, accum, tokens, peers):
+def total_of(count, sums, tokens, peers):
+    chunks, rows, width = sums.shape
     return pl.pallas_call(
         functools.partial(total_kernel, chunks=sums.shape[0], tokens=tokens),
-        in_specs=[pl.BlockSpec(memory_space=pltpu.SMEM)] + [vmem_spec()] * 2,
+        in_specs=[pl.BlockSpec(memory_space=pltpu.SMEM), vmem_spec()],
         out_specs=[vmem_spec()] * 2,
         out_shape=[
-            jax.ShapeDtypeStruct(accum.shape, f32),
+            jax.ShapeDtypeStruct((rows, chunks * width), f32),
             jax.ShapeDtypeStruct((peers, 8, 128), f32),
         ],
         name="total_of",
-    )(count, sums, accum)
+    )(count, sums)
 
 
 def adam(total_grad, master, moment1, moment2, clip_factor):
@@ -313,35 +349,47 @@
 
     sent = lax.dynamic_slice(top_grad, (0, (1 - core) * half), (rows, half))
     other = swap(jnp.concatenate([sent, slab_own], axis=1), "core")
-    slab_other = other[:, half:]
-
-    w_sent = weight[:, 2 * slab : span]
+
+    known = known_part(section[None], top_grad, weight, slab, span, 4)
+    known_all = [known, down(known, 1), down(known, 2), down(known, 3)]
+    w_sent = lax.optimization_barrier((weight, known))[0][:, 2 * slab : span]
     w_one = lax.ppermute(w_sent, "pipe", [(2, 1), (1, 0)])
     w_two = lax.ppermute(w_sent, "pipe", [(2, 0)])
-    known = known_part(section[None], top_grad, weight, slab, span, 4)
-    known_all = [known, down(known, 1), down(known, 2), down(known, 3)]
+
+    here = jnp.arange(slab)
+    source = here // (n_x * n_z) * (n_x * n_z) + here % n_z * n_x + here // n_z % n_x
+    order = (here[None, :] == source[:, None]).astype(bf16)
+    other, known = lax.optimization_barrier((other, known))
+    tail, slab_a, slab_b = tail_product(core[None], order, slab_own, top_grad, other, span)
+    tail = lax.all_to_all(tail, ("y", "x"), split_axis=0, concat_axis=0, tiled=True)
+
     head, section_grad = relay(
         section[None], top_grad, known_all, [weight, w_one, w_two], slab, span
     )
     head_other = swap(head, "core")
-
-    here = jnp.arange(slab)
-    source = here // (n_x * n_z) * (n_x * n_z) + here % n_z * n_x + here // n_z % n_x
-    order = (here[None, :] == source[:, None]).astype(bf16)
-    product = slab_product(
-        core[None], order, slab_own, slab_other, head, head_other, top_grad, other, 4
+    ahead = head_product(core[None], slab_a, slab_b, head, head_other, top_grad, other)
+    ahead, tail = lax.optimization_barrier((ahead, tail))
+    ahead = lax.all_to_all(ahead, ("y", "x"), split_axis=0, concat_axis=0, tiled=True)
+
+    row = lax.axis_index("z").astype(jnp.int32)
+    parts = fold_chunks(
+        row[None],
+        grad_accum[0].reshape(1, half),
+        ahead.reshape(n_y * n_x, n_z, span),
+        tail.reshape(n_y * n_x, n_z, half - span),
+        n_z,
+        tokens,
     )
-    parts = lax.all_to_all(product, ("y", "x"), split_axis=0, concat_axis=0, tiled=True)
-    parts = fold_chunks(parts.reshape(n_y * n_x, n_z, half), n_z)
     parts = lax.all_to_all(parts, "z", split_axis=0, concat_axis=0, tiled=True)
     sums = lax.all_to_all(fold(parts), "z", split_axis=0, concat_axis=0, tiled=True)
 
-    state = state.transpose(1, 0, 2, 3).reshape(4, n_z, half)
     group = ("pipe", "y", "x", "core")
     count = lax.dynamic_slice(layer_counts, (section,), (1,))
-    total_grad, squares = total_of(count, sums, state[3], tokens, lax.axis_size(group))
+    total_grad, squares = total_of(count, sums, tokens, lax.axis_size(group))
+    squares, state = lax.optimization_barrier((squares, state))
     squares = lax.all_to_all(squares, group, split_axis=0, concat_axis=0, tiled=True)
 
+    state = state.transpose(1, 0, 2, 3).reshape(4, n_z, half)
     fresh, factor = fresh_weights(squares, total_grad, state[:3])
     fresh = lax.all_gather(fresh, "y", axis=0, tiled=False)
     fresh = jnp.broadcast_to(fresh[None], (n_x, n_y, n_z, half))
@@ -353,7 +401,7 @@
     new_weights = place(core[None], order, fresh, 2)
     new_weights = place(1 - core[None], order, fresh_other, 2, new_weights)
 
-    own = lax.dynamic_slice(total_grad, (lax.axis_index("z"), 0), (1, half)).reshape(shard)
+    own = lax.dynamic_slice(total_grad, (row, 0), (1, half)).reshape(shard)
     adam_step, new_master = adam(own, master[0], moment1[0], moment2[0], factor[0, 0])
     return (new_weights[None], adam_step[None], new_master[None], section_grad[None])
 

time: 216 us -> 203 us (0.940)
  waiting for transfers between devices: 58 us -> 36.8 us
  blocking collectives: 41.7 us -> 48.1 us
  Pallas kernels: 24.2 us -> 27.6 us
    all_gather x1, waiting for transfers between devices: 24.7 us -> 0.01 us  [local(): state = lax.all_gather(state, 'z', axis=0, tiled=False)]
    all_to_all x1, waiting for transfers between devices: 0.01 us -> 12.4 us  [local(): lax.all_to_all(fold(parts), 'z', split_axis=0, concat_axis=0, tiled=True)]
    all_to_all x1 -> x2, waiting for transfers between devices: 14.2 us -> 5.46 us  [the longest x1 5.46 us: local(): lax.all_to_all(ahead, ('y', 'x'), split_axis=0, concat_axis=0, tiled=True)]
    all_to_all x1, starting transfers between devices: 17.8 us -> 10.5 us  [local(): lax.all_to_all(squares, group, split_axis=0, concat_axis=0, tiled=True)]
    all_to_all x1 -> x2, starting transfers between devices: 3.7 us -> 10.4 us  [the longest x1 6.76 us: local(): lax.all_to_all(ahead, ('y', 'x'), split_axis=0, concat_axis=0, tiled=True)]
    all_to_all x1, blocking collectives: 20.1 us -> 26.5 us  [local(): parts = lax.all_to_all(parts, 'z', split_axis=0, concat_axis=0, tiled=True)]
    pallas_call x2 -> x3, Pallas kernels: 6.44 us -> 9.97 us  [the longest x1 5.88 us: tail_product(): pl.pallas_call(tail_kernel, grid_spec=pltpu.PrefetchScalarGridSpec(num_sc...]
    ppermute x3, waiting for transfers between devices: 6.82 us -> 3.9 us  [down(): return lax.ppermute(x, 'pipe', [(i, i - by) for i in range(by, 4)])]
  transfers between devices with their start and end apart: 12 -> 13, of which waited for: 6 -> 7; matrix products, arithmetic and copies ran while one was open for 5% -> 5% of each run, Pallas kernels for 6% -> 8%
where the time goes in v3:
time: 203 us; the launch traced here: 201 us
  starting transfers between devices  57.9 us (29%)
  blocking collectives  48.1 us (24%)
  waiting for transfers between devices  36.8 us (18%)
  Pallas kernels  27.6 us (14%)
  between operations  14.3 us (7%)
  local copies, waits for them, and re-layouts  12.3 us (6%)
  other arithmetic  4.31 us (2%)
    all_to_all x1, blocking collectives, local(): parts = lax.all_to_all(parts, 'z', split_axis=0, concat_axis=0, tiled=True)  26.5 us
    ppermute x3, starting transfers between devices, swap(): return lax.ppermute(x, axis, [(0, 1), (1, 0)])  23.3 us
    all_to_all x1, blocking collectives, local(): fresh = lax.all_to_all(fresh, 'x', split_axis=0, concat_axis=0, tiled=True)  15.9 us
    all_to_all x1, waiting for transfers between devices, local(): lax.all_to_all(fold(parts), 'z', split_axis=0, concat_axis=0, tiled=True)  12.4 us
    all_to_all x1, waiting for transfers between devices, local(): lax.all_to_all(squares, group, split_axis=0, concat_axis=0, tiled=True)  10.9 us
    all_to_all x1, starting transfers between devices, local(): lax.all_to_all(squares, group, split_axis=0, concat_axis=0, tiled=True)  10.5 us
    all_to_all x1, starting transfers between devices, local(): lax.all_to_all(fold(parts), 'z', split_axis=0, concat_axis=0, tiled=True)  7.15 us
    all_to_all x1, starting transfers between devices, local(): lax.all_to_all(ahead, ('y', 'x'), split_axis=0, concat_axis=0, tiled=True)  6.76 us
  transfers between devices with their start and end apart: 13, of which 7 were waited for; matrix products, arithmetic and copies ran while one was open for 5% of the time, Pallas kernels for 8%

profile of v3, /device:TPU:1, one launch (start us, length us, event | category | flops | bytes accessed | tf_op | source)
XLA Modules:
  0.0 201.4 jit_solution(182226787297146955)
XLA Ops:
  7.2 0.0 copy-start.8
  7.2 1.3 constant_dynamic-slice_fusion
  8.5 0.0 copy-done.8
  8.5 0.1 pad_maximum_fusion
  8.6 16.1 %collective-permute-start = (bf16[128,4224]{1,0:T(8,128)(2,1)S(1)}, bf16[128,4224]{1,0:T(8,128)(2,1)S(1)}, u32[]{:S(2)}, u32[]{:S(2)}) collective-permute-start(bf16[128,4224]{1,0:T(8,128)(2,1)S(1)} %pad_maximum_fusion), channel_id=1, source_target_pairs={{0,1},{1,0},{2,3},{3,2},{4,5},{5,4},{6,7},{7,6},{8,9},{9,8},{10,11... | collective-permute-start | bytes 3244040 | tf_op jit(solution)/shard_map/ppermute | solution.py:331
  24.7 4.1 %known_part.1.own_ref = f32[128,128]{1,0:T(8,128)} custom-call(s32[1]{0:T(128)} %bitcast.4.section_ref, bf16[128,8192]{1,0:T(8,128)(2,1)} %top_ref.7, bf16[128,8192]{1,0:T(8,128)(2,1)} %bitcast.22), custom_call_target="tpu_custom_call" | custom-call | tf_op jit(solution)/shard_map/known_part/pallas_call | solution.py:50
  28.7 0.7 fusion.1.order_ref
  29.5 0.0 collective-permute-done.slab_b_ref.other_ref
  29.5 1.0 copy-done
  30.4 5.9 %tail_product.1 = (bf16[128,3584]{1,0:T(8,128)(2,1)}, bf16[128,128]{1,0:T(8,128)(2,1)}, bf16[128,128]{1,0:T(8,128)(2,1)}) custom-call(s32[1]{0:T(128)} %bitcast.core_ref.side_ref, bf16[128,128]{1,0:T(8,128)(2,1)} %fusion.1.order_ref, bf16[128,128]{1,0:T(8,128)(2,1)} %bitcast.33, bf16[128,4224]{1,0:T(8,128)(2,1)} %copy-done, bf16[128,8192]{1,0:T(8,128)(2,1)} %top_ref.7, ...), custom_call_target="tpu_custom_call" | custom-call | tf_op jit(solution)/shard_map/tail_product/pallas_call | solution.py:138
  36.3 3.7 %all-to-all-start = ((bf16[8,16,3584]{2,1,0:T(8,128)(2,1)}), bf16[8,16,3584]{2,1,0:T(8,128)(2,1)S(1)}, u32[]{:S(2)}, u32[]{:S(2)}) async-start(bf16[8,16,3584]{2,1,0:T(8,128)(2,1)} %bitcast.31), calls=%async_computation | async-start | bytes 1835008 | tf_op jit(solution)/shard_map/all_to_all | solution.py:364
  40.0 0.0 all-gather.4.cloned.1.call-start
  40.1 0.6 pad_maximum_fusion.1
  40.7 0.0 all-gather.4.cloned.1.call-update
  40.8 0.8 slice.12
  41.6 1.3 collective-permute-start.5
  42.9 1.3 collective-permute-start.4
  44.2 0.0 copy-done.7
  44.2 1.3 collective-permute-start.3
  45.5 1.3 collective-permute-start.2
  46.8 1.3 collective-permute-start.1
  48.1 3.0 %collective-permute-done.5.w_two_ref = bf16[128,256]{1,0:T(8,128)(2,1)S(1)} collective-permute-done((bf16[128,256]{1,0:T(8,128)(2,1)S(1)}, bf16[128,256]{1,0:T(8,128)(2,1)S(1)}, u32[]{:S(2)}, u32[]{:S(2)}) %collective-permute-start.5) | collective-permute-done | bytes 65568 | tf_op jit(solution)/shard_map/ppermute | solution.py:357
  51.1 0.0 collective-permute-done.4.w_one_ref
  51.1 1.8 collective-permute-done.3.three_ref
  52.9 2.1 %collective-permute-done.2.two_ref = f32[128,128]{1,0:T(8,128)S(1)} collective-permute-done((f32[128,128]{1,0:T(8,128)S(1)}, f32[128,128]{1,0:T(8,128)S(1)}, u32[]{:S(2)}, u32[]{:S(2)}) %collective-permute-start.2) | collective-permute-done | bytes 65568 | tf_op jit(solution)/shard_map/ppermute | solution.py:327
  55.0 0.0 collective-permute-done.1.one_ref
  55.1 0.6 copy-done.13
  55.6 0.6 copy-done.14
  56.2 2.4 %relay.1 = (bf16[128,512]{1,0:T(8,128)(2,1)}, bf16[128,128]{1,0:T(8,128)(2,1)}) custom-call(s32[1]{0:T(128)} %bitcast.4.section_ref, bf16[128,8192]{1,0:T(8,128)(2,1)} %top_ref.7, f32[128,128]{1,0:T(8,128)} %known_part.1.own_ref, f32[128,128]{1,0:T(8,128)} %copy-done.14, f32[128,128]{1,0:T(8,128)} %copy-done.13, f32[128,128]{1,0:T(8,128)} %copy-done.12, ...), custom_call_target="tpu_custom_call" | custom-call | tf_op jit(solution)/shard_map/relay/pallas_call | solution.py:100
  58.6 2.8 %collective-permute-start.6 = (bf16[128,512]{1,0:T(8,128)(2,1)}, bf16[128,512]{1,0:T(8,128)(2,1)S(1)}, u32[]{:S(2)}, u32[]{:S(2)}) collective-permute-start(bf16[128,512]{1,0:T(8,128)(2,1)} %get-tuple-element.23.head_a_ref), channel_id=1, source_target_pairs={{0,1},{1,0},{2,3},{3,2},{4,5},{5,4},{6,7},{7,6},{8,9},{9,8},{10,11... | collective-permute-start | bytes 393224 | tf_op jit(solution)/shard_map/ppermute | solution.py:331
  61.4 1.2 collective-permute-done.6.head_b_ref
  62.6 0.7 copy-done.9
  63.2 2.0 head_product.1
  65.3 0.0 all-to-all-done
  65.3 6.8 %all-to-all-start.1 = ((bf16[8,16,512]{2,1,0:T(8,128)(2,1)}), bf16[8,16,512]{2,1,0:T(8,128)(2,1)S(1)}, u32[]{:S(2)}, u32[]{:S(2)}) async-start(bf16[8,16,512]{2,1,0:T(8,128)(2,1)} %bitcast.32), calls=%async_computation.1 | async-start | bytes 262144 | tf_op jit(solution)/shard_map/all_to_all | solution.py:372
  72.0 5.5 %all-to-all-done.1.head_ref = bf16[8,16,512]{2,1,0:T(8,128)(2,1)S(1)} async-done(((bf16[8,16,512]{2,1,0:T(8,128)(2,1)}), bf16[8,16,512]{2,1,0:T(8,128)(2,1)S(1)}, u32[]{:S(2)}, u32[]{:S(2)}) %all-to-all-start.1) | async-done | bytes 131104 | tf_op jit(solution)/shard_map/all_to_all | solution.py:372
  77.5 0.6 copy-done.6
  78.1 2.1 %fold_chunks.1 = bf16[16,16,256]{2,1,0:T(8,128)(2,1)} custom-call(s32[1]{0:T(128)} %bitcast.1.row_ref, f32[1,4096]{1,0:T(1,128)} %bitcast.35, bf16[8,16,512]{2,1,0:T(8,128)(2,1)} %copy-done.6, bf16[8,16,3584]{2,1,0:T(8,128)(2,1)} %copy-done.2), custom_call_target="tpu_custom_call" | custom-call | tf_op jit(solution)/shard_map/fold_chunks/pallas_call | solution.py:229
  80.2 26.5 %all_to_all.41.parts_ref = bf16[16,16,256]{2,1,0:T(8,128)(2,1)} all-to-all(bf16[16,16,256]{2,1,0:T(8,128)(2,1)} %fold_chunks.1), channel_id=1, replica_groups=mesh['pipe'=4,'y'=2,'z'=16,'x'=4,'core'=2] {'z'}, dimensions={0} | all-to-all | bytes 262144 | tf_op jit(solution)/shard_map/all_to_all | solution.py:383
  106.7 1.6 fold.1
  108.4 7.2 %all-to-all-start.3 = ((f32[16,16,256]{2,1,0:T(8,128)}), f32[16,16,256]{2,1,0:T(8,128)S(1)}, u32[]{:S(2)}, u32[]{:S(2)}) async-start(f32[16,16,256]{2,1,0:T(8,128)} %fold.1), calls=%async_computation.3 | async-start | bytes 524288 | tf_op jit(solution)/shard_map/all_to_all | solution.py:384
  115.6 0.6 dynamic_slice.9.count_ref
  116.2 12.4 %all-to-all-done.3.sums_ref = f32[16,16,256]{2,1,0:T(8,128)S(1)} async-done(((f32[16,16,256]{2,1,0:T(8,128)}), f32[16,16,256]{2,1,0:T(8,128)S(1)}, u32[]{:S(2)}, u32[]{:S(2)}) %all-to-all-start.3) | async-done | bytes 262176 | tf_op jit(solution)/shard_map/all_to_all | solution.py:384
  128.5 0.7 copy-done.4
  129.2 2.5 %total_of.1 = (f32[16,4096]{1,0:T(8,128)}, f32[64,8,128]{2,1,0:T(8,128)}) custom-call(s32[1]{0:T(128)} %dynamic_slice.9.count_ref, f32[16,16,256]{2,1,0:T(8,128)} %copy-done.4), custom_call_target="tpu_custom_call" | custom-call | tf_op jit(solution)/shard_map/total_of/pallas_call | solution.py:251
  131.7 10.5 %all-to-all-start.4 = ((f32[64,8,128]{2,1,0:T(8,128)}), f32[64,8,128]{2,1,0:T(8,128)S(1)}, u32[]{:S(2)}, u32[]{:S(2)}) async-start(f32[64,8,128]{2,1,0:T(8,128)} %get-tuple-element.28), calls=%async_computation.4 | async-start | bytes 524288 | tf_op jit(solution)/shard_map/all_to_all | solution.py:390
  142.2 1.3 copy.16
  143.5 0.1 slice.16
  143.6 1.0 slice.14.state_ref
  144.6 10.9 %all-to-all-done.4.squares_ref = f32[64,8,128]{2,1,0:T(8,128)S(1)} async-done(((f32[64,8,128]{2,1,0:T(8,128)}), f32[64,8,128]{2,1,0:T(8,128)S(1)}, u32[]{:S(2)}, u32[]{:S(2)}) %all-to-all-start.4) | async-done | bytes 262176 | tf_op jit(solution)/shard_map/all_to_all | solution.py:390
  155.5 0.7 copy-done.3
  156.2 2.3 %fresh_weights.1 = (bf16[16,4096]{1,0:T(8,128)(2,1)}, f32[8,128]{1,0:T(8,128)}) custom-call(f32[64,8,128]{2,1,0:T(8,128)} %copy-done.3, f32[16,4096]{1,0:T(8,128)} %get-tuple-element.29.total_ref, f32[3,16,4096]{2,1,0:T(8,128)} %slice.14.state_ref), custom_call_target="tpu_custom_call" | custom-call | tf_op jit(solution)/shard_map/fresh_weights/pallas_call | solution.py:284
  158.4 5.7 %all-gather.1 = bf16[32,4096]{1,0:T(8,128)(2,1)S(1)} all-gather(bf16[16,4096]{1,0:T(8,128)(2,1)} %get-tuple-element.31), channel_id=3, replica_groups=mesh['pipe'=4,'y'=2,'z'=16,'x'=4,'core'=2] {'y'}, dimensions={0}, use_global_device_ids=true | all-gather | bytes 393216 | tf_op jit(solution)/shard_map/all_gather | solution.py:394
  164.1 0.1 broadcast_in_dim.15
  164.2 15.9 %all_to_all.42 = bf16[4,2,16,4096]{3,2,1,0:T(8,128)(2,1)S(1)} all-to-all(bf16[4,2,16,4096]{3,2,1,0:T(8,128)(2,1)S(1)} %broadcast_in_dim.15), channel_id=1, replica_groups=mesh['pipe'=4,'y'=2,'z'=16,'x'=4,'core'=2] {'x'}, dimensions={0} | all-to-all | bytes 2097152 | tf_op jit(solution)/shard_map/all_to_all | solution.py:396
  180.1 4.5 %collective-permute-start.7 = (bf16[128,4096]{1,0:T(8,128)(2,1)S(1)}, bf16[128,4096]{1,0:T(8,128)(2,1)S(1)}, u32[]{:S(2)}, u32[]{:S(2)}) collective-permute-start(bf16[128,4096]{1,0:T(8,128)(2,1)S(1)} %bitcast.26), channel_id=1, source_target_pairs={{0,1},{1,0},{2,3},{3,2},{4,5},{5,4},{6,7},{7,6},{8,9},{9,8},{10,11... | collective-permute-start | bytes 3145736 | tf_op jit(solution)/shard_map/ppermute | solution.py:331
  184.6 0.7 fusion.order_ref
  185.3 1.2 slice.15
  186.5 1.6 dynamic-slice_multiply_fusion
  188.1 0.6 multiply_subtract_fusion
  188.7 2.4 %place.2.refs_0_ = bf16[128,8192]{1,0:T(8,128)(2,1)} custom-call(s32[1]{0:T(128)} %bitcast.core_ref.side_ref, bf16[128,128]{1,0:T(8,128)(2,1)} %fusion.order_ref, bf16[128,4096]{1,0:T(8,128)(2,1)} %bitcast.27), custom_call_target="tpu_custom_call" | custom-call | flops 134217728 | bytes 2097152 | tf_op jit(solution)/shard_map/place/pallas_call | solution.py:305
  191.1 0.0 collective-permute-done.7.half_ref
  191.1 1.0 copy-done.5
  192.1 2.4 %place.3 = bf16[128,8192]{1,0:T(8,128)(2,1)} custom-call(s32[1]{0:T(128)S(6)} %sub.26.side_ref, bf16[128,128]{1,0:T(8,128)(2,1)} %fusion.order_ref, bf16[128,4096]{1,0:T(8,128)(2,1)} %copy-done.5, bf16[128,8192]{1,0:T(8,128)(2,1)} %place.2.refs_0_), custom_call_target="tpu_custom_call", output_to_operand_aliasing={{}: (3, {})} | custom-call | flops 134217728 | bytes 2097152 | tf_op jit(solution)/shard_map/place/pallas_call | solution.py:305
  (32 shorter events, 0.1 us)
Async XLA Ops:
  7.2 1.3 copy-start.8
  8.6 20.9 %collective-permute-start = (bf16[128,4224]{1,0:T(8,128)(2,1)S(1)}, bf16[128,4224]{1,0:T(8,128)(2,1)S(1)}, u32[]{:S(2)}, u32[]{:S(2)}) collective-permute-start(bf16[128,4224]{1,0:T(8,128)(2,1)S(1)} %pad_maximum_fusion), channel_id=1, source_target_pairs={{0,1},{1,0},{2,3},{3,2},{4,5},{5,4},{6,7},{7,6},{8,9},{9,8},{10,11... | collective-permute-start | bytes 3244040 | tf_op jit(solution)/shard_map/ppermute | solution.py:331
  29.5 1.0 copy-start
  30.4 9.6 %copy-start.15 = (f32[1,32,128]{2,1,0:T(8,128)S(1)}, f32[1,32,128]{2,1,0:T(8,128)}, u32[]{:S(2)}) copy-start(f32[1,32,128]{2,1,0:T(8,128)} %param.14) | copy-start | bytes 49156
  30.4 9.6 %copy-start.16 = (f32[1,32,128]{2,1,0:T(8,128)S(1)}, f32[1,32,128]{2,1,0:T(8,128)}, u32[]{:S(2)}) copy-start(f32[1,32,128]{2,1,0:T(8,128)} %param.13) | copy-start | bytes 49156
  30.4 9.7 %copy-start.17 = (f32[1,32,128]{2,1,0:T(8,128)S(1)}, f32[1,32,128]{2,1,0:T(8,128)}, u32[]{:S(2)}) copy-start(f32[1,32,128]{2,1,0:T(8,128)} %param.12) | copy-start | bytes 49156
  30.4 9.7 %copy-start.18 = (f32[1,32,128]{2,1,0:T(8,128)S(1)}, f32[1,32,128]{2,1,0:T(8,128)}, u32[]{:S(2)}) copy-start(f32[1,32,128]{2,1,0:T(8,128)} %param.11) | copy-start | bytes 49156
  36.3 7.9 %copy-start.7 = (f32[128,128]{1,0:T(8,128)S(1)}, f32[128,128]{1,0:T(8,128)}, u32[]{:S(2)}) copy-start(f32[128,128]{1,0:T(8,128)} %known_part.1.own_ref) | copy-start | bytes 196612
  36.3 28.9 %all-to-all-start = ((bf16[8,16,3584]{2,1,0:T(8,128)(2,1)}), bf16[8,16,3584]{2,1,0:T(8,128)(2,1)S(1)}, u32[]{:S(2)}, u32[]{:S(2)}) async-start(bf16[8,16,3584]{2,1,0:T(8,128)(2,1)} %bitcast.31), calls=%async_computation | async-start | bytes 1835008 | tf_op jit(solution)/shard_map/all_to_all | solution.py:364
  40.0 91.7 %all-gather.4.cloned.1.call-start = ((), (), s32[]{:S(2)}) async-start(), calls=%async_computation.6 | async-start | bytes 1114112 | tf_op jit(solution)/shard_map/all_gather | solution.py:348
  41.6 9.5 %collective-permute-start.5 = (bf16[128,256]{1,0:T(8,128)(2,1)S(1)}, bf16[128,256]{1,0:T(8,128)(2,1)S(1)}, u32[]{:S(2)}, u32[]{:S(2)}) collective-permute-start(bf16[128,256]{1,0:T(8,128)(2,1)S(1)} %slice.12), channel_id=1, source_target_pairs={{512,0},{513,1},{514,2},{515,3},{516,4},{517,5},{518,6},{519,7},{5... | collective-permute-start | bytes 196616 | tf_op jit(solution)/shard_map/ppermute | solution.py:357
  42.9 8.2 %collective-permute-start.4 = (bf16[128,256]{1,0:T(8,128)(2,1)S(1)}, bf16[128,256]{1,0:T(8,128)(2,1)S(1)}, u32[]{:S(2)}, u32[]{:S(2)}) collective-permute-start(bf16[128,256]{1,0:T(8,128)(2,1)S(1)} %slice.12), channel_id=1, source_target_pairs={{512,256},{256,0},{513,257},{257,1},{514,258},{258,2},{515,259},{2... | collective-permute-start | bytes 196616 | tf_op jit(solution)/shard_map/ppermute | solution.py:356
  44.2 8.7 %collective-permute-start.3 = (f32[128,128]{1,0:T(8,128)S(1)}, f32[128,128]{1,0:T(8,128)S(1)}, u32[]{:S(2)}, u32[]{:S(2)}) collective-permute-start(f32[128,128]{1,0:T(8,128)S(1)} %copy-done.7), channel_id=1, source_target_pairs={{768,0},{769,1},{770,2},{771,3},{772,4},{773,5},{774,6},{775,7},{7... | collective-permute-start | bytes 196616 | tf_op jit(solution)/shard_map/ppermute | solution.py:327
  45.5 9.5 %collective-permute-start.2 = (f32[128,128]{1,0:T(8,128)S(1)}, f32[128,128]{1,0:T(8,128)S(1)}, u32[]{:S(2)}, u32[]{:S(2)}) collective-permute-start(f32[128,128]{1,0:T(8,128)S(1)} %copy-done.7), channel_id=1, source_target_pairs={{512,0},{768,256},{513,1},{769,257},{514,2},{770,258},{515,3},{771... | collective-permute-start | bytes 196616 | tf_op jit(solution)/shard_map/ppermute | solution.py:327
  46.8 8.2 %collective-permute-start.1 = (f32[128,128]{1,0:T(8,128)S(1)}, f32[128,128]{1,0:T(8,128)S(1)}, u32[]{:S(2)}, u32[]{:S(2)}) collective-permute-start(f32[128,128]{1,0:T(8,128)S(1)} %copy-done.7), channel_id=1, source_target_pairs={{256,0},{512,256},{768,512},{257,1},{513,257},{769,513},{258,2},{5... | collective-permute-start | bytes 196616 | tf_op jit(solution)/shard_map/ppermute | solution.py:327
  51.1 3.9 %copy-start.10 = (bf16[128,256]{1,0:T(8,128)(2,1)}, bf16[128,256]{1,0:T(8,128)(2,1)S(1)}, u32[]{:S(2)}) copy-start(bf16[128,256]{1,0:T(8,128)(2,1)S(1)} %collective-permute-done.5.w_two_ref) | copy-start | bytes 196612
  51.1 3.9 %copy-start.11 = (bf16[128,256]{1,0:T(8,128)(2,1)}, bf16[128,256]{1,0:T(8,128)(2,1)S(1)}, u32[]{:S(2)}) copy-start(bf16[128,256]{1,0:T(8,128)(2,1)S(1)} %collective-permute-done.4.w_one_ref) | copy-start | bytes 196612
  52.9 2.1 %copy-start.12 = (f32[128,128]{1,0:T(8,128)}, f32[128,128]{1,0:T(8,128)S(1)}, u32[]{:S(2)}) copy-start(f32[128,128]{1,0:T(8,128)S(1)} %collective-permute-done.3.three_ref) | copy-start | bytes 196612
  55.0 0.6 copy-start.13
  55.6 0.6 copy-start.14
  58.6 4.0 %collective-permute-start.6 = (bf16[128,512]{1,0:T(8,128)(2,1)}, bf16[128,512]{1,0:T(8,128)(2,1)S(1)}, u32[]{:S(2)}, u32[]{:S(2)}) collective-permute-start(bf16[128,512]{1,0:T(8,128)(2,1)} %get-tuple-element.23.head_a_ref), channel_id=1, source_target_pairs={{0,1},{1,0},{2,3},{3,2},{4,5},{5,4},{6,7},{7,6},{8,9},{9,8},{10,11... | collective-permute-start | bytes 393224 | tf_op jit(solution)/shard_map/ppermute | solution.py:331
  62.6 0.7 copy-start.9
  65.2 50.3 %copy-start.19 = (s32[4]{0:T(128)S(1)}, s32[4]{0:T(128)}, u32[]{:S(2)}) copy-start(s32[4]{0:T(128)} %param.15) | copy-start | bytes 52
  65.3 12.2 %copy-start.2 = (bf16[8,16,3584]{2,1,0:T(8,128)(2,1)}, bf16[8,16,3584]{2,1,0:T(8,128)(2,1)S(1)}, u32[]{:S(2)}) copy-start(bf16[8,16,3584]{2,1,0:T(8,128)(2,1)S(1)} %all-to-all-done) | copy-start | bytes 2752516
  65.3 12.2 %all-to-all-start.1 = ((bf16[8,16,512]{2,1,0:T(8,128)(2,1)}), bf16[8,16,512]{2,1,0:T(8,128)(2,1)S(1)}, u32[]{:S(2)}, u32[]{:S(2)}) async-start(bf16[8,16,512]{2,1,0:T(8,128)(2,1)} %bitcast.32), calls=%async_computation.1 | async-start | bytes 262144 | tf_op jit(solution)/shard_map/all_to_all | solution.py:372
  77.5 0.7 copy-start.6
  108.4 20.1 %all-to-all-start.3 = ((f32[16,16,256]{2,1,0:T(8,128)}), f32[16,16,256]{2,1,0:T(8,128)S(1)}, u32[]{:S(2)}, u32[]{:S(2)}) async-start(f32[16,16,256]{2,1,0:T(8,128)} %fold.1), calls=%async_computation.3 | async-start | bytes 524288 | tf_op jit(solution)/shard_map/all_to_all | solution.py:384
  128.5 0.7 copy-start.4
  131.7 23.8 %all-to-all-start.4 = ((f32[64,8,128]{2,1,0:T(8,128)}), f32[64,8,128]{2,1,0:T(8,128)S(1)}, u32[]{:S(2)}, u32[]{:S(2)}) async-start(f32[64,8,128]{2,1,0:T(8,128)} %get-tuple-element.28), calls=%async_computation.4 | async-start | bytes 524288 | tf_op jit(solution)/shard_map/all_to_all | solution.py:390
  155.5 0.7 copy-start.3
  180.1 8.6 %copy-start.1 = (bf16[4,2,16,4096]{3,2,1,0:T(8,128)(2,1)}, bf16[4,2,16,4096]{3,2,1,0:T(8,128)(2,1)S(1)}, u32[]{:S(2)}) copy-start(bf16[4,2,16,4096]{3,2,1,0:T(8,128)(2,1)S(1)} %all_to_all.42) | copy-start | bytes 3145732
  180.1 11.0 %collective-permute-start.7 = (bf16[128,4096]{1,0:T(8,128)(2,1)S(1)}, bf16[128,4096]{1,0:T(8,128)(2,1)S(1)}, u32[]{:S(2)}, u32[]{:S(2)}) collective-permute-start(bf16[128,4096]{1,0:T(8,128)(2,1)S(1)} %bitcast.26), channel_id=1, source_target_pairs={{0,1},{1,0},{2,3},{3,2},{4,5},{5,4},{6,7},{7,6},{8,9},{9,8},{10,11... | collective-permute-start | bytes 3145736 | tf_op jit(solution)/shard_map/ppermute | solution.py:331
  191.1 1.0 copy-start.5
Sparse Core Ops, SparseCore 0:
  43.5 61.4 all-gather.3

commit v4 on v3

--- a/solution.py
+++ b/solution.py
@@ -17,6 +17,7 @@
 
 bf16 = jnp.bfloat16
 f32 = jnp.float32
+VMEM_BYTES = 16 * 2**20
 DP_AXES = ("y", "z", "x", "core")
 DP_SIZES = (2, 16, 4, 2)
 
@@ -59,6 +60,7 @@
             out_specs=pl.BlockSpec((rows, slab), lambda i, s: (0, 0)),
         ),
         out_shape=jax.ShapeDtypeStruct((rows, slab), f32),
+        compiler_params=pltpu.CompilerParams(vmem_limit_bytes=56 * 2**20),
         name="known_part",
     )(section, top_grad, weight)
 
@@ -109,6 +111,7 @@
             jax.ShapeDtypeStruct((rows, span), bf16),
             jax.ShapeDtypeStruct((rows, slab), bf16),
         ],
+        compiler_params=pltpu.CompilerParams(vmem_limit_bytes=VMEM_BYTES),
         name="relay",
     )(section, top_grad, *known, *weights)
 
@@ -147,18 +150,19 @@
                 pl.BlockSpec((rows, span), lambda i, c: (0, c[0] * blocks + i + 1)),
                 pl.BlockSpec((rows, span), lambda i, c: (0, i + 1)),
             ],
-            out_specs=[pl.BlockSpec((slab, span), lambda i, c: (0, i)), turned, turned],
+            out_specs=[pl.BlockSpec((slab, span), lambda i, c: (0, i + 1)), turned, turned],
         ),
         out_shape=[
-            jax.ShapeDtypeStruct((slab, half - span), bf16),
+            jax.ShapeDtypeStruct((slab, half), bf16),
             jax.ShapeDtypeStruct((slab, rows), bf16),
             jax.ShapeDtypeStruct((slab, rows), bf16),
         ],
+        compiler_params=pltpu.CompilerParams(vmem_limit_bytes=VMEM_BYTES),
         name="tail_product",
     )(core, order, slab_a, other, top_grad, other)
 
 
-def head_kernel(core_ref, a_ref, b_ref, head_a_ref, head_b_ref, top_ref, other_ref, out_ref):
+def head_kernel(core_ref, a_ref, b_ref, head_a_ref, head_b_ref, top_ref, other_ref, tail_ref, out_ref):
     @pl.when(core_ref[0] == 0)
     def _():
         out_ref[...] = (
@@ -172,7 +176,7 @@
         ).astype(bf16)
 
 
-def head_product(core, a, b, head_a, head_b, top_grad, other):
+def head_product(core, a, b, head_a, head_b, top_grad, other, tail):
     rows, span = head_a.shape
     slab = a.shape[0]
     blocks = top_grad.shape[1] // 2 // span
@@ -183,12 +187,15 @@
         grid_spec=pltpu.PrefetchScalarGridSpec(
             num_scalar_prefetch=1,
             grid=(1,),
-            in_specs=[turned, turned, first, first, pl.BlockSpec((rows, span), lambda i, c: (0, c[0] * blocks)), first],
+            in_specs=[turned, turned, first, first, pl.BlockSpec((rows, span), lambda i, c: (0, c[0] * blocks)), first]
+            + [pl.BlockSpec(memory_space=pl.ANY)],
             out_specs=pl.BlockSpec((slab, span), lambda i, c: (0, 0)),
         ),
-        out_shape=jax.ShapeDtypeStruct((slab, span), bf16),
+        out_shape=jax.ShapeDtypeStruct(tail.shape, bf16),
+        input_output_aliases={7: 0},
+        compiler_params=pltpu.CompilerParams(vmem_limit_bytes=VMEM_BYTES),
         name="head_product",
-    )(core, a, b, head_a, head_b, top_grad, other)
+    )(core, a, b, head_a, head_b, top_grad, other, tail)
 
 
 def fold_kernel(parts_ref, out_ref, *, count):
@@ -205,34 +212,33 @@
         in_specs=[vmem_spec()],
         out_specs=vmem_spec(),
         out_shape=jax.ShapeDtypeStruct(parts.shape, f32),
+        compiler_params=pltpu.CompilerParams(vmem_limit_bytes=VMEM_BYTES),
         name="fold",
     )(parts)
 
 
-def fold_chunks_kernel(row_ref, accum_ref, head_ref, tail_ref, out_ref, *, tokens):
-    count, rows, span = head_ref.shape
+def fold_chunks_kernel(row_ref, accum_ref, parts_ref, out_ref, *, tokens):
+    count, rows, _ = parts_ref.shape
     chunks, _, width = out_ref.shape
     own = lax.broadcasted_iota(jnp.int32, (rows, width), 0) == row_ref[0]
     for j in range(chunks):
-        at = j * width
-        ref, start = (head_ref, at) if at < span else (tail_ref, at - span)
-        cols = slice(start, start + width)
-        total = jnp.where(own, accum_ref[:, at : at + width] * tokens, 0.0)
+        cols = slice(j * width, (j + 1) * width)
+        total = jnp.where(own, accum_ref[:, cols] * tokens, 0.0)
         for i in range(count):
-            total = total + ref[i, :, cols].astype(f32)
+            total = total + parts_ref[i, :, cols].astype(f32)
         out_ref[j] = total.astype(bf16)
 
 
-def fold_chunks(row, accum, head, tail, chunks, tokens):
-    rows = head.shape[1]
-    width = accum.shape[1]
+def fold_chunks(row, accum, parts, chunks, tokens):
+    _, rows, width = parts.shape
     return pl.pallas_call(
         functools.partial(fold_chunks_kernel, tokens=float(tokens)),
-        in_specs=[pl.BlockSpec(memory_space=pltpu.SMEM)] + [vmem_spec()] * 3,
+        in_specs=[pl.BlockSpec(memory_space=pltpu.SMEM)] + [vmem_spec()] * 2,
         out_specs=vmem_spec(),
         out_shape=jax.ShapeDtypeStruct((chunks, rows, width // chunks), bf16),
+        compiler_params=pltpu.CompilerParams(vmem_limit_bytes=VMEM_BYTES),
         name="fold_chunks",
-    )(row, accum, head, tail)
+    )(row, accum, parts)
 
 
 def total_kernel(count_ref, sums_ref, total_ref, square_ref, *, chunks, tokens):
@@ -256,6 +262,7 @@
             jax.ShapeDtypeStruct((rows, chunks * width), f32),
             jax.ShapeDtypeStruct((peers, 8, 128), f32),
         ],
+        compiler_params=pltpu.CompilerParams(vmem_limit_bytes=VMEM_BYTES),
         name="total_of",
     )(count, sums)
 
@@ -289,6 +296,7 @@
             jax.ShapeDtypeStruct(total_grad.shape, bf16),
             jax.ShapeDtypeStruct((8, 128), f32),
         ],
+        compiler_params=pltpu.CompilerParams(vmem_limit_bytes=VMEM_BYTES),
         name="fresh_weights",
     )(squares, total_grad, state)
 
@@ -319,6 +327,7 @@
         cost_estimate=pl.CostEstimate(
             flops=2 * slab * slab * half, bytes_accessed=4 * slab * half, transcendentals=0
         ),
+        compiler_params=pltpu.CompilerParams(vmem_limit_bytes=VMEM_BYTES),
         name="place",
     )(side, order, values, *rest)
 
@@ -344,39 +353,37 @@
     slab_own, weight = slab_inputs[0], weights[0]
     shard = master.shape[1:]
 
-    state = jnp.stack([master[0], moment1[0], moment2[0], grad_accum[0]])
+    state = jnp.concatenate([master, moment1, moment2, grad_accum] * 2)
     state = lax.all_gather(state, "z", axis=0, tiled=False)
-
-    sent = lax.dynamic_slice(top_grad, (0, (1 - core) * half), (rows, half))
-    other = swap(jnp.concatenate([sent, slab_own], axis=1), "core")
 
     known = known_part(section[None], top_grad, weight, slab, span, 4)
     known_all = [known, down(known, 1), down(known, 2), down(known, 3)]
-    w_sent = lax.optimization_barrier((weight, known))[0][:, 2 * slab : span]
+
+    late, _ = lax.optimization_barrier((top_grad, known))
+    sent = lax.dynamic_slice(late, (0, (1 - core) * half), (rows, half))
+    sent = jnp.concatenate([sent, slab_own], axis=1)
+    other = swap(sent, "core")
+    w_sent = lax.optimization_barrier((weight, other))[0]
+    w_sent = w_sent[:, 2 * slab : span]
     w_one = lax.ppermute(w_sent, "pipe", [(2, 1), (1, 0)])
     w_two = lax.ppermute(w_sent, "pipe", [(2, 0)])
 
     here = jnp.arange(slab)
     source = here // (n_x * n_z) * (n_x * n_z) + here % n_z * n_x + here // n_z % n_x
     order = (here[None, :] == source[:, None]).astype(bf16)
-    other, known = lax.optimization_barrier((other, known))
     tail, slab_a, slab_b = tail_product(core[None], order, slab_own, top_grad, other, span)
-    tail = lax.all_to_all(tail, ("y", "x"), split_axis=0, concat_axis=0, tiled=True)
 
     head, section_grad = relay(
         section[None], top_grad, known_all, [weight, w_one, w_two], slab, span
     )
     head_other = swap(head, "core")
-    ahead = head_product(core[None], slab_a, slab_b, head, head_other, top_grad, other)
-    ahead, tail = lax.optimization_barrier((ahead, tail))
-    ahead = lax.all_to_all(ahead, ("y", "x"), split_axis=0, concat_axis=0, tiled=True)
-
+    product = head_product(core[None], slab_a, slab_b, head, head_other, top_grad, other, tail)
+    parts = lax.all_to_all(product, ("y", "x"), split_axis=0, concat_axis=0, tiled=True)
     row = lax.axis_index("z").astype(jnp.int32)
     parts = fold_chunks(
         row[None],
         grad_accum[0].reshape(1, half),
-        ahead.reshape(n_y * n_x, n_z, span),
-        tail.reshape(n_y * n_x, n_z, half - span),
+        parts.reshape(n_y * n_x, n_z, half),
         n_z,
         tokens,
     )
@@ -389,7 +396,7 @@
     squares, state = lax.optimization_barrier((squares, state))
     squares = lax.all_to_all(squares, group, split_axis=0, concat_axis=0, tiled=True)
 
-    state = state.transpose(1, 0, 2, 3).reshape(4, n_z, half)
+    state = state.transpose(1, 0, 2, 3).reshape(8, n_z, half)
     fresh, factor = fresh_weights(squares, total_grad, state[:3])
     fresh = lax.all_gather(fresh, "y", axis=0, tiled=False)
     fresh = jnp.broadcast_to(fresh[None], (n_x, n_y, n_z, half))

time: 203 us -> 182 us (0.90)
  Pallas kernels: 27.6 us -> 13.7 us
  waiting for transfers between devices: 36.8 us -> 46.5 us
  blocking collectives: 48.1 us -> 41.6 us
  local copies, waits for them, and re-layouts: 12.3 us -> 7.99 us
  starting transfers between devices: 57.9 us -> 54.1 us
    all_to_all x2 -> x1, waiting for transfers between devices: 5.46 us -> 15.1 us  [local(): lax.all_to_all(product, ('y', 'x'), split_axis=0, concat_axis=0, tiled=True)]
    all_to_all x2 -> x1, starting transfers between devices: 10.4 us -> 3.69 us  [local(): lax.all_to_all(product, ('y', 'x'), split_axis=0, concat_axis=0, tiled=True)]
    all_to_all x1, blocking collectives: 26.5 us -> 20.3 us  [local(): parts = lax.all_to_all(parts, 'z', split_axis=0, concat_axis=0, tiled=True)]
    pallas_call x1, Pallas kernels: 5.88 us -> 2.32 us  [tail_product(): pl.pallas_call(tail_kernel, grid_spec=pltpu.PrefetchScalarGridSpec(num_sc...]
    ppermute x3, waiting for transfers between devices: 3.9 us -> 6.4 us  [down(): return lax.ppermute(x, 'pipe', [(i, i - by) for i in range(by, 4)])]
    unnamed x40 -> x29, local copies, waits for them, and re-layouts: 5.92 us -> 3.85 us
  transfers between devices with their start and end apart: 13 -> 12, of which waited for: 7 -> 6; matrix products, arithmetic and copies ran while one was open for 5% -> 3% of each run, Pallas kernels for 8% -> 4%
where the time goes in v4:
time: 182 us; the launch traced here: 181 us
  starting transfers between devices  54.1 us (30%)
  waiting for transfers between devices  46.5 us (26%)
  blocking collectives  41.6 us (23%)
  between operations  14.4 us (8%)
  Pallas kernels  13.7 us (8%)
  local copies, waits for them, and re-layouts  7.99 us (4%)
  other arithmetic  2.54 us (1%)
    ppermute x3, starting transfers between devices, swap(): return lax.ppermute(x, axis, [(0, 1), (1, 0)])  23.9 us
    all_to_all x1, blocking collectives, local(): parts = lax.all_to_all(parts, 'z', split_axis=0, concat_axis=0, tiled=True)  20.3 us
    all_to_all x1, blocking collectives, local(): fresh = lax.all_to_all(fresh, 'x', split_axis=0, concat_axis=0, tiled=True)  15.8 us
    all_to_all x1, waiting for transfers between devices, local(): lax.all_to_all(product, ('y', 'x'), split_axis=0, concat_axis=0, tiled=True)  15.1 us
    all_to_all x1, waiting for transfers between devices, local(): lax.all_to_all(fold(parts), 'z', split_axis=0, concat_axis=0, tiled=True)  12.4 us
    all_to_all x1, starting transfers between devices, local(): lax.all_to_all(squares, group, split_axis=0, concat_axis=0, tiled=True)  12.3 us
    all_to_all x1, waiting for transfers between devices, local(): lax.all_to_all(squares, group, split_axis=0, concat_axis=0, tiled=True)  11.2 us
    all_to_all x1, starting transfers between devices, local(): lax.all_to_all(fold(parts), 'z', split_axis=0, concat_axis=0, tiled=True)  7.71 us
  transfers between devices with their start and end apart: 12, of which 6 were waited for; matrix products, arithmetic and copies ran while one was open for 3% of the time, Pallas kernels for 4%

profile of v4, /device:TPU:1, one launch (start us, length us, event | category | flops | bytes accessed | tf_op | source)
XLA Modules:
  0.0 180.8 jit_solution(10043594424091767402)
XLA Ops:
  7.2 0.0 all-gather.4.cloned.1.call-start
  7.2 0.0 copy-start
  7.2 4.2 %known_part.1.own_ref = f32[128,128]{1,0:T(8,128)} custom-call(s32[1]{0:T(128)} %bitcast.4.section_ref, bf16[128,8192]{1,0:T(8,128)(2,1)} %top_ref.7, bf16[128,8192]{1,0:T(8,128)(2,1)} %bitcast.19), custom_call_target="tpu_custom_call" | custom-call | tf_op jit(solution)/shard_map/known_part/pallas_call | solution.py:51
  11.4 0.0 copy-done
  11.4 0.0 copy-start.8
  11.5 0.0 copy-start.9
  11.5 0.0 copy-start.4
  11.5 0.0 copy-start.3
  11.5 0.1 constant_dynamic-slice_fusion
  11.6 0.6 copy-done.5
  12.2 1.1 pad_maximum_fusion
  13.3 16.0 %collective-permute-start = (bf16[128,4224]{1,0:T(8,128)(2,1)}, bf16[128,4224]{1,0:T(8,128)(2,1)S(1)}, u32[]{:S(2)}, u32[]{:S(2)}) collective-permute-start(bf16[128,4224]{1,0:T(8,128)(2,1)} %pad_maximum_fusion), channel_id=1, source_target_pairs={{0,1},{1,0},{2,3},{3,2},{4,5},{5,4},{6,7},{7,6},{8,9},{9,8},{10,11... | collective-permute-start | bytes 3244040 | tf_op jit(solution)/shard_map/ppermute | solution.py:340
  29.4 0.0 copy-start.6
  29.4 0.6 copy-done.6
  30.1 0.0 all-gather.4.cloned.1.call-update
  30.1 0.0 copy-done.3
  30.1 1.3 collective-permute-start.1
  31.4 1.3 collective-permute-start.2
  32.7 1.3 collective-permute-start.3
  34.0 0.0 collective-permute-done.slab_b_ref.other_ref
  34.0 0.8 slice.12
  34.9 1.3 collective-permute-start.4
  36.2 1.3 collective-permute-start.5
  37.5 0.0 collective-permute-done.1.one_ref
  37.5 3.4 %collective-permute-done.2.two_ref = f32[128,128]{1,0:T(8,128)S(1)} collective-permute-done((f32[128,128]{1,0:T(8,128)S(1)}, f32[128,128]{1,0:T(8,128)S(1)}, u32[]{:S(2)}, u32[]{:S(2)}) %collective-permute-start.2) | collective-permute-done | bytes 65568 | tf_op jit(solution)/shard_map/ppermute | solution.py:336
  40.9 3.0 %collective-permute-done.3.three_ref = f32[128,128]{1,0:T(8,128)S(1)} collective-permute-done((f32[128,128]{1,0:T(8,128)S(1)}, f32[128,128]{1,0:T(8,128)S(1)}, u32[]{:S(2)}, u32[]{:S(2)}) %collective-permute-start.3) | collective-permute-done | bytes 65568 | tf_op jit(solution)/shard_map/ppermute | solution.py:336
  43.9 0.0 collective-permute-done.4.w_one_ref
  43.9 1.5 collective-permute-done.5.w_two_ref
  45.4 1.6 copy-done.1
  46.9 1.2 relay.1
  48.2 3.3 %collective-permute-start.6 = (bf16[128,512]{1,0:T(8,128)(2,1)S(1)}, bf16[128,512]{1,0:T(8,128)(2,1)S(1)}, u32[]{:S(2)}, u32[]{:S(2)}) collective-permute-start(bf16[128,512]{1,0:T(8,128)(2,1)S(1)} %get-tuple-element.21.head_a_ref), channel_id=1, source_target_pairs={{0,1},{1,0},{2,3},{3,2},{4,5},{5,4},{6,7},{7,6},{8,9},{9,8},{10,11... | collective-permute-start | bytes 393224 | tf_op jit(solution)/shard_map/ppermute | solution.py:340
  51.5 0.1 fusion.1.order_ref
  51.6 2.3 %tail_product.1 = (bf16[128,4096]{1,0:T(8,128)(2,1)S(1)}, bf16[128,128]{1,0:T(8,128)(2,1)S(1)}, bf16[128,128]{1,0:T(8,128)(2,1)S(1)}) custom-call(s32[1]{0:T(128)} %bitcast.core_ref.side_ref, bf16[128,128]{1,0:T(8,128)(2,1)S(1)} %fusion.1.order_ref, bf16[128,128]{1,0:T(8,128)(2,1)S(1)} %bitcast.27, ...), custom_call_target="tpu_custom_call" | custom-call | tf_op jit(solution)/shard_map/tail_product/pallas_call | solution.py:141
  54.0 0.0 collective-permute-done.6.head_b_ref
  54.0 0.2 head_product.1
  54.2 0.0 copy-start.2
  54.2 1.0 copy-done.2
  55.2 3.7 %all-to-all-start = ((bf16[8,16,4096]{2,1,0:T(8,128)(2,1)}), bf16[8,16,4096]{2,1,0:T(8,128)(2,1)S(1)}, u32[]{:S(2)}, u32[]{:S(2)}) async-start(bf16[8,16,4096]{2,1,0:T(8,128)(2,1)} %bitcast.24), calls=%async_computation | async-start | bytes 2097152 | tf_op jit(solution)/shard_map/all_to_all | solution.py:381
  58.9 15.1 %all-to-all-done.parts_ref = bf16[8,16,4096]{2,1,0:T(8,128)(2,1)S(1)} async-done(((bf16[8,16,4096]{2,1,0:T(8,128)(2,1)}), bf16[8,16,4096]{2,1,0:T(8,128)(2,1)S(1)}, u32[]{:S(2)}, u32[]{:S(2)}) %all-to-all-start) | async-done | bytes 1048608 | tf_op jit(solution)/shard_map/all_to_all | solution.py:381
  74.0 0.2 fold_chunks.1
  74.1 20.3 %all_to_all.29.parts_ref = bf16[16,16,256]{2,1,0:T(8,128)(2,1)S(1)} all-to-all(bf16[16,16,256]{2,1,0:T(8,128)(2,1)S(1)} %fold_chunks.1), channel_id=1, replica_groups=mesh['pipe'=4,'y'=2,'z'=16,'x'=4,'core'=2] {'z'}, dimensions={0} | all-to-all | bytes 262144 | tf_op jit(solution)/shard_map/all_to_all | solution.py:390
  94.4 0.7 fold.1
  95.2 7.7 %all-to-all-start.2 = ((f32[16,16,256]{2,1,0:T(8,128)}), f32[16,16,256]{2,1,0:T(8,128)S(1)}, u32[]{:S(2)}, u32[]{:S(2)}) async-start(f32[16,16,256]{2,1,0:T(8,128)} %fold.1), calls=%async_computation.2 | async-start | bytes 524288 | tf_op jit(solution)/shard_map/all_to_all | solution.py:391
  102.9 0.0 copy-done.10
  102.9 0.6 dynamic_slice.9.count_ref
  103.5 12.4 %all-to-all-done.2.sums_ref = f32[16,16,256]{2,1,0:T(8,128)S(1)} async-done(((f32[16,16,256]{2,1,0:T(8,128)}), f32[16,16,256]{2,1,0:T(8,128)S(1)}, u32[]{:S(2)}, u32[]{:S(2)}) %all-to-all-start.2) | async-done | bytes 262176 | tf_op jit(solution)/shard_map/all_to_all | solution.py:391
  115.8 1.5 total_of.1
  117.3 12.3 %all-to-all-start.3 = ((f32[64,8,128]{2,1,0:T(8,128)}), f32[64,8,128]{2,1,0:T(8,128)S(1)}, u32[]{:S(2)}, u32[]{:S(2)}) async-start(f32[64,8,128]{2,1,0:T(8,128)} %get-tuple-element.24), calls=%async_computation.3 | async-start | bytes 524288 | tf_op jit(solution)/shard_map/all_to_all | solution.py:397
  129.6 1.8 copy.17
  131.4 0.1 slice.16
  131.5 0.1 slice.14.state_ref
  131.6 11.2 %all-to-all-done.3.squares_ref = f32[64,8,128]{2,1,0:T(8,128)S(1)} async-done(((f32[64,8,128]{2,1,0:T(8,128)}), f32[64,8,128]{2,1,0:T(8,128)S(1)}, u32[]{:S(2)}, u32[]{:S(2)}) %all-to-all-start.3) | async-done | bytes 262176 | tf_op jit(solution)/shard_map/all_to_all | solution.py:397
  142.8 0.3 fresh_weights.1
  143.1 5.5 %all-gather.1 = bf16[32,4096]{1,0:T(8,128)(2,1)S(1)} all-gather(bf16[16,4096]{1,0:T(8,128)(2,1)S(1)} %get-tuple-element.27), channel_id=3, replica_groups=mesh['pipe'=4,'y'=2,'z'=16,'x'=4,'core'=2] {'y'}, dimensions={0}, use_global_device_ids=true | all-gather | bytes 393216 | tf_op jit(solution)/shard_map/all_gather | solution.py:401
  148.6 0.1 broadcast_in_dim.15
  148.7 15.8 %all_to_all.30 = bf16[4,2,16,4096]{3,2,1,0:T(8,128)(2,1)S(1)} all-to-all(bf16[4,2,16,4096]{3,2,1,0:T(8,128)(2,1)S(1)} %broadcast_in_dim.15), channel_id=1, replica_groups=mesh['pipe'=4,'y'=2,'z'=16,'x'=4,'core'=2] {'x'}, dimensions={0} | all-to-all | bytes 2097152 | tf_op jit(solution)/shard_map/all_to_all | solution.py:403
  164.5 4.5 %collective-permute-start.7 = (bf16[128,4096]{1,0:T(8,128)(2,1)S(1)}, bf16[128,4096]{1,0:T(8,128)(2,1)S(1)}, u32[]{:S(2)}, u32[]{:S(2)}) collective-permute-start(bf16[128,4096]{1,0:T(8,128)(2,1)S(1)} %bitcast.22), channel_id=1, source_target_pairs={{0,1},{1,0},{2,3},{3,2},{4,5},{5,4},{6,7},{7,6},{8,9},{9,8},{10,11... | collective-permute-start | bytes 3145736 | tf_op jit(solution)/shard_map/ppermute | solution.py:340
  169.1 0.1 fusion.order_ref
  169.2 0.5 slice.15
  169.7 0.7 dynamic-slice_multiply_fusion
  170.4 0.6 multiply_subtract_fusion
  171.0 1.5 place.2.refs_0_
  172.5 0.0 collective-permute-done.7.half_ref
  172.5 1.5 place.3
  (19 shorter events, 0.1 us)
Async XLA Ops:
  7.2 110.2 %all-gather.4.cloned.1.call-start = ((), (), s32[]{:S(2)}) async-start(), calls=%async_computation.5 | async-start | bytes 2228224 | tf_op jit(solution)/shard_map/all_gather | solution.py:357
  7.2 4.2 %copy-start = (bf16[128,8192]{1,0:T(8,128)(2,1)S(1)}, bf16[128,8192]{1,0:T(8,128)(2,1)}, u32[]{:S(2)}) copy-start(bf16[128,8192]{1,0:T(8,128)(2,1)} %top_ref.7) | copy-start | bytes 6291460
  11.4 0.8 copy-start.5
  11.4 17.9 %copy-start.7 = (f32[1,32,128]{2,1,0:T(8,128)S(1)}, f32[1,32,128]{2,1,0:T(8,128)}, u32[]{:S(2)}) copy-start(f32[1,32,128]{2,1,0:T(8,128)} %param.11) | copy-start | bytes 49156
  11.4 17.9 %copy-start.8 = (f32[1,32,128]{2,1,0:T(8,128)S(1)}, f32[1,32,128]{2,1,0:T(8,128)}, u32[]{:S(2)}) copy-start(f32[1,32,128]{2,1,0:T(8,128)} %param.12) | copy-start | bytes 49156
  11.5 17.9 %copy-start.9 = (f32[1,32,128]{2,1,0:T(8,128)S(1)}, f32[1,32,128]{2,1,0:T(8,128)}, u32[]{:S(2)}) copy-start(f32[1,32,128]{2,1,0:T(8,128)} %param.13) | copy-start | bytes 49156
  11.5 17.9 %copy-start.4 = (f32[1,32,128]{2,1,0:T(8,128)S(1)}, f32[1,32,128]{2,1,0:T(8,128)}, u32[]{:S(2)}) copy-start(f32[1,32,128]{2,1,0:T(8,128)} %param.14) | copy-start | bytes 49156
  11.5 18.6 %copy-start.3 = (f32[128,128]{1,0:T(8,128)S(1)}, f32[128,128]{1,0:T(8,128)}, u32[]{:S(2)}) copy-start(f32[128,128]{1,0:T(8,128)} %known_part.1.own_ref) | copy-start | bytes 196612
  13.3 20.8 %collective-permute-start = (bf16[128,4224]{1,0:T(8,128)(2,1)}, bf16[128,4224]{1,0:T(8,128)(2,1)S(1)}, u32[]{:S(2)}, u32[]{:S(2)}) collective-permute-start(bf16[128,4224]{1,0:T(8,128)(2,1)} %pad_maximum_fusion), channel_id=1, source_target_pairs={{0,1},{1,0},{2,3},{3,2},{4,5},{5,4},{6,7},{7,6},{8,9},{9,8},{10,11... | collective-permute-start | bytes 3244040 | tf_op jit(solution)/shard_map/ppermute | solution.py:340
  29.4 0.6 copy-start.6
  30.1 7.4 %collective-permute-start.1 = (f32[128,128]{1,0:T(8,128)S(1)}, f32[128,128]{1,0:T(8,128)S(1)}, u32[]{:S(2)}, u32[]{:S(2)}) collective-permute-start(f32[128,128]{1,0:T(8,128)S(1)} %copy-done.3), channel_id=1, source_target_pairs={{256,0},{512,256},{768,512},{257,1},{513,257},{769,513},{258,2},{5... | collective-permute-start | bytes 196616 | tf_op jit(solution)/shard_map/ppermute | solution.py:336
  31.4 9.5 %collective-permute-start.2 = (f32[128,128]{1,0:T(8,128)S(1)}, f32[128,128]{1,0:T(8,128)S(1)}, u32[]{:S(2)}, u32[]{:S(2)}) collective-permute-start(f32[128,128]{1,0:T(8,128)S(1)} %copy-done.3), channel_id=1, source_target_pairs={{512,0},{768,256},{513,1},{769,257},{514,2},{770,258},{515,3},{771... | collective-permute-start | bytes 196616 | tf_op jit(solution)/shard_map/ppermute | solution.py:336
  32.7 11.2 %collective-permute-start.3 = (f32[128,128]{1,0:T(8,128)S(1)}, f32[128,128]{1,0:T(8,128)S(1)}, u32[]{:S(2)}, u32[]{:S(2)}) collective-permute-start(f32[128,128]{1,0:T(8,128)S(1)} %copy-done.3), channel_id=1, source_target_pairs={{768,0},{769,1},{770,2},{771,3},{772,4},{773,5},{774,6},{775,7},{7... | collective-permute-start | bytes 196616 | tf_op jit(solution)/shard_map/ppermute | solution.py:336
  34.9 9.0 %collective-permute-start.4 = (bf16[128,256]{1,0:T(8,128)(2,1)S(1)}, bf16[128,256]{1,0:T(8,128)(2,1)S(1)}, u32[]{:S(2)}, u32[]{:S(2)}) collective-permute-start(bf16[128,256]{1,0:T(8,128)(2,1)S(1)} %slice.12), channel_id=1, source_target_pairs={{512,256},{256,0},{513,257},{257,1},{514,258},{258,2},{515,259},{2... | collective-permute-start | bytes 196616 | tf_op jit(solution)/shard_map/ppermute | solution.py:368
  36.2 9.2 %collective-permute-start.5 = (bf16[128,256]{1,0:T(8,128)(2,1)S(1)}, bf16[128,256]{1,0:T(8,128)(2,1)S(1)}, u32[]{:S(2)}, u32[]{:S(2)}) collective-permute-start(bf16[128,256]{1,0:T(8,128)(2,1)S(1)} %slice.12), channel_id=1, source_target_pairs={{512,0},{513,1},{514,2},{515,3},{516,4},{517,5},{518,6},{519,7},{5... | collective-permute-start | bytes 196616 | tf_op jit(solution)/shard_map/ppermute | solution.py:369
  45.4 1.6 copy-start.1
  48.2 5.8 %collective-permute-start.6 = (bf16[128,512]{1,0:T(8,128)(2,1)S(1)}, bf16[128,512]{1,0:T(8,128)(2,1)S(1)}, u32[]{:S(2)}, u32[]{:S(2)}) collective-permute-start(bf16[128,512]{1,0:T(8,128)(2,1)S(1)} %get-tuple-element.21.head_a_ref), channel_id=1, source_target_pairs={{0,1},{1,0},{2,3},{3,2},{4,5},{5,4},{6,7},{7,6},{8,9},{9,8},{10,11... | collective-permute-start | bytes 393224 | tf_op jit(solution)/shard_map/ppermute | solution.py:340
  54.2 1.0 copy-start.2
  55.2 47.7 %copy-start.10 = (s32[4]{0:T(128)S(1)}, s32[4]{0:T(128)}, u32[]{:S(2)}) copy-start(s32[4]{0:T(128)} %param.15) | copy-start | bytes 52
  55.2 18.8 %all-to-all-start = ((bf16[8,16,4096]{2,1,0:T(8,128)(2,1)}), bf16[8,16,4096]{2,1,0:T(8,128)(2,1)S(1)}, u32[]{:S(2)}, u32[]{:S(2)}) async-start(bf16[8,16,4096]{2,1,0:T(8,128)(2,1)} %bitcast.24), calls=%async_computation | async-start | bytes 2097152 | tf_op jit(solution)/shard_map/all_to_all | solution.py:381
  95.2 20.7 %all-to-all-start.2 = ((f32[16,16,256]{2,1,0:T(8,128)}), f32[16,16,256]{2,1,0:T(8,128)S(1)}, u32[]{:S(2)}, u32[]{:S(2)}) async-start(f32[16,16,256]{2,1,0:T(8,128)} %fold.1), calls=%async_computation.2 | async-start | bytes 524288 | tf_op jit(solution)/shard_map/all_to_all | solution.py:391
  117.3 25.4 %all-to-all-start.3 = ((f32[64,8,128]{2,1,0:T(8,128)}), f32[64,8,128]{2,1,0:T(8,128)S(1)}, u32[]{:S(2)}, u32[]{:S(2)}) async-start(f32[64,8,128]{2,1,0:T(8,128)} %get-tuple-element.24), calls=%async_computation.3 | async-start | bytes 524288 | tf_op jit(solution)/shard_map/all_to_all | solution.py:397
  164.5 8.0 %collective-permute-start.7 = (bf16[128,4096]{1,0:T(8,128)(2,1)S(1)}, bf16[128,4096]{1,0:T(8,128)(2,1)S(1)}, u32[]{:S(2)}, u32[]{:S(2)}) collective-permute-start(bf16[128,4096]{1,0:T(8,128)(2,1)S(1)} %bitcast.22), channel_id=1, source_target_pairs={{0,1},{1,0},{2,3},{3,2},{4,5},{5,4},{6,7},{7,6},{8,9},{9,8},{10,11... | collective-permute-start | bytes 3145736 | tf_op jit(solution)/shard_map/ppermute | solution.py:340
Sparse Core Ops, SparseCore 0:
  30.2 65.8 all-gather.3

commit v5 on v4

--- a/solution.py
+++ b/solution.py
@@ -81,7 +81,8 @@
                 if v >= 2:
                     narrow = slice((v - 2) * slab, (v - 1) * slab)
                     weight = jnp.where(offset == 1, w_one_ref[:, narrow].astype(f32), weight)
-                    weight = jnp.where(offset == 2, w_two_ref[:, narrow].astype(f32), weight)
+                if v == 3:
+                    weight = jnp.where(offset == 2, w_two_ref[...].astype(f32), weight)
                 total = total + dot(head_ref[:, block], weight.astype(bf16), ((1,), (1,)))
             branch = total.astype(bf16)
             here = slice(u * slab, (u + 1) * slab)
@@ -105,7 +106,7 @@
         in_specs=[pl.BlockSpec(memory_space=pltpu.SMEM), first]
         + [pl.BlockSpec((rows, slab), lambda i: (0, 0))] * 4
         + [pl.BlockSpec((slab, span), lambda i: (0, 0))]
-        + [pl.BlockSpec((slab, span // 2), lambda i: (0, 0))] * 2,
+        + [pl.BlockSpec((slab, span // 2), lambda i: (0, 0)), pl.BlockSpec((slab, slab), lambda i: (0, 0))],
         out_specs=[first, pl.BlockSpec((rows, slab), lambda i: (0, 0))],
         out_shape=[
             jax.ShapeDtypeStruct((rows, span), bf16),
@@ -203,7 +204,7 @@
     for i in range(1, count):
         total = total + parts_ref[i].astype(f32)
     for i in range(count):
-        out_ref[i] = total
+        out_ref[i] = total.astype(bf16)
 
 
 def fold(parts):
@@ -211,7 +212,7 @@
         functools.partial(fold_kernel, count=parts.shape[0]),
         in_specs=[vmem_spec()],
         out_specs=vmem_spec(),
-        out_shape=jax.ShapeDtypeStruct(parts.shape, f32),
+        out_shape=jax.ShapeDtypeStruct(parts.shape, bf16),
         compiler_params=pltpu.CompilerParams(vmem_limit_bytes=VMEM_BYTES),
         name="fold",
     )(parts)
@@ -246,7 +247,7 @@
     square = jnp.zeros((rows, width), f32)
     for j in range(chunks):
         cols = slice(j * width, (j + 1) * width)
-        total = sums_ref[j] * (1.0 / tokens)
+        total = sums_ref[j].astype(f32) * (1.0 / tokens)
         total_ref[:, cols] = total
         square = square + total * total
     square_ref[...] = jnp.full(square_ref.shape, jnp.sum(square) * count_ref[0].astype(f32), f32)
@@ -282,18 +283,20 @@
     lanes = factor_ref.shape[1]
     for j in range(total_ref.shape[1] // lanes):
         cols = slice(j * lanes, (j + 1) * lanes)
-        out_ref[:, cols] = adam(
+        fresh = adam(
             total_ref[:, cols], state_ref[0, :, cols], state_ref[1, :, cols], state_ref[2, :, cols], clip_factor
         )[1].astype(bf16)
-
-
-def fresh_weights(squares, total_grad, state):
+        for copy in range(out_ref.shape[0]):
+            out_ref[copy, :, cols] = fresh
+
+
+def fresh_weights(squares, total_grad, state, copies):
     return pl.pallas_call(
         fresh_kernel,
         in_specs=[vmem_spec()] * 3,
         out_specs=[vmem_spec()] * 2,
         out_shape=[
-            jax.ShapeDtypeStruct(total_grad.shape, bf16),
+            jax.ShapeDtypeStruct((copies,) + total_grad.shape, bf16),
             jax.ShapeDtypeStruct((8, 128), f32),
         ],
         compiler_params=pltpu.CompilerParams(vmem_limit_bytes=VMEM_BYTES),
@@ -356,17 +359,17 @@
     state = jnp.concatenate([master, moment1, moment2, grad_accum] * 2)
     state = lax.all_gather(state, "z", axis=0, tiled=False)
 
+    w_one = lax.ppermute(weight[:, 2 * slab : span], "pipe", [(2, 1), (1, 0)])
+    w_two = lax.ppermute(weight[:, 3 * slab : span], "pipe", [(2, 0)])
     known = known_part(section[None], top_grad, weight, slab, span, 4)
     known_all = [known, down(known, 1), down(known, 2), down(known, 3)]
-
-    late, _ = lax.optimization_barrier((top_grad, known))
+    w_head = lax.optimization_barrier((weight, known))[0][:, :span]
+
+    late, known_all, w_head, w_one, w_two = lax.optimization_barrier(
+        (top_grad, known_all, w_head, w_one, w_two)
+    )
     sent = lax.dynamic_slice(late, (0, (1 - core) * half), (rows, half))
-    sent = jnp.concatenate([sent, slab_own], axis=1)
-    other = swap(sent, "core")
-    w_sent = lax.optimization_barrier((weight, other))[0]
-    w_sent = w_sent[:, 2 * slab : span]
-    w_one = lax.ppermute(w_sent, "pipe", [(2, 1), (1, 0)])
-    w_two = lax.ppermute(w_sent, "pipe", [(2, 0)])
+    other = swap(jnp.concatenate([sent, slab_own], axis=1), "core")
 
     here = jnp.arange(slab)
     source = here // (n_x * n_z) * (n_x * n_z) + here % n_z * n_x + here // n_z % n_x
@@ -374,7 +377,7 @@
     tail, slab_a, slab_b = tail_product(core[None], order, slab_own, top_grad, other, span)
 
     head, section_grad = relay(
-        section[None], top_grad, known_all, [weight, w_one, w_two], slab, span
+        section[None], top_grad, known_all, [w_head, w_one, w_two], slab, span
     )
     head_other = swap(head, "core")
     product = head_product(core[None], slab_a, slab_b, head, head_other, top_grad, other, tail)
@@ -397,12 +400,10 @@
     squares = lax.all_to_all(squares, group, split_axis=0, concat_axis=0, tiled=True)
 
     state = state.transpose(1, 0, 2, 3).reshape(8, n_z, half)
-    fresh, factor = fresh_weights(squares, total_grad, state[:3])
-    fresh = lax.all_gather(fresh, "y", axis=0, tiled=False)
-    fresh = jnp.broadcast_to(fresh[None], (n_x, n_y, n_z, half))
-    fresh = lax.all_to_all(fresh, "x", split_axis=0, concat_axis=0, tiled=True)
+    fresh, factor = fresh_weights(squares, total_grad, state[:3], n_y * n_x)
+    fresh = lax.all_to_all(fresh, ("y", "x"), split_axis=0, concat_axis=0, tiled=True)
     fresh = fresh.reshape(slab, half)
-    source = here % n_x * (n_y * n_z) + here // n_x
+    source = here // (n_x * n_z) * (n_x * n_z) + here % n_x * n_z + here // n_x % n_z
     order = (here[None, :] == source[:, None]).astype(bf16)
     fresh_other = swap(fresh, "core")
     new_weights = place(core[None], order, fresh, 2)

time: 182 us -> 172 us (0.945)
  blocking collectives: 41.6 us -> 36.6 us
  starting transfers between devices: 54.1 us -> 51.6 us
  waiting for transfers between devices: 46.5 us -> 44.3 us
  Pallas kernels: 13.7 us -> 15.9 us
    ppermute x3, waiting for transfers between devices: 6.4 us -> 0.01 us  [down(): return lax.ppermute(x, 'pipe', [(i, i - by) for i in range(by, 4)])]
    all_gather x1 -> x0, blocking collectives: 5.52 us -> none  [local(): fresh = lax.all_gather(fresh, 'y', axis=0, tiled=False)]
    ppermute x2, waiting for transfers between devices: 1.47 us -> 6.59 us  [the longest x1 6.58 us: local(): w_two = lax.ppermute(weight[:, 3 * slab:span], 'pipe', [(2, 0)])]
    unnamed x29 -> x25, local copies, waits for them, and re-layouts: 3.85 us -> 0.7 us
  transfers between devices with their start and end apart: 12 -> 12, of which waited for: 6 -> 4; matrix products, arithmetic and copies ran while one was open for 3% -> 4% of each run, Pallas kernels for 4% -> 6%
where the time goes in v5:
time: 172 us; the launch traced here: 171 us
  starting transfers between devices  51.6 us (30%)
  waiting for transfers between devices  44.3 us (26%)
  blocking collectives  36.6 us (21%)
  Pallas kernels  15.9 us (9%)
  between operations  14.4 us (8%)
  local copies, waits for them, and re-layouts  6.42 us (4%)
    ppermute x3, starting transfers between devices, swap(): return lax.ppermute(x, axis, [(0, 1), (1, 0)])  22.7 us
    all_to_all x1, blocking collectives, local(): parts = lax.all_to_all(parts, 'z', split_axis=0, concat_axis=0, tiled=True)  19 us
    all_to_all x1, blocking collectives, local(): lax.all_to_all(fresh, ('y', 'x'), split_axis=0, concat_axis=0, tiled=True)  17.5 us
    all_to_all x1, waiting for transfers between devices, local(): lax.all_to_all(product, ('y', 'x'), split_axis=0, concat_axis=0, tiled=True)  15 us
    all_to_all x1, waiting for transfers between devices, local(): lax.all_to_all(fold(parts), 'z', split_axis=0, concat_axis=0, tiled=True)  11.5 us
    all_to_all x1, waiting for transfers between devices, local(): lax.all_to_all(squares, group, split_axis=0, concat_axis=0, tiled=True)  11.2 us
    all_to_all x1, starting transfers between devices, local(): lax.all_to_all(squares, group, split_axis=0, concat_axis=0, tiled=True)  10.6 us
    all_to_all x1, starting transfers between devices, local(): lax.all_to_all(fold(parts), 'z', split_axis=0, concat_axis=0, tiled=True)  7.91 us
  transfers between devices with their start and end apart: 12, of which 4 were waited for; matrix products, arithmetic and copies ran while one was open for 4% of the time, Pallas kernels for 6%

profile of v5, /device:TPU:1, one launch (start us, length us, event | category | flops | bytes accessed | tf_op | source)
XLA Modules:
  0.0 170.7 jit_solution(16013377299965706473)
XLA Ops:
  7.2 0.0 all-gather.3.cloned.1.call-start
  7.2 0.0 copy-start.5
  7.2 0.0 copy-start.6
  7.2 0.0 copy-start.7
  7.2 0.0 copy-start.2
  7.3 0.0 copy-start
  7.3 4.2 %known_part.1.own_ref = f32[128,128]{1,0:T(8,128)} custom-call(s32[1]{0:T(128)} %bitcast.4.section_ref, bf16[128,8192]{1,0:T(8,128)(2,1)} %top_ref.7, bf16[128,8192]{1,0:T(8,128)(2,1)} %bitcast.25), custom_call_target="tpu_custom_call" | custom-call | tf_op jit(solution)/shard_map/known_part/pallas_call | solution.py:51
  11.5 1.4 collective-permute-start
  12.9 1.3 collective-permute-start.1
  14.2 1.3 collective-permute-start.2
  15.5 0.8 slice.24
  16.4 1.3 collective-permute-start.3
  17.6 0.8 slice.25
  18.4 1.3 collective-permute-start.4
  19.7 0.0 copy-done.5
  19.7 0.0 copy-done.6
  19.7 0.0 copy-done.7
  19.8 0.0 copy-done.2
  19.8 0.0 copy-start.4
  19.8 0.6 copy-done.4
  20.5 0.0 all-gather.3.cloned.1.call-update
  20.5 0.9 slice.18.w_own_ref
  21.4 0.0 copy-start.1
  21.4 6.6 %collective-permute-done.4.w_two_ref = bf16[128,128]{1,0:T(8,128)(2,1)S(1)} collective-permute-done((bf16[128,128]{1,0:T(8,128)(2,1)S(1)}, bf16[128,128]{1,0:T(8,128)(2,1)S(1)}, u32[]{:S(2)}, u32[]{:S(2)}) %collective-permute-start.4) | collective-permute-done | bytes 32800 | tf_op jit(solution)/shard_map/ppermute | solution.py:363
  28.0 0.0 collective-permute-done.one_ref
  28.0 0.0 collective-permute-done.1.two_ref
  28.0 0.0 collective-permute-done.2.three_ref
  28.0 0.0 collective-permute-done.3.w_one_ref
  28.0 0.1 constant_dynamic-slice_fusion
  28.2 0.0 copy-done.3
  28.2 0.1 pad_maximum_fusion
  28.2 16.7 %collective-permute-start.5 = (bf16[128,4224]{1,0:T(8,128)(2,1)S(1)}, bf16[128,4224]{1,0:T(8,128)(2,1)S(1)}, u32[]{:S(2)}, u32[]{:S(2)}) collective-permute-start(bf16[128,4224]{1,0:T(8,128)(2,1)S(1)} %pad_maximum_fusion), channel_id=1, source_target_pairs={{0,1},{1,0},{2,3},{3,2},{4,5},{5,4},{6,7},{7,6},{8,9},{9,8},{10,11... | collective-permute-start | bytes 3244040 | tf_op jit(solution)/shard_map/ppermute | solution.py:343
  45.0 0.0 copy-done.1
  45.0 1.2 relay.1
  46.2 1.9 %collective-permute-start.6 = (bf16[128,512]{1,0:T(8,128)(2,1)S(1)}, bf16[128,512]{1,0:T(8,128)(2,1)S(1)}, u32[]{:S(2)}, u32[]{:S(2)}) collective-permute-start(bf16[128,512]{1,0:T(8,128)(2,1)S(1)} %get-tuple-element.35.head_a_ref), channel_id=1, source_target_pairs={{0,1},{1,0},{2,3},{3,2},{4,5},{5,4},{6,7},{7,6},{8,9},{9,8},{10,11... | collective-permute-start | bytes 393224 | tf_op jit(solution)/shard_map/ppermute | solution.py:343
  48.1 0.1 fusion.1.order_ref
  48.2 0.0 collective-permute-done.5.slab_b_ref.other_ref
  48.2 3.9 %tail_product.1 = (bf16[128,4096]{1,0:T(8,128)(2,1)}, bf16[128,128]{1,0:T(8,128)(2,1)S(1)}, bf16[128,128]{1,0:T(8,128)(2,1)S(1)}) custom-call(s32[1]{0:T(128)} %bitcast.core_ref.side_ref, bf16[128,128]{1,0:T(8,128)(2,1)S(1)} %fusion.1.order_ref, bf16[128,128]{1,0:T(8,128)(2,1)S(1)} %bitcast.22, ...), custom_call_target="tpu_custom_call" | custom-call | tf_op jit(solution)/shard_map/tail_product/pallas_call | solution.py:142
  52.1 0.0 collective-permute-done.6.head_b_ref
  52.1 0.9 head_product.1
  53.0 3.7 %all-to-all-start = ((bf16[8,16,4096]{2,1,0:T(8,128)(2,1)}), bf16[8,16,4096]{2,1,0:T(8,128)(2,1)S(1)}, u32[]{:S(2)}, u32[]{:S(2)}) async-start(bf16[8,16,4096]{2,1,0:T(8,128)(2,1)} %bitcast.6), calls=%async_computation | async-start | bytes 2097152 | tf_op jit(solution)/shard_map/all_to_all | solution.py:384
  56.7 15.0 %all-to-all-done.parts_ref = bf16[8,16,4096]{2,1,0:T(8,128)(2,1)S(1)} async-done(((bf16[8,16,4096]{2,1,0:T(8,128)(2,1)}), bf16[8,16,4096]{2,1,0:T(8,128)(2,1)S(1)}, u32[]{:S(2)}, u32[]{:S(2)}) %all-to-all-start) | async-done | bytes 1048608 | tf_op jit(solution)/shard_map/all_to_all | solution.py:384
  71.7 0.2 fold_chunks.1
  71.9 19.0 %all_to_all.29.parts_ref = bf16[16,16,256]{2,1,0:T(8,128)(2,1)S(1)} all-to-all(bf16[16,16,256]{2,1,0:T(8,128)(2,1)S(1)} %fold_chunks.1), channel_id=1, replica_groups=mesh['pipe'=4,'y'=2,'z'=16,'x'=4,'core'=2] {'z'}, dimensions={0} | all-to-all | bytes 262144 | tf_op jit(solution)/shard_map/all_to_all | solution.py:393
  90.9 0.7 fold.1
  91.6 7.9 %all-to-all-start.2 = ((bf16[16,16,256]{2,1,0:T(8,128)(2,1)}), bf16[16,16,256]{2,1,0:T(8,128)(2,1)S(1)}, u32[]{:S(2)}, u32[]{:S(2)}) async-start(bf16[16,16,256]{2,1,0:T(8,128)(2,1)} %fold.1), calls=%async_computation.2 | async-start | bytes 262144 | tf_op jit(solution)/shard_map/all_to_all | solution.py:394
  99.5 0.6 dynamic_slice.9.count_ref
  100.1 11.5 %all-to-all-done.2.sums_ref = bf16[16,16,256]{2,1,0:T(8,128)(2,1)S(1)} async-done(((bf16[16,16,256]{2,1,0:T(8,128)(2,1)}), bf16[16,16,256]{2,1,0:T(8,128)(2,1)S(1)}, u32[]{:S(2)}, u32[]{:S(2)}) %all-to-all-start.2) | async-done | bytes 131104 | tf_op jit(solution)/shard_map/all_to_all | solution.py:394
  111.6 1.5 total_of.1
  113.1 10.6 %all-to-all-start.3 = ((f32[64,8,128]{2,1,0:T(8,128)}), f32[64,8,128]{2,1,0:T(8,128)S(1)}, u32[]{:S(2)}, u32[]{:S(2)}) async-start(f32[64,8,128]{2,1,0:T(8,128)} %get-tuple-element.38), calls=%async_computation.3 | async-start | bytes 524288 | tf_op jit(solution)/shard_map/all_to_all | solution.py:400
  123.8 1.8 %copy.17 = f32[16,8,32,128]{3,2,0,1:T(8,128)S(1)} copy(f32[16,8,32,128]{3,2,1,0:T(8,128)} %bitcast.29) | data formatting | bytes 4194304 | tf_op jit(solution)/shard_map/optimization_barrier | solution.py:399
  125.6 0.1 slice.26
  125.7 0.1 slice.22.state_ref
  125.8 11.2 %all-to-all-done.3.squares_ref = f32[64,8,128]{2,1,0:T(8,128)S(1)} async-done(((f32[64,8,128]{2,1,0:T(8,128)}), f32[64,8,128]{2,1,0:T(8,128)S(1)}, u32[]{:S(2)}, u32[]{:S(2)}) %all-to-all-start.3) | async-done | bytes 262176 | tf_op jit(solution)/shard_map/all_to_all | solution.py:400
  137.0 0.4 fresh_weights.1
  137.4 17.5 %all_to_all.30 = bf16[8,16,4096]{2,1,0:T(8,128)(2,1)S(1)} all-to-all(bf16[8,16,4096]{2,1,0:T(8,128)(2,1)S(1)} %get-tuple-element.41), channel_id=1, replica_groups=mesh['pipe'=4,'y'=2,'z'=16,'x'=4,'core'=2] {'y','x'}, dimensions={0} | all-to-all | bytes 2097152 | tf_op jit(solution)/shard_map/all_to_all | solution.py:404
  154.9 4.1 %collective-permute-start.7 = (bf16[128,4096]{1,0:T(8,128)(2,1)S(1)}, bf16[128,4096]{1,0:T(8,128)(2,1)S(1)}, u32[]{:S(2)}, u32[]{:S(2)}) collective-permute-start(bf16[128,4096]{1,0:T(8,128)(2,1)S(1)} %bitcast.18), channel_id=1, source_target_pairs={{0,1},{1,0},{2,3},{3,2},{4,5},{5,4},{6,7},{7,6},{8,9},{9,8},{10,11... | collective-permute-start | bytes 3145736 | tf_op jit(solution)/shard_map/ppermute | solution.py:343
  159.0 0.1 fusion.order_ref
  159.1 0.5 slice.23
  159.6 0.7 dynamic-slice_multiply_fusion
  160.3 0.6 multiply_subtract_fusion
  160.9 1.5 place.2.refs_0_
  162.4 0.0 collective-permute-done.7.half_ref
  162.4 1.5 place.3
  (15 shorter events, 0.1 us)
Async XLA Ops:
  7.2 106.0 %all-gather.3.cloned.1.call-start = ((), (), s32[]{:S(2)}) async-start(), calls=%async_computation.5 | async-start | bytes 2228224 | tf_op jit(solution)/shard_map/all_gather | solution.py:360
  7.2 12.5 %copy-start.5 = (f32[1,32,128]{2,1,0:T(8,128)S(1)}, f32[1,32,128]{2,1,0:T(8,128)}, u32[]{:S(2)}) copy-start(f32[1,32,128]{2,1,0:T(8,128)} %param.11) | copy-start | bytes 49156
  7.2 12.5 %copy-start.6 = (f32[1,32,128]{2,1,0:T(8,128)S(1)}, f32[1,32,128]{2,1,0:T(8,128)}, u32[]{:S(2)}) copy-start(f32[1,32,128]{2,1,0:T(8,128)} %param.12) | copy-start | bytes 49156
  7.2 12.5 %copy-start.7 = (f32[1,32,128]{2,1,0:T(8,128)S(1)}, f32[1,32,128]{2,1,0:T(8,128)}, u32[]{:S(2)}) copy-start(f32[1,32,128]{2,1,0:T(8,128)} %param.13) | copy-start | bytes 49156
  7.2 12.5 %copy-start.2 = (f32[1,32,128]{2,1,0:T(8,128)S(1)}, f32[1,32,128]{2,1,0:T(8,128)}, u32[]{:S(2)}) copy-start(f32[1,32,128]{2,1,0:T(8,128)} %param.14) | copy-start | bytes 49156
  7.3 20.8 %copy-start = (bf16[128,8192]{1,0:T(8,128)(2,1)S(1)}, bf16[128,8192]{1,0:T(8,128)(2,1)}, u32[]{:S(2)}) copy-start(bf16[128,8192]{1,0:T(8,128)(2,1)} %top_ref.7) | copy-start | bytes 6291460
  11.5 16.7 %copy-start.3 = (bf16[1,128,128]{2,1,0:T(8,128)(2,1)S(1)}, bf16[1,128,128]{2,1,0:T(8,128)(2,1)}, u32[]{:S(2)}) copy-start(bf16[1,128,128]{2,1,0:T(8,128)(2,1)} %param.9) | copy-start | bytes 98308
  11.5 16.5 %collective-permute-start = (f32[128,128]{1,0:T(8,128)}, f32[128,128]{1,0:T(8,128)S(1)}, u32[]{:S(2)}, u32[]{:S(2)}) collective-permute-start(f32[128,128]{1,0:T(8,128)} %known_part.1.own_ref), channel_id=1, source_target_pairs={{256,0},{512,256},{768,512},{257,1},{513,257},{769,513},{258,2},{5... | collective-permute-start | bytes 196616 | tf_op jit(solution)/shard_map/ppermute | solution.py:339
  12.9 15.1 %collective-permute-start.1 = (f32[128,128]{1,0:T(8,128)}, f32[128,128]{1,0:T(8,128)S(1)}, u32[]{:S(2)}, u32[]{:S(2)}) collective-permute-start(f32[128,128]{1,0:T(8,128)} %known_part.1.own_ref), channel_id=1, source_target_pairs={{512,0},{768,256},{513,1},{769,257},{514,2},{770,258},{515,3},{771... | collective-permute-start | bytes 196616 | tf_op jit(solution)/shard_map/ppermute | solution.py:339
  14.2 13.8 %collective-permute-start.2 = (f32[128,128]{1,0:T(8,128)}, f32[128,128]{1,0:T(8,128)S(1)}, u32[]{:S(2)}, u32[]{:S(2)}) collective-permute-start(f32[128,128]{1,0:T(8,128)} %known_part.1.own_ref), channel_id=1, source_target_pairs={{768,0},{769,1},{770,2},{771,3},{772,4},{773,5},{774,6},{775,7},{7... | collective-permute-start | bytes 196616 | tf_op jit(solution)/shard_map/ppermute | solution.py:339
  16.4 11.7 %collective-permute-start.3 = (bf16[128,256]{1,0:T(8,128)(2,1)S(1)}, bf16[128,256]{1,0:T(8,128)(2,1)S(1)}, u32[]{:S(2)}, u32[]{:S(2)}) collective-permute-start(bf16[128,256]{1,0:T(8,128)(2,1)S(1)} %slice.24), channel_id=1, source_target_pairs={{512,256},{256,0},{513,257},{257,1},{514,258},{258,2},{515,259},{2... | collective-permute-start | bytes 196616 | tf_op jit(solution)/shard_map/ppermute | solution.py:362
  18.4 9.6 %collective-permute-start.4 = (bf16[128,128]{1,0:T(8,128)(2,1)S(1)}, bf16[128,128]{1,0:T(8,128)(2,1)S(1)}, u32[]{:S(2)}, u32[]{:S(2)}) collective-permute-start(bf16[128,128]{1,0:T(8,128)(2,1)S(1)} %slice.25), channel_id=1, source_target_pairs={{512,0},{513,1},{514,2},{515,3},{516,4},{517,5},{518,6},{519,7},{5... | collective-permute-start | bytes 98312 | tf_op jit(solution)/shard_map/ppermute | solution.py:363
  19.8 0.6 copy-start.4
  21.4 23.6 %copy-start.1 = (f32[128,128]{1,0:T(8,128)S(1)}, f32[128,128]{1,0:T(8,128)}, u32[]{:S(2)}) copy-start(f32[128,128]{1,0:T(8,128)} %known_part.1.own_ref) | copy-start | bytes 196612
  28.2 20.0 %collective-permute-start.5 = (bf16[128,4224]{1,0:T(8,128)(2,1)S(1)}, bf16[128,4224]{1,0:T(8,128)(2,1)S(1)}, u32[]{:S(2)}, u32[]{:S(2)}) collective-permute-start(bf16[128,4224]{1,0:T(8,128)(2,1)S(1)} %pad_maximum_fusion), channel_id=1, source_target_pairs={{0,1},{1,0},{2,3},{3,2},{4,5},{5,4},{6,7},{7,6},{8,9},{9,8},{10,11... | collective-permute-start | bytes 3244040 | tf_op jit(solution)/shard_map/ppermute | solution.py:343
  46.2 5.9 %collective-permute-start.6 = (bf16[128,512]{1,0:T(8,128)(2,1)S(1)}, bf16[128,512]{1,0:T(8,128)(2,1)S(1)}, u32[]{:S(2)}, u32[]{:S(2)}) collective-permute-start(bf16[128,512]{1,0:T(8,128)(2,1)S(1)} %get-tuple-element.35.head_a_ref), channel_id=1, source_target_pairs={{0,1},{1,0},{2,3},{3,2},{4,5},{5,4},{6,7},{7,6},{8,9},{9,8},{10,11... | collective-permute-start | bytes 393224 | tf_op jit(solution)/shard_map/ppermute | solution.py:343
  53.0 46.5 %copy-start.8 = (s32[4]{0:T(128)S(1)}, s32[4]{0:T(128)}, u32[]{:S(2)}) copy-start(s32[4]{0:T(128)} %param.15) | copy-start | bytes 52
  53.0 18.7 %all-to-all-start = ((bf16[8,16,4096]{2,1,0:T(8,128)(2,1)}), bf16[8,16,4096]{2,1,0:T(8,128)(2,1)S(1)}, u32[]{:S(2)}, u32[]{:S(2)}) async-start(bf16[8,16,4096]{2,1,0:T(8,128)(2,1)} %bitcast.6), calls=%async_computation | async-start | bytes 2097152 | tf_op jit(solution)/shard_map/all_to_all | solution.py:384
  91.6 20.0 %all-to-all-start.2 = ((bf16[16,16,256]{2,1,0:T(8,128)(2,1)}), bf16[16,16,256]{2,1,0:T(8,128)(2,1)S(1)}, u32[]{:S(2)}, u32[]{:S(2)}) async-start(bf16[16,16,256]{2,1,0:T(8,128)(2,1)} %fold.1), calls=%async_computation.2 | async-start | bytes 262144 | tf_op jit(solution)/shard_map/all_to_all | solution.py:394
  113.1 23.8 %all-to-all-start.3 = ((f32[64,8,128]{2,1,0:T(8,128)}), f32[64,8,128]{2,1,0:T(8,128)S(1)}, u32[]{:S(2)}, u32[]{:S(2)}) async-start(f32[64,8,128]{2,1,0:T(8,128)} %get-tuple-element.38), calls=%async_computation.3 | async-start | bytes 524288 | tf_op jit(solution)/shard_map/all_to_all | solution.py:400
  154.9 7.5 %collective-permute-start.7 = (bf16[128,4096]{1,0:T(8,128)(2,1)S(1)}, bf16[128,4096]{1,0:T(8,128)(2,1)S(1)}, u32[]{:S(2)}, u32[]{:S(2)}) collective-permute-start(bf16[128,4096]{1,0:T(8,128)(2,1)S(1)} %bitcast.18), channel_id=1, source_target_pairs={{0,1},{1,0},{2,3},{3,2},{4,5},{5,4},{6,7},{7,6},{8,9},{9,8},{10,11... | collective-permute-start | bytes 3145736 | tf_op jit(solution)/shard_map/ppermute | solution.py:343
Sparse Core Ops, SparseCore 0:
  20.6 81.8 all-gather.2

commit v6 on v5

--- a/solution.py
+++ b/solution.py
@@ -30,59 +30,101 @@
     return pl.BlockSpec(memory_space=pltpu.VMEM)
 
 
-def known_kernel(section_ref, top_ref, weight_ref, out_ref, *, slab, span):
-    step = pl.program_id(0)
-
-    @pl.when(step == 0)
+def known_kernel(place_ref, top_ref, weight_ref, slab_ref, out_ref, one_ref, two_ref, three_ref, sent_ref, tops_ref, weights_ref, sems, *, slab, span, steps):
+    rows, width = tops_ref.shape
+    block, half = width // steps, width // 2
+    section, core = place_ref[0], place_ref[1]
+
+    def copies(step):
+        cols = pl.ds(step * block, block)
+        return (
+            pltpu.make_async_copy(top_ref.at[:, cols], tops_ref.at[:, cols], sems.at[0, step]),
+            pltpu.make_async_copy(weight_ref.at[:, cols], weights_ref.at[:, cols], sems.at[1, step]),
+        )
+
+    for step in range(steps):
+        for copy in copies(step):
+            copy.start()
+    sent_ref[:, half:] = slab_ref[...]
+    for step in range(steps):
+        for copy in copies(step):
+            copy.wait()
+        start, end = step * block, (step + 1) * block
+        if step == 0:
+            column = lax.broadcasted_iota(jnp.int32, (rows, span), 1)
+            later = column >= (section + 1) * slab
+            known = jnp.where(later, 0.0, tops_ref[:, :span].astype(f32)).astype(bf16)
+            total = dot(known, weights_ref[:, :span], ((1,), (1,)))
+            one_ref[:, : 2 * slab] = weights_ref[:, 2 * slab : span]
+            two_ref[:, :slab] = weights_ref[:, 3 * slab : span]
+            start = span
+        if start < end:
+            total = total + dot(tops_ref[:, start:end], weights_ref[:, start:end], ((1,), (1,)))
+    high = total.astype(bf16)
+    low = (total - high.astype(f32)).astype(bf16)
+    out_ref[...] = total
+    for ref in (one_ref, two_ref, three_ref):
+        end = ref.shape[1]
+        ref[:, end - 2 * slab : end - slab] = high
+        ref[:, end - slab :] = low
+
+    @pl.when(core == 0)
     def _():
-        column = lax.broadcasted_iota(jnp.int32, top_ref.shape, 1)
-        later = (column >= (section_ref[0] + 1) * slab) & (column < span)
-        known = jnp.where(later, 0.0, top_ref[...].astype(f32)).astype(bf16)
-        out_ref[...] = dot(known, weight_ref[...], ((1,), (1,)))
-
-    @pl.when(step != 0)
+        sent_ref[:, :half] = tops_ref[:, half:]
+
+    @pl.when(core != 0)
     def _():
-        out_ref[...] += dot(top_ref[...], weight_ref[...], ((1,), (1,)))
-
-
-def known_part(section, top_grad, weight, slab, span, steps):
+        sent_ref[:, :half] = tops_ref[:, :half]
+
+
+def known_part(place, top_grad, weight, slab_own, span, steps):
     rows, width = top_grad.shape
-    block = width // steps
-    return pl.pallas_call(
-        functools.partial(known_kernel, slab=slab, span=span),
-        grid_spec=pltpu.PrefetchScalarGridSpec(
-            num_scalar_prefetch=1,
-            grid=(steps,),
-            in_specs=[
-                pl.BlockSpec((rows, block), lambda i, s: (0, i)),
-                pl.BlockSpec((slab, block), lambda i, s: (0, i)),
-            ],
-            out_specs=pl.BlockSpec((rows, slab), lambda i, s: (0, 0)),
-        ),
-        out_shape=jax.ShapeDtypeStruct((rows, slab), f32),
+    slab = slab_own.shape[1]
+    widths = [slab, 4 * slab, 3 * slab, 2 * slab, width // 2 + slab]
+    types = [f32, bf16, bf16, bf16, bf16]
+    return pl.pallas_call(
+        functools.partial(known_kernel, slab=slab, span=span, steps=steps),
+        in_specs=[
+            pl.BlockSpec(memory_space=pltpu.SMEM),
+            pl.BlockSpec(memory_space=pltpu.HBM),
+            pl.BlockSpec(memory_space=pltpu.HBM),
+            vmem_spec(),
+        ],
+        out_specs=[vmem_spec()] * 5,
+        out_shape=[jax.ShapeDtypeStruct((rows, w), t) for w, t in zip(widths, types)],
+        scratch_shapes=[
+            pltpu.VMEM((rows, width), bf16),
+            pltpu.VMEM((slab, width), bf16),
+            pltpu.SemaphoreType.DMA((2, steps)),
+        ],
         compiler_params=pltpu.CompilerParams(vmem_limit_bytes=56 * 2**20),
         name="known_part",
-    )(section, top_grad, weight)
-
-
-def relay_kernel(section_ref, top_ref, own_ref, one_ref, two_ref, three_ref, w_own_ref, w_one_ref, w_two_ref, head_ref, grad_ref, *, slab):
+    )(place, top_grad, weight, slab_own)
+
+
+def relay_kernel(section_ref, top_ref, own_ref, one_ref, two_ref, three_ref, w_own_ref, head_ref, grad_ref, *, slab):
     section = section_ref[0]
-    known = (own_ref, one_ref, two_ref, three_ref)
+
+    def pair(ref):
+        end = ref.shape[1]
+        return ref[:, end - 2 * slab : end - slab].astype(f32) + ref[:, end - slab :].astype(f32)
+
     for u in range(3, -1, -1):
         @pl.when(section <= u)
         def _(u=u):
             offset = u - section
-            total = known[3][...]
-            for k in (2, 1, 0):
-                total = jnp.where(offset == k, known[k][...], total)
+            total = pair(three_ref)
+            total = jnp.where(offset == 2, pair(two_ref), total)
+            total = jnp.where(offset == 1, pair(one_ref), total)
+            total = jnp.where(offset == 0, own_ref[...], total)
             for v in range(u + 1, 4):
                 block = slice(v * slab, (v + 1) * slab)
                 weight = w_own_ref[:, block].astype(f32)
                 if v >= 2:
                     narrow = slice((v - 2) * slab, (v - 1) * slab)
-                    weight = jnp.where(offset == 1, w_one_ref[:, narrow].astype(f32), weight)
+                    weight = jnp.where(offset == 1, one_ref[:, narrow].astype(f32), weight)
                 if v == 3:
-                    weight = jnp.where(offset == 2, w_two_ref[...].astype(f32), weight)
+                    weight = jnp.where(offset == 2, two_ref[:, :slab].astype(f32), weight)
                 total = total + dot(head_ref[:, block], weight.astype(bf16), ((1,), (1,)))
             branch = total.astype(bf16)
             here = slice(u * slab, (u + 1) * slab)
@@ -97,16 +139,15 @@
             head_ref[:, here] = top_ref[:, here]
 
 
-def relay(section, top_grad, known, weights, slab, span):
+def relay(section, top_grad, known, weight, slab, span):
     rows = top_grad.shape[0]
     first = pl.BlockSpec((rows, span), lambda i: (0, 0))
     return pl.pallas_call(
         functools.partial(relay_kernel, slab=slab),
         grid=(1,),
         in_specs=[pl.BlockSpec(memory_space=pltpu.SMEM), first]
-        + [pl.BlockSpec((rows, slab), lambda i: (0, 0))] * 4
-        + [pl.BlockSpec((slab, span), lambda i: (0, 0))]
-        + [pl.BlockSpec((slab, span // 2), lambda i: (0, 0)), pl.BlockSpec((slab, slab), lambda i: (0, 0))],
+        + [pl.BlockSpec(k.shape, lambda i: (0, 0)) for k in known]
+        + [pl.BlockSpec((slab, span), lambda i: (0, 0))],
         out_specs=[first, pl.BlockSpec((rows, slab), lambda i: (0, 0))],
         out_shape=[
             jax.ShapeDtypeStruct((rows, span), bf16),
@@ -114,7 +155,7 @@
         ],
         compiler_params=pltpu.CompilerParams(vmem_limit_bytes=VMEM_BYTES),
         name="relay",
-    )(section, top_grad, *known, *weights)
+    )(section, top_grad, *known, weight)
 
 
 def turn_kernel(order_ref, a_in_ref, b_in_ref, a_ref, b_ref):
@@ -359,26 +400,19 @@
     state = jnp.concatenate([master, moment1, moment2, grad_accum] * 2)
     state = lax.all_gather(state, "z", axis=0, tiled=False)
 
-    w_one = lax.ppermute(weight[:, 2 * slab : span], "pipe", [(2, 1), (1, 0)])
-    w_two = lax.ppermute(weight[:, 3 * slab : span], "pipe", [(2, 0)])
-    known = known_part(section[None], top_grad, weight, slab, span, 4)
-    known_all = [known, down(known, 1), down(known, 2), down(known, 3)]
+    known, one, two, three, sent = known_part(
+        jnp.stack([section, core]), top_grad, weight, slab_own, span, 8
+    )
+    known_all = [known, down(one, 1), down(two, 2), down(three, 3)]
+    other = swap(sent, "core")
     w_head = lax.optimization_barrier((weight, known))[0][:, :span]
-
-    late, known_all, w_head, w_one, w_two = lax.optimization_barrier(
-        (top_grad, known_all, w_head, w_one, w_two)
-    )
-    sent = lax.dynamic_slice(late, (0, (1 - core) * half), (rows, half))
-    other = swap(jnp.concatenate([sent, slab_own], axis=1), "core")
 
     here = jnp.arange(slab)
     source = here // (n_x * n_z) * (n_x * n_z) + here % n_z * n_x + here // n_z % n_x
     order = (here[None, :] == source[:, None]).astype(bf16)
     tail, slab_a, slab_b = tail_product(core[None], order, slab_own, top_grad, other, span)
 
-    head, section_grad = relay(
-        section[None], top_grad, known_all, [w_head, w_one, w_two], slab, span
-    )
+    head, section_grad = relay(section[None], top_grad, known_all, w_head, slab, span)
     head_other = swap(head, "core")
     product = head_product(core[None], slab_a, slab_b, head, head_other, top_grad, other, tail)
     parts = lax.all_to_all(product, ("y", "x"), split_axis=0, concat_axis=0, tiled=True)
@@ -396,12 +430,14 @@
     group = ("pipe", "y", "x", "core")
     count = lax.dynamic_slice(layer_counts, (section,), (1,))
     total_grad, squares = total_of(count, sums, tokens, lax.axis_size(group))
-    squares, state = lax.optimization_barrier((squares, state))
     squares = lax.all_to_all(squares, group, split_axis=0, concat_axis=0, tiled=True)
 
     state = state.transpose(1, 0, 2, 3).reshape(8, n_z, half)
     fresh, factor = fresh_weights(squares, total_grad, state[:3], n_y * n_x)
     fresh = lax.all_to_all(fresh, ("y", "x"), split_axis=0, concat_axis=0, tiled=True)
+    own = lax.dynamic_slice(total_grad, (row, 0), (1, half)).reshape(shard)
+    adam_step, new_master = adam(own, master[0], moment1[0], moment2[0], factor[0, 0])
+    fresh, adam_step, new_master = lax.optimization_barrier((fresh, adam_step, new_master))
     fresh = fresh.reshape(slab, half)
     source = here // (n_x * n_z) * (n_x * n_z) + here % n_x * n_z + here // n_x % n_z
     order = (here[None, :] == source[:, None]).astype(bf16)
@@ -409,8 +445,6 @@
     new_weights = place(core[None], order, fresh, 2)
     new_weights = place(1 - core[None], order, fresh_other, 2, new_weights)
 
-    own = lax.dynamic_slice(total_grad, (row, 0), (1, half)).reshape(shard)
-    adam_step, new_master = adam(own, master[0], moment1[0], moment2[0], factor[0, 0])
     return (new_weights[None], adam_step[None], new_master[None], section_grad[None])
 
 

time: 172 us -> 172 us (level)
  waiting for transfers between devices: 44.3 us -> 59.4 us
  blocking collectives: 36.6 us -> 25.1 us
  starting transfers between devices: 51.6 us -> 48.4 us
    all_to_all x1 -> x0, blocking collectives: 17.5 us -> none  [local(): lax.all_to_all(fresh, ('y', 'x'), split_axis=0, concat_axis=0, tiled=True)]
    all_to_all x0 -> x1, waiting for transfers between devices: none -> 13.1 us  [local(): lax.all_to_all(fresh, ('y', 'x'), split_axis=0, concat_axis=0, tiled=True)]
    ppermute x3, waiting for transfers between devices: 0.01 us -> 8.2 us  [down(): return lax.ppermute(x, 'pipe', [(i, i - by) for i in range(by, 4)])]
    ppermute x2 -> x0, waiting for transfers between devices: 6.59 us -> none  [the longest x1 6.58 us: local(): w_two = lax.ppermute(weight[:, 3 * slab:span], 'pipe', [(2, 0)])]
    all_to_all x1, blocking collectives: 19 us -> 25.1 us  [local(): parts = lax.all_to_all(parts, 'z', split_axis=0, concat_axis=0, tiled=True)]
    all_to_all x0 -> x1, starting transfers between devices: none -> 3.56 us  [local(): lax.all_to_all(fresh, ('y', 'x'), split_axis=0, concat_axis=0, tiled=True)]
    all_to_all x1, starting transfers between devices: 10.6 us -> 7.98 us  [local(): lax.all_to_all(squares, group, split_axis=0, concat_axis=0, tiled=True)]
    ppermute x2 -> x0, starting transfers between devices: 2.56 us -> none  [the longest x1 1.28 us: local(): w_one = lax.ppermute(weight[:, 2 * slab:span], 'pipe', [(2, 1), (1, 0)])]
  transfers between devices with their start and end apart: 12 -> 11, of which waited for: 4 -> 7; matrix products, arithmetic and copies ran while one was open for 4% -> 3% of each run, Pallas kernels for 6% -> 4%
where the time goes in v6:
time: 172 us; the launch traced here: 171 us
  waiting for transfers between devices  59.4 us (35%)
  starting transfers between devices  48.4 us (28%)
  blocking collectives  25.1 us (15%)
  Pallas kernels  15.4 us (9%)
  between operations  14.4 us (8%)
  local copies, waits for them, and re-layouts  6.51 us (4%)
  other arithmetic  2.07 us (1%)
    all_to_all x1, blocking collectives, local(): parts = lax.all_to_all(parts, 'z', split_axis=0, concat_axis=0, tiled=True)  25.1 us
    ppermute x3, starting transfers between devices, swap(): return lax.ppermute(x, axis, [(0, 1), (1, 0)])  21.5 us
    all_to_all x1, waiting for transfers between devices, local(): lax.all_to_all(product, ('y', 'x'), split_axis=0, concat_axis=0, tiled=True)  15 us
    all_to_all x1, waiting for transfers between devices, local(): lax.all_to_all(fresh, ('y', 'x'), split_axis=0, concat_axis=0, tiled=True)  13.1 us
    all_to_all x1, waiting for transfers between devices, local(): lax.all_to_all(fold(parts), 'z', split_axis=0, concat_axis=0, tiled=True)  11.4 us
    all_to_all x1, waiting for transfers between devices, local(): lax.all_to_all(squares, group, split_axis=0, concat_axis=0, tiled=True)  11.1 us
    ppermute x3, waiting for transfers between devices, down(): return lax.ppermute(x, 'pipe', [(i, i - by) for i in range(by, 4)])  8.2 us
    all_to_all x1, starting transfers between devices, local(): lax.all_to_all(squares, group, split_axis=0, concat_axis=0, tiled=True)  7.98 us
  transfers between devices with their start and end apart: 11, of which 7 were waited for; matrix products, arithmetic and copies ran while one was open for 3% of the time, Pallas kernels for 4%

profile of v6, /device:TPU:1, one launch (start us, length us, event | category | flops | bytes accessed | tf_op | source)
XLA Modules:
  0.0 171.2 jit_solution(6801346054023606770)
XLA Ops:
  7.2 0.0 all-gather.3.cloned.1.call-start
  7.2 0.6 pad_add_fusion.place_ref
  7.8 0.0 copy-start.6
  7.8 0.0 copy-start.7
  7.8 0.0 copy-start.8
  7.8 0.0 copy-start.2
  7.8 0.0 copy-start
  7.8 4.9 %known_part.1 = (f32[128,128]{1,0:T(8,128)}, bf16[128,512]{1,0:T(8,128)(2,1)}, bf16[128,384]{1,0:T(8,128)(2,1)}, bf16[128,256]{1,0:T(8,128)(2,1)}, bf16[128,4224]{1,0:T(8,128)(2,1)}) custom-call(s32[2]{0:T(128)} %pad_add_fusion.place_ref, bf16[128,8192]{1,0:T(8,128)(2,1)} %top_ref.7, bf16[128,8192]{1,0:T(8,128)(2,1)} %bitcast.44, bf16[128,128]{1,0:T(8,128)(2,1)} %bitcast.40), custom_call_target="tpu_custom_call" | custom-call | tf_op jit(solution)/shard_map/known_part/pallas_call | solution.py:85
  12.7 0.0 copy-start.3
  12.7 16.1 %collective-permute-start = (bf16[128,4224]{1,0:T(8,128)(2,1)}, bf16[128,4224]{1,0:T(8,128)(2,1)S(1)}, u32[]{:S(2)}, u32[]{:S(2)}) collective-permute-start(bf16[128,4224]{1,0:T(8,128)(2,1)} %get-tuple-element.22), channel_id=1, source_target_pairs={{0,1},{1,0},{2,3},{3,2},{4,5},{5,4},{6,7},{7,6},{8,9},{9,8},{10,11... | collective-permute-start | bytes 3244040 | tf_op jit(solution)/shard_map/ppermute | solution.py:384
  28.8 0.0 copy-done.6
  28.8 0.0 copy-done.7
  28.8 0.0 copy-done.8
  28.8 0.0 copy-done.2
  28.9 0.0 copy-start.5
  28.9 0.6 copy-done.5
  29.6 0.0 all-gather.3.cloned.1.call-update
  29.6 1.3 collective-permute-start.1
  30.9 1.3 collective-permute-start.3
  32.2 1.3 collective-permute-start.2
  33.5 0.9 slice.12.w_own_ref
  34.4 4.4 %collective-permute-done.3.three_ref = bf16[128,256]{1,0:T(8,128)(2,1)S(1)} collective-permute-done((bf16[128,256]{1,0:T(8,128)(2,1)}, bf16[128,256]{1,0:T(8,128)(2,1)S(1)}, u32[]{:S(2)}, u32[]{:S(2)}) %collective-permute-start.3) | collective-permute-done | bytes 65568 | tf_op jit(solution)/shard_map/ppermute | solution.py:380
  38.8 3.8 %collective-permute-done.2.two_ref = bf16[128,384]{1,0:T(8,128)(2,1)S(1)} collective-permute-done((bf16[128,384]{1,0:T(8,128)(2,1)}, bf16[128,384]{1,0:T(8,128)(2,1)S(1)}, u32[]{:S(2)}, u32[]{:S(2)}) %collective-permute-start.2) | collective-permute-done | bytes 98336 | tf_op jit(solution)/shard_map/ppermute | solution.py:380
  42.6 0.0 collective-permute-done.1.one_ref
  42.6 0.0 copy-done
  42.6 0.0 copy-start.4
  42.6 0.8 copy-done.4
  43.5 1.2 relay.1
  44.7 2.8 %collective-permute-start.4 = (bf16[128,512]{1,0:T(8,128)(2,1)S(1)}, bf16[128,512]{1,0:T(8,128)(2,1)S(1)}, u32[]{:S(2)}, u32[]{:S(2)}) collective-permute-start(bf16[128,512]{1,0:T(8,128)(2,1)S(1)} %get-tuple-element.30.head_a_ref), channel_id=1, source_target_pairs={{0,1},{1,0},{2,3},{3,2},{4,5},{5,4},{6,7},{7,6},{8,9},{9,8},{10,11... | collective-permute-start | bytes 393224 | tf_op jit(solution)/shard_map/ppermute | solution.py:384
  47.5 0.1 fusion.1.order_ref
  47.6 0.0 collective-permute-done.slab_b_ref.other_ref
  47.6 0.0 copy-done.3
  47.6 2.3 %tail_product.1 = (bf16[128,4096]{1,0:T(8,128)(2,1)S(1)}, bf16[128,128]{1,0:T(8,128)(2,1)S(1)}, bf16[128,128]{1,0:T(8,128)(2,1)S(1)}) custom-call(s32[1]{0:T(128)} %bitcast.core_ref.side_ref, bf16[128,128]{1,0:T(8,128)(2,1)S(1)} %fusion.1.order_ref, bf16[128,128]{1,0:T(8,128)(2,1)S(1)} %bitcast.41, ...), custom_call_target="tpu_custom_call" | custom-call | tf_op jit(solution)/shard_map/tail_product/pallas_call | solution.py:183
  49.9 0.0 collective-permute-done.4.head_b_ref
  50.0 0.2 head_product.1
  50.2 0.0 copy-start.1
  50.2 1.0 copy-done.1
  51.2 3.7 %all-to-all-start = ((bf16[8,16,4096]{2,1,0:T(8,128)(2,1)}), bf16[8,16,4096]{2,1,0:T(8,128)(2,1)S(1)}, u32[]{:S(2)}, u32[]{:S(2)}) async-start(bf16[8,16,4096]{2,1,0:T(8,128)(2,1)} %bitcast.38), calls=%async_computation | async-start | bytes 2097152 | tf_op jit(solution)/shard_map/all_to_all | solution.py:418
  54.9 15.0 %all-to-all-done.parts_ref = bf16[8,16,4096]{2,1,0:T(8,128)(2,1)S(1)} async-done(((bf16[8,16,4096]{2,1,0:T(8,128)(2,1)}), bf16[8,16,4096]{2,1,0:T(8,128)(2,1)S(1)}, u32[]{:S(2)}, u32[]{:S(2)}) %all-to-all-start) | async-done | bytes 1048608 | tf_op jit(solution)/shard_map/all_to_all | solution.py:418
  69.8 0.2 fold_chunks.1
  70.0 25.1 %all_to_all.29.parts_ref = bf16[16,16,256]{2,1,0:T(8,128)(2,1)S(1)} all-to-all(bf16[16,16,256]{2,1,0:T(8,128)(2,1)S(1)} %fold_chunks.1), channel_id=1, replica_groups=mesh['pipe'=4,'y'=2,'z'=16,'x'=4,'core'=2] {'z'}, dimensions={0} | all-to-all | bytes 262144 | tf_op jit(solution)/shard_map/all_to_all | solution.py:427
  95.1 0.7 fold.1
  95.8 7.7 %all-to-all-start.2 = ((bf16[16,16,256]{2,1,0:T(8,128)(2,1)}), bf16[16,16,256]{2,1,0:T(8,128)(2,1)S(1)}, u32[]{:S(2)}, u32[]{:S(2)}) async-start(bf16[16,16,256]{2,1,0:T(8,128)(2,1)} %fold.1), calls=%async_computation.2 | async-start | bytes 262144 | tf_op jit(solution)/shard_map/all_to_all | solution.py:428
  103.5 0.0 copy-done.9
  103.5 0.6 dynamic_slice.6.count_ref
  104.1 11.4 %all-to-all-done.2.sums_ref = bf16[16,16,256]{2,1,0:T(8,128)(2,1)S(1)} async-done(((bf16[16,16,256]{2,1,0:T(8,128)(2,1)}), bf16[16,16,256]{2,1,0:T(8,128)(2,1)S(1)}, u32[]{:S(2)}, u32[]{:S(2)}) %all-to-all-start.2) | async-done | bytes 131104 | tf_op jit(solution)/shard_map/all_to_all | solution.py:428
  115.5 1.5 total_of.1
  117.0 8.0 %all-to-all-start.3 = ((f32[64,8,128]{2,1,0:T(8,128)}), f32[64,8,128]{2,1,0:T(8,128)S(1)}, u32[]{:S(2)}, u32[]{:S(2)}) async-start(f32[64,8,128]{2,1,0:T(8,128)} %get-tuple-element.32), calls=%async_computation.3 | async-start | bytes 524288 | tf_op jit(solution)/shard_map/all_to_all | solution.py:433
  125.0 0.0 all-gather.3.cloned.1.call-done
  125.0 1.8 %copy.17 = f32[16,8,32,128]{3,2,0,1:T(8,128)S(1)} copy(f32[16,8,32,128]{3,2,1,0:T(8,128)} %bitcast.46) | data formatting | bytes 4194304 | tf_op jit(solution)/shard_map/all_gather | solution.py:401
  126.8 0.1 slice.16
  126.9 0.1 slice.14.state_ref
  127.0 11.1 %all-to-all-done.3.squares_ref = f32[64,8,128]{2,1,0:T(8,128)S(1)} async-done(((f32[64,8,128]{2,1,0:T(8,128)}), f32[64,8,128]{2,1,0:T(8,128)S(1)}, u32[]{:S(2)}, u32[]{:S(2)}) %all-to-all-start.3) | async-done | bytes 262176 | tf_op jit(solution)/shard_map/all_to_all | solution.py:433
  138.1 1.4 fresh_weights.1
  139.5 3.6 %all-to-all-start.4 = ((bf16[8,16,4096]{2,1,0:T(8,128)(2,1)}), bf16[8,16,4096]{2,1,0:T(8,128)(2,1)S(1)}, u32[]{:S(2)}, u32[]{:S(2)}) async-start(bf16[8,16,4096]{2,1,0:T(8,128)(2,1)} %get-tuple-element.34), calls=%async_computation.4 | async-start | bytes 2097152 | tf_op jit(solution)/shard_map/all_to_all | solution.py:437
  143.1 0.5 slice.15
  143.6 0.7 dynamic-slice_multiply_fusion
  144.3 0.6 bitcast_subtract_fusion
  144.9 13.1 %all-to-all-done.4 = bf16[8,16,4096]{2,1,0:T(8,128)(2,1)S(1)} async-done(((bf16[8,16,4096]{2,1,0:T(8,128)(2,1)}), bf16[8,16,4096]{2,1,0:T(8,128)(2,1)S(1)}, u32[]{:S(2)}, u32[]{:S(2)}) %all-to-all-start.4) | async-done | bytes 1048608 | tf_op jit(solution)/shard_map/all_to_all | solution.py:437
  158.0 2.7 %collective-permute-start.5 = (bf16[128,4096]{1,0:T(8,128)(2,1)S(1)}, bf16[128,4096]{1,0:T(8,128)(2,1)S(1)}, u32[]{:S(2)}, u32[]{:S(2)}) collective-permute-start(bf16[128,4096]{1,0:T(8,128)(2,1)S(1)} %bitcast.36), channel_id=1, source_target_pairs={{0,1},{1,0},{2,3},{3,2},{4,5},{5,4},{6,7},{7,6},{8,9},{9,8},{10,11... | collective-permute-start | bytes 3145736 | tf_op jit(solution)/shard_map/ppermute | solution.py:384
  160.7 0.1 fusion.order_ref
  160.7 1.5 place.2.refs_0_
  162.2 0.7 collective-permute-done.5.half_ref
  162.9 1.5 place.3
  (11 shorter events, 0.0 us)
Async XLA Ops:
  7.2 117.8 %all-gather.3.cloned.1.call-start = ((), (), s32[]{:S(2)}) async-start(), calls=%async_computation.5 | async-start | bytes 2228224 | tf_op jit(solution)/shard_map/all_gather | solution.py:401
  7.8 21.0 %copy-start.6 = (f32[1,32,128]{2,1,0:T(8,128)S(1)}, f32[1,32,128]{2,1,0:T(8,128)}, u32[]{:S(2)}) copy-start(f32[1,32,128]{2,1,0:T(8,128)} %param.11) | copy-start | bytes 49156
  7.8 21.0 %copy-start.7 = (f32[1,32,128]{2,1,0:T(8,128)S(1)}, f32[1,32,128]{2,1,0:T(8,128)}, u32[]{:S(2)}) copy-start(f32[1,32,128]{2,1,0:T(8,128)} %param.12) | copy-start | bytes 49156
  7.8 21.0 %copy-start.8 = (f32[1,32,128]{2,1,0:T(8,128)S(1)}, f32[1,32,128]{2,1,0:T(8,128)}, u32[]{:S(2)}) copy-start(f32[1,32,128]{2,1,0:T(8,128)} %param.13) | copy-start | bytes 49156
  7.8 21.0 %copy-start.2 = (f32[1,32,128]{2,1,0:T(8,128)S(1)}, f32[1,32,128]{2,1,0:T(8,128)}, u32[]{:S(2)}) copy-start(f32[1,32,128]{2,1,0:T(8,128)} %param.14) | copy-start | bytes 49156
  7.8 34.8 %copy-start = (bf16[128,8192]{1,0:T(8,128)(2,1)S(1)}, bf16[128,8192]{1,0:T(8,128)(2,1)}, u32[]{:S(2)}) copy-start(bf16[128,8192]{1,0:T(8,128)(2,1)} %top_ref.7) | copy-start | bytes 6291460
  12.7 34.9 %copy-start.3 = (bf16[1,128,128]{2,1,0:T(8,128)(2,1)S(1)}, bf16[1,128,128]{2,1,0:T(8,128)(2,1)}, u32[]{:S(2)}) copy-start(bf16[1,128,128]{2,1,0:T(8,128)(2,1)} %param.9) | copy-start | bytes 98308
  12.7 34.9 %collective-permute-start = (bf16[128,4224]{1,0:T(8,128)(2,1)}, bf16[128,4224]{1,0:T(8,128)(2,1)S(1)}, u32[]{:S(2)}, u32[]{:S(2)}) collective-permute-start(bf16[128,4224]{1,0:T(8,128)(2,1)} %get-tuple-element.22), channel_id=1, source_target_pairs={{0,1},{1,0},{2,3},{3,2},{4,5},{5,4},{6,7},{7,6},{8,9},{9,8},{10,11... | collective-permute-start | bytes 3244040 | tf_op jit(solution)/shard_map/ppermute | solution.py:384
  28.9 0.6 copy-start.5
  29.6 13.0 %collective-permute-start.1 = (bf16[128,512]{1,0:T(8,128)(2,1)}, bf16[128,512]{1,0:T(8,128)(2,1)S(1)}, u32[]{:S(2)}, u32[]{:S(2)}) collective-permute-start(bf16[128,512]{1,0:T(8,128)(2,1)} %get-tuple-element.26), channel_id=1, source_target_pairs={{256,0},{512,256},{768,512},{257,1},{513,257},{769,513},{258,2},{5... | collective-permute-start | bytes 393224 | tf_op jit(solution)/shard_map/ppermute | solution.py:380
  30.9 7.9 %collective-permute-start.3 = (bf16[128,256]{1,0:T(8,128)(2,1)}, bf16[128,256]{1,0:T(8,128)(2,1)S(1)}, u32[]{:S(2)}, u32[]{:S(2)}) collective-permute-start(bf16[128,256]{1,0:T(8,128)(2,1)} %get-tuple-element.28), channel_id=1, source_target_pairs={{768,0},{769,1},{770,2},{771,3},{772,4},{773,5},{774,6},{775,7},{7... | collective-permute-start | bytes 196616 | tf_op jit(solution)/shard_map/ppermute | solution.py:380
  32.2 10.4 %collective-permute-start.2 = (bf16[128,384]{1,0:T(8,128)(2,1)}, bf16[128,384]{1,0:T(8,128)(2,1)S(1)}, u32[]{:S(2)}, u32[]{:S(2)}) collective-permute-start(bf16[128,384]{1,0:T(8,128)(2,1)} %get-tuple-element.27), channel_id=1, source_target_pairs={{512,0},{768,256},{513,1},{769,257},{514,2},{770,258},{515,3},{771... | collective-permute-start | bytes 294920 | tf_op jit(solution)/shard_map/ppermute | solution.py:380
  42.6 0.8 copy-start.4
  44.7 5.2 %collective-permute-start.4 = (bf16[128,512]{1,0:T(8,128)(2,1)S(1)}, bf16[128,512]{1,0:T(8,128)(2,1)S(1)}, u32[]{:S(2)}, u32[]{:S(2)}) collective-permute-start(bf16[128,512]{1,0:T(8,128)(2,1)S(1)} %get-tuple-element.30.head_a_ref), channel_id=1, source_target_pairs={{0,1},{1,0},{2,3},{3,2},{4,5},{5,4},{6,7},{7,6},{8,9},{9,8},{10,11... | collective-permute-start | bytes 393224 | tf_op jit(solution)/shard_map/ppermute | solution.py:384
  50.2 1.0 copy-start.1
  51.2 52.3 %copy-start.9 = (s32[4]{0:T(128)S(1)}, s32[4]{0:T(128)}, u32[]{:S(2)}) copy-start(s32[4]{0:T(128)} %param.15) | copy-start | bytes 52
  51.2 18.7 %all-to-all-start = ((bf16[8,16,4096]{2,1,0:T(8,128)(2,1)}), bf16[8,16,4096]{2,1,0:T(8,128)(2,1)S(1)}, u32[]{:S(2)}, u32[]{:S(2)}) async-start(bf16[8,16,4096]{2,1,0:T(8,128)(2,1)} %bitcast.38), calls=%async_computation | async-start | bytes 2097152 | tf_op jit(solution)/shard_map/all_to_all | solution.py:418
  95.8 19.7 %all-to-all-start.2 = ((bf16[16,16,256]{2,1,0:T(8,128)(2,1)}), bf16[16,16,256]{2,1,0:T(8,128)(2,1)S(1)}, u32[]{:S(2)}, u32[]{:S(2)}) async-start(bf16[16,16,256]{2,1,0:T(8,128)(2,1)} %fold.1), calls=%async_computation.2 | async-start | bytes 262144 | tf_op jit(solution)/shard_map/all_to_all | solution.py:428
  117.0 21.2 %all-to-all-start.3 = ((f32[64,8,128]{2,1,0:T(8,128)}), f32[64,8,128]{2,1,0:T(8,128)S(1)}, u32[]{:S(2)}, u32[]{:S(2)}) async-start(f32[64,8,128]{2,1,0:T(8,128)} %get-tuple-element.32), calls=%async_computation.3 | async-start | bytes 524288 | tf_op jit(solution)/shard_map/all_to_all | solution.py:433
  139.5 18.4 %all-to-all-start.4 = ((bf16[8,16,4096]{2,1,0:T(8,128)(2,1)}), bf16[8,16,4096]{2,1,0:T(8,128)(2,1)S(1)}, u32[]{:S(2)}, u32[]{:S(2)}) async-start(bf16[8,16,4096]{2,1,0:T(8,128)(2,1)} %get-tuple-element.34), calls=%async_computation.4 | async-start | bytes 2097152 | tf_op jit(solution)/shard_map/all_to_all | solution.py:437
  158.0 5.0 %collective-permute-start.5 = (bf16[128,4096]{1,0:T(8,128)(2,1)S(1)}, bf16[128,4096]{1,0:T(8,128)(2,1)S(1)}, u32[]{:S(2)}, u32[]{:S(2)}) collective-permute-start(bf16[128,4096]{1,0:T(8,128)(2,1)S(1)} %bitcast.36), channel_id=1, source_target_pairs={{0,1},{1,0},{2,3},{3,2},{4,5},{5,4},{6,7},{7,6},{8,9},{9,8},{10,11... | collective-permute-start | bytes 3145736 | tf_op jit(solution)/shard_map/ppermute | solution.py:384
Sparse Core Ops, SparseCore 0:
  29.7 65.1 all-gather.2

commit v7 on v6

--- a/solution.py
+++ b/solution.py
@@ -30,10 +30,10 @@
     return pl.BlockSpec(memory_space=pltpu.VMEM)
 
 
-def known_kernel(place_ref, top_ref, weight_ref, slab_ref, out_ref, one_ref, two_ref, three_ref, sent_ref, tops_ref, weights_ref, sems, *, slab, span, steps):
+def known_kernel(section_ref, core_ref, top_ref, weight_ref, slab_ref, out_ref, one_ref, two_ref, three_ref, sent_ref, tops_ref, weights_ref, sems, *, slab, span, steps):
     rows, width = tops_ref.shape
     block, half = width // steps, width // 2
-    section, core = place_ref[0], place_ref[1]
+    section, core = section_ref[0], core_ref[0]
 
     def copies(step):
         cols = pl.ds(step * block, block)
@@ -77,7 +77,7 @@
         sent_ref[:, :half] = tops_ref[:, :half]
 
 
-def known_part(place, top_grad, weight, slab_own, span, steps):
+def known_part(section, core, top_grad, weight, slab_own, span, steps):
     rows, width = top_grad.shape
     slab = slab_own.shape[1]
     widths = [slab, 4 * slab, 3 * slab, 2 * slab, width // 2 + slab]
@@ -85,6 +85,7 @@
     return pl.pallas_call(
         functools.partial(known_kernel, slab=slab, span=span, steps=steps),
         in_specs=[
+            pl.BlockSpec(memory_space=pltpu.SMEM),
             pl.BlockSpec(memory_space=pltpu.SMEM),
             pl.BlockSpec(memory_space=pltpu.HBM),
             pl.BlockSpec(memory_space=pltpu.HBM),
@@ -99,7 +100,7 @@
         ],
         compiler_params=pltpu.CompilerParams(vmem_limit_bytes=56 * 2**20),
         name="known_part",
-    )(place, top_grad, weight, slab_own)
+    )(section, core, top_grad, weight, slab_own)
 
 
 def relay_kernel(section_ref, top_ref, own_ref, one_ref, two_ref, three_ref, w_own_ref, head_ref, grad_ref, *, slab):
@@ -302,7 +303,7 @@
         out_specs=[vmem_spec()] * 2,
         out_shape=[
             jax.ShapeDtypeStruct((rows, chunks * width), f32),
-            jax.ShapeDtypeStruct((peers, 8, 128), f32),
+            jax.ShapeDtypeStruct((peers, 1, 128), f32),
         ],
         compiler_params=pltpu.CompilerParams(vmem_limit_bytes=VMEM_BYTES),
         name="total_of",
@@ -318,7 +319,7 @@
 
 
 def fresh_kernel(squares_ref, total_ref, state_ref, out_ref, factor_ref):
-    square_norm = jnp.sum(squares_ref[...], axis=0)[:1]
+    square_norm = jnp.sum(squares_ref[...], axis=0)
     clip_factor = jnp.minimum(1.0, clip_norm / jnp.sqrt(square_norm))
     factor_ref[...] = jnp.broadcast_to(clip_factor, factor_ref.shape)
     lanes = factor_ref.shape[1]
@@ -401,7 +402,7 @@
     state = lax.all_gather(state, "z", axis=0, tiled=False)
 
     known, one, two, three, sent = known_part(
-        jnp.stack([section, core]), top_grad, weight, slab_own, span, 8
+        section[None], core[None], top_grad, weight, slab_own, span, 4
     )
     known_all = [known, down(one, 1), down(two, 2), down(three, 3)]
     other = swap(sent, "core")

time: 172 us -> 167 us (0.971)
  waiting for transfers between devices: 59.4 us -> 55.6 us
    all_to_all x1, waiting for transfers between devices: 11.1 us -> 7.26 us  [local(): lax.all_to_all(squares, group, split_axis=0, concat_axis=0, tiled=True)]
  transfers between devices with their start and end apart: 11 -> 11, of which waited for: 7 -> 7; matrix products, arithmetic and copies ran while one was open for 3% -> 3% of each run, Pallas kernels for 4% -> 5%
where the time goes in v7:
time: 167 us
  waiting for transfers between devices  55.6 us (33%)
  starting transfers between devices  47.5 us (28%)
  blocking collectives  25.8 us (15%)
  Pallas kernels  15.2 us (9%)
  between operations  14.4 us (9%)
  local copies, waits for them, and re-layouts  6.51 us (4%)
    all_to_all x1, blocking collectives, local(): parts = lax.all_to_all(parts, 'z', split_axis=0, concat_axis=0, tiled=True)  25.8 us
    ppermute x3, starting transfers between devices, swap(): return lax.ppermute(x, axis, [(0, 1), (1, 0)])  21.5 us
    all_to_all x1, waiting for transfers between devices, local(): lax.all_to_all(product, ('y', 'x'), split_axis=0, concat_axis=0, tiled=True)  15 us
    all_to_all x1, waiting for transfers between devices, local(): lax.all_to_all(fresh, ('y', 'x'), split_axis=0, concat_axis=0, tiled=True)  13 us
    all_to_all x1, waiting for transfers between devices, local(): lax.all_to_all(fold(parts), 'z', split_axis=0, concat_axis=0, tiled=True)  11.4 us
    ppermute x3, waiting for transfers between devices, down(): return lax.ppermute(x, 'pipe', [(i, i - by) for i in range(by, 4)])  8.2 us
    all_to_all x1, starting transfers between devices, local(): lax.all_to_all(squares, group, split_axis=0, concat_axis=0, tiled=True)  7.85 us
    all_to_all x1, waiting for transfers between devices, local(): lax.all_to_all(squares, group, split_axis=0, concat_axis=0, tiled=True)  7.26 us
  transfers between devices with their start and end apart: 11, of which 7 were waited for; matrix products, arithmetic and copies ran while one was open for 3% of the time, Pallas kernels for 5%

profile of v7, /device:TPU:1, one launch (start us, length us, event | category | flops | bytes accessed | tf_op | source)
XLA Modules:
  0.0 166.5 jit_solution(9929016503737373098)
XLA Ops:
  7.2 0.0 all-gather.3.cloned.1.call-start
  7.2 0.0 copy-start.6
  7.2 0.0 copy-start.7
  7.2 0.0 copy-start.8
  7.2 0.0 copy-start.2
  7.3 0.0 copy-start
  7.3 4.8 %known_part.1 = (f32[128,128]{1,0:T(8,128)}, bf16[128,512]{1,0:T(8,128)(2,1)}, bf16[128,384]{1,0:T(8,128)(2,1)}, bf16[128,256]{1,0:T(8,128)(2,1)}, bf16[128,4224]{1,0:T(8,128)(2,1)}) custom-call(s32[1]{0:T(128)} %bitcast.4.section_ref, s32[1]{0:T(128)} %bitcast.core_ref.side_ref, bf16[128,8192]{1,0:T(8,128)(2,1)} %top_ref.7, bf16[128,8192]{1,0:T(8,128)(2,1)} %bitcast.44, ...), custom_call_target="tpu_custom_call" | custom-call | tf_op jit(solution)/shard_map/known_part/pallas_call | solution.py:85
  12.1 0.0 copy-start.3
  12.1 16.1 %collective-permute-start = (bf16[128,4224]{1,0:T(8,128)(2,1)}, bf16[128,4224]{1,0:T(8,128)(2,1)S(1)}, u32[]{:S(2)}, u32[]{:S(2)}) collective-permute-start(bf16[128,4224]{1,0:T(8,128)(2,1)} %get-tuple-element.22), channel_id=1, source_target_pairs={{0,1},{1,0},{2,3},{3,2},{4,5},{5,4},{6,7},{7,6},{8,9},{9,8},{10,11... | collective-permute-start | bytes 3244040 | tf_op jit(solution)/shard_map/ppermute | solution.py:385
  28.2 0.0 copy-done.6
  28.2 0.0 copy-done.7
  28.2 0.0 copy-done.8
  28.2 0.0 copy-done.2
  28.3 0.0 copy-start.5
  28.3 0.6 copy-done.5
  29.0 0.0 all-gather.3.cloned.1.call-update
  29.0 1.3 collective-permute-start.1
  30.3 1.3 collective-permute-start.3
  31.6 1.3 collective-permute-start.2
  32.9 0.9 slice.12.w_own_ref
  33.8 4.4 %collective-permute-done.3.three_ref = bf16[128,256]{1,0:T(8,128)(2,1)S(1)} collective-permute-done((bf16[128,256]{1,0:T(8,128)(2,1)}, bf16[128,256]{1,0:T(8,128)(2,1)S(1)}, u32[]{:S(2)}, u32[]{:S(2)}) %collective-permute-start.3) | collective-permute-done | bytes 65568 | tf_op jit(solution)/shard_map/ppermute | solution.py:381
  38.2 3.8 %collective-permute-done.2.two_ref = bf16[128,384]{1,0:T(8,128)(2,1)S(1)} collective-permute-done((bf16[128,384]{1,0:T(8,128)(2,1)}, bf16[128,384]{1,0:T(8,128)(2,1)S(1)}, u32[]{:S(2)}, u32[]{:S(2)}) %collective-permute-start.2) | collective-permute-done | bytes 98336 | tf_op jit(solution)/shard_map/ppermute | solution.py:381
  42.0 0.0 collective-permute-done.1.one_ref
  42.0 0.0 copy-done
  42.0 0.0 copy-start.4
  42.0 0.8 copy-done.4
  42.9 1.2 relay.1
  44.1 2.8 %collective-permute-start.4 = (bf16[128,512]{1,0:T(8,128)(2,1)S(1)}, bf16[128,512]{1,0:T(8,128)(2,1)S(1)}, u32[]{:S(2)}, u32[]{:S(2)}) collective-permute-start(bf16[128,512]{1,0:T(8,128)(2,1)S(1)} %get-tuple-element.30.head_a_ref), channel_id=1, source_target_pairs={{0,1},{1,0},{2,3},{3,2},{4,5},{5,4},{6,7},{7,6},{8,9},{9,8},{10,11... | collective-permute-start | bytes 393224 | tf_op jit(solution)/shard_map/ppermute | solution.py:385
  46.9 0.1 fusion.1.order_ref
  47.0 0.0 collective-permute-done.slab_b_ref.other_ref
  47.0 0.0 copy-done.3
  47.0 2.3 %tail_product.1 = (bf16[128,4096]{1,0:T(8,128)(2,1)S(1)}, bf16[128,128]{1,0:T(8,128)(2,1)S(1)}, bf16[128,128]{1,0:T(8,128)(2,1)S(1)}) custom-call(s32[1]{0:T(128)} %bitcast.core_ref.side_ref, bf16[128,128]{1,0:T(8,128)(2,1)S(1)} %fusion.1.order_ref, bf16[128,128]{1,0:T(8,128)(2,1)S(1)} %bitcast.41, ...), custom_call_target="tpu_custom_call" | custom-call | tf_op jit(solution)/shard_map/tail_product/pallas_call | solution.py:184
  49.3 0.0 collective-permute-done.4.head_b_ref
  49.3 0.2 head_product.1
  49.6 0.0 copy-start.1
  49.6 1.0 copy-done.1
  50.6 0.0 copy-start.9
  50.6 3.7 %all-to-all-start = ((bf16[8,16,4096]{2,1,0:T(8,128)(2,1)}), bf16[8,16,4096]{2,1,0:T(8,128)(2,1)S(1)}, u32[]{:S(2)}, u32[]{:S(2)}) async-start(bf16[8,16,4096]{2,1,0:T(8,128)(2,1)} %bitcast.38), calls=%async_computation | async-start | bytes 2097152 | tf_op jit(solution)/shard_map/all_to_all | solution.py:419
  54.3 15.0 %all-to-all-done.parts_ref = bf16[8,16,4096]{2,1,0:T(8,128)(2,1)S(1)} async-done(((bf16[8,16,4096]{2,1,0:T(8,128)(2,1)}), bf16[8,16,4096]{2,1,0:T(8,128)(2,1)S(1)}, u32[]{:S(2)}, u32[]{:S(2)}) %all-to-all-start) | async-done | bytes 1048608 | tf_op jit(solution)/shard_map/all_to_all | solution.py:419
  69.2 0.2 fold_chunks.1
  69.4 25.8 %all_to_all.29.parts_ref = bf16[16,16,256]{2,1,0:T(8,128)(2,1)S(1)} all-to-all(bf16[16,16,256]{2,1,0:T(8,128)(2,1)S(1)} %fold_chunks.1), channel_id=1, replica_groups=mesh['pipe'=4,'y'=2,'z'=16,'x'=4,'core'=2] {'z'}, dimensions={0} | all-to-all | bytes 262144 | tf_op jit(solution)/shard_map/all_to_all | solution.py:428
  95.2 0.7 fold.1
  95.9 6.9 %all-to-all-start.2 = ((bf16[16,16,256]{2,1,0:T(8,128)(2,1)}), bf16[16,16,256]{2,1,0:T(8,128)(2,1)S(1)}, u32[]{:S(2)}, u32[]{:S(2)}) async-start(bf16[16,16,256]{2,1,0:T(8,128)(2,1)} %fold.1), calls=%async_computation.2 | async-start | bytes 262144 | tf_op jit(solution)/shard_map/all_to_all | solution.py:429
  102.9 0.0 copy-done.9
  102.9 0.6 dynamic_slice.6.count_ref
  103.5 11.4 %all-to-all-done.2.sums_ref = bf16[16,16,256]{2,1,0:T(8,128)(2,1)S(1)} async-done(((bf16[16,16,256]{2,1,0:T(8,128)(2,1)}), bf16[16,16,256]{2,1,0:T(8,128)(2,1)S(1)}, u32[]{:S(2)}, u32[]{:S(2)}) %all-to-all-start.2) | async-done | bytes 131104 | tf_op jit(solution)/shard_map/all_to_all | solution.py:429
  114.9 1.4 total_of.1
  116.3 7.9 %all-to-all-start.3 = ((f32[64,1,128]{2,1,0:T(1,128)}), f32[64,1,128]{2,1,0:T(1,128)S(1)}, u32[]{:S(2)}, u32[]{:S(2)}) async-start(f32[64,1,128]{2,1,0:T(1,128)} %get-tuple-element.32), calls=%async_computation.3 | async-start | bytes 65536 | tf_op jit(solution)/shard_map/all_to_all | solution.py:434
  124.2 0.0 all-gather.3.cloned.1.call-done
  124.2 1.8 %copy.17 = f32[16,8,32,128]{3,2,0,1:T(8,128)S(1)} copy(f32[16,8,32,128]{3,2,1,0:T(8,128)} %bitcast.46) | data formatting | bytes 4194304 | tf_op jit(solution)/shard_map/all_gather | solution.py:402
  126.0 0.1 slice.16
  126.0 0.1 slice.14.state_ref
  126.2 7.3 %all-to-all-done.3.squares_ref = f32[64,1,128]{2,1,0:T(1,128)S(1)} async-done(((f32[64,1,128]{2,1,0:T(1,128)}), f32[64,1,128]{2,1,0:T(1,128)S(1)}, u32[]{:S(2)}, u32[]{:S(2)}) %all-to-all-start.3) | async-done | bytes 32800 | tf_op jit(solution)/shard_map/all_to_all | solution.py:434
  133.5 1.4 fresh_weights.1
  134.8 3.6 %all-to-all-start.4 = ((bf16[8,16,4096]{2,1,0:T(8,128)(2,1)}), bf16[8,16,4096]{2,1,0:T(8,128)(2,1)S(1)}, u32[]{:S(2)}, u32[]{:S(2)}) async-start(bf16[8,16,4096]{2,1,0:T(8,128)(2,1)} %get-tuple-element.34), calls=%async_computation.4 | async-start | bytes 2097152 | tf_op jit(solution)/shard_map/all_to_all | solution.py:438
  138.4 0.5 slice.15
  138.9 0.7 dynamic-slice_multiply_fusion
  139.6 0.6 bitcast_subtract_fusion
  140.2 13.0 %all-to-all-done.4 = bf16[8,16,4096]{2,1,0:T(8,128)(2,1)S(1)} async-done(((bf16[8,16,4096]{2,1,0:T(8,128)(2,1)}), bf16[8,16,4096]{2,1,0:T(8,128)(2,1)S(1)}, u32[]{:S(2)}, u32[]{:S(2)}) %all-to-all-start.4) | async-done | bytes 1048608 | tf_op jit(solution)/shard_map/all_to_all | solution.py:438
  153.3 2.7 %collective-permute-start.5 = (bf16[128,4096]{1,0:T(8,128)(2,1)S(1)}, bf16[128,4096]{1,0:T(8,128)(2,1)S(1)}, u32[]{:S(2)}, u32[]{:S(2)}) collective-permute-start(bf16[128,4096]{1,0:T(8,128)(2,1)S(1)} %bitcast.36), channel_id=1, source_target_pairs={{0,1},{1,0},{2,3},{3,2},{4,5},{5,4},{6,7},{7,6},{8,9},{9,8},{10,11... | collective-permute-start | bytes 3145736 | tf_op jit(solution)/shard_map/ppermute | solution.py:385
  156.0 0.1 fusion.order_ref
  156.1 1.5 place.2.refs_0_
  157.6 0.7 collective-permute-done.5.half_ref
  158.2 1.5 place.3
  (10 shorter events, 0.0 us)
Async XLA Ops:
  7.2 117.0 %all-gather.3.cloned.1.call-start = ((), (), s32[]{:S(2)}) async-start(), calls=%async_computation.5 | async-start | bytes 2228224 | tf_op jit(solution)/shard_map/all_gather | solution.py:402
  7.2 21.0 %copy-start.6 = (f32[1,32,128]{2,1,0:T(8,128)S(1)}, f32[1,32,128]{2,1,0:T(8,128)}, u32[]{:S(2)}) copy-start(f32[1,32,128]{2,1,0:T(8,128)} %param.11) | copy-start | bytes 49156
  7.2 21.0 %copy-start.7 = (f32[1,32,128]{2,1,0:T(8,128)S(1)}, f32[1,32,128]{2,1,0:T(8,128)}, u32[]{:S(2)}) copy-start(f32[1,32,128]{2,1,0:T(8,128)} %param.12) | copy-start | bytes 49156
  7.2 21.0 %copy-start.8 = (f32[1,32,128]{2,1,0:T(8,128)S(1)}, f32[1,32,128]{2,1,0:T(8,128)}, u32[]{:S(2)}) copy-start(f32[1,32,128]{2,1,0:T(8,128)} %param.13) | copy-start | bytes 49156
  7.2 21.0 %copy-start.2 = (f32[1,32,128]{2,1,0:T(8,128)S(1)}, f32[1,32,128]{2,1,0:T(8,128)}, u32[]{:S(2)}) copy-start(f32[1,32,128]{2,1,0:T(8,128)} %param.14) | copy-start | bytes 49156
  7.3 34.8 %copy-start = (bf16[128,8192]{1,0:T(8,128)(2,1)S(1)}, bf16[128,8192]{1,0:T(8,128)(2,1)}, u32[]{:S(2)}) copy-start(bf16[128,8192]{1,0:T(8,128)(2,1)} %top_ref.7) | copy-start | bytes 6291460
  12.1 34.9 %copy-start.3 = (bf16[1,128,128]{2,1,0:T(8,128)(2,1)S(1)}, bf16[1,128,128]{2,1,0:T(8,128)(2,1)}, u32[]{:S(2)}) copy-start(bf16[1,128,128]{2,1,0:T(8,128)(2,1)} %param.9) | copy-start | bytes 98308
  12.1 34.9 %collective-permute-start = (bf16[128,4224]{1,0:T(8,128)(2,1)}, bf16[128,4224]{1,0:T(8,128)(2,1)S(1)}, u32[]{:S(2)}, u32[]{:S(2)}) collective-permute-start(bf16[128,4224]{1,0:T(8,128)(2,1)} %get-tuple-element.22), channel_id=1, source_target_pairs={{0,1},{1,0},{2,3},{3,2},{4,5},{5,4},{6,7},{7,6},{8,9},{9,8},{10,11... | collective-permute-start | bytes 3244040 | tf_op jit(solution)/shard_map/ppermute | solution.py:385
  28.3 0.6 copy-start.5
  29.0 13.0 %collective-permute-start.1 = (bf16[128,512]{1,0:T(8,128)(2,1)}, bf16[128,512]{1,0:T(8,128)(2,1)S(1)}, u32[]{:S(2)}, u32[]{:S(2)}) collective-permute-start(bf16[128,512]{1,0:T(8,128)(2,1)} %get-tuple-element.26), channel_id=1, source_target_pairs={{256,0},{512,256},{768,512},{257,1},{513,257},{769,513},{258,2},{5... | collective-permute-start | bytes 393224 | tf_op jit(solution)/shard_map/ppermute | solution.py:381
  30.3 7.9 %collective-permute-start.3 = (bf16[128,256]{1,0:T(8,128)(2,1)}, bf16[128,256]{1,0:T(8,128)(2,1)S(1)}, u32[]{:S(2)}, u32[]{:S(2)}) collective-permute-start(bf16[128,256]{1,0:T(8,128)(2,1)} %get-tuple-element.28), channel_id=1, source_target_pairs={{768,0},{769,1},{770,2},{771,3},{772,4},{773,5},{774,6},{775,7},{7... | collective-permute-start | bytes 196616 | tf_op jit(solution)/shard_map/ppermute | solution.py:381
  31.6 10.4 %collective-permute-start.2 = (bf16[128,384]{1,0:T(8,128)(2,1)}, bf16[128,384]{1,0:T(8,128)(2,1)S(1)}, u32[]{:S(2)}, u32[]{:S(2)}) collective-permute-start(bf16[128,384]{1,0:T(8,128)(2,1)} %get-tuple-element.27), channel_id=1, source_target_pairs={{512,0},{768,256},{513,1},{769,257},{514,2},{770,258},{515,3},{771... | collective-permute-start | bytes 294920 | tf_op jit(solution)/shard_map/ppermute | solution.py:381
  42.0 0.8 copy-start.4
  44.1 5.2 %collective-permute-start.4 = (bf16[128,512]{1,0:T(8,128)(2,1)S(1)}, bf16[128,512]{1,0:T(8,128)(2,1)S(1)}, u32[]{:S(2)}, u32[]{:S(2)}) collective-permute-start(bf16[128,512]{1,0:T(8,128)(2,1)S(1)} %get-tuple-element.30.head_a_ref), channel_id=1, source_target_pairs={{0,1},{1,0},{2,3},{3,2},{4,5},{5,4},{6,7},{7,6},{8,9},{9,8},{10,11... | collective-permute-start | bytes 393224 | tf_op jit(solution)/shard_map/ppermute | solution.py:385
  49.6 1.0 copy-start.1
  50.6 52.3 %copy-start.9 = (s32[4]{0:T(128)S(1)}, s32[4]{0:T(128)}, u32[]{:S(2)}) copy-start(s32[4]{0:T(128)} %param.15) | copy-start | bytes 52
  50.6 18.7 %all-to-all-start = ((bf16[8,16,4096]{2,1,0:T(8,128)(2,1)}), bf16[8,16,4096]{2,1,0:T(8,128)(2,1)S(1)}, u32[]{:S(2)}, u32[]{:S(2)}) async-start(bf16[8,16,4096]{2,1,0:T(8,128)(2,1)} %bitcast.38), calls=%async_computation | async-start | bytes 2097152 | tf_op jit(solution)/shard_map/all_to_all | solution.py:419
  95.9 18.9 %all-to-all-start.2 = ((bf16[16,16,256]{2,1,0:T(8,128)(2,1)}), bf16[16,16,256]{2,1,0:T(8,128)(2,1)S(1)}, u32[]{:S(2)}, u32[]{:S(2)}) async-start(bf16[16,16,256]{2,1,0:T(8,128)(2,1)} %fold.1), calls=%async_computation.2 | async-start | bytes 262144 | tf_op jit(solution)/shard_map/all_to_all | solution.py:429
  116.3 17.2 %all-to-all-start.3 = ((f32[64,1,128]{2,1,0:T(1,128)}), f32[64,1,128]{2,1,0:T(1,128)S(1)}, u32[]{:S(2)}, u32[]{:S(2)}) async-start(f32[64,1,128]{2,1,0:T(1,128)} %get-tuple-element.32), calls=%async_computation.3 | async-start | bytes 65536 | tf_op jit(solution)/shard_map/all_to_all | solution.py:434
  134.8 18.4 %all-to-all-start.4 = ((bf16[8,16,4096]{2,1,0:T(8,128)(2,1)}), bf16[8,16,4096]{2,1,0:T(8,128)(2,1)S(1)}, u32[]{:S(2)}, u32[]{:S(2)}) async-start(bf16[8,16,4096]{2,1,0:T(8,128)(2,1)} %get-tuple-element.34), calls=%async_computation.4 | async-start | bytes 2097152 | tf_op jit(solution)/shard_map/all_to_all | solution.py:438
  153.3 5.0 %collective-permute-start.5 = (bf16[128,4096]{1,0:T(8,128)(2,1)S(1)}, bf16[128,4096]{1,0:T(8,128)(2,1)S(1)}, u32[]{:S(2)}, u32[]{:S(2)}) collective-permute-start(bf16[128,4096]{1,0:T(8,128)(2,1)S(1)} %bitcast.36), channel_id=1, source_target_pairs={{0,1},{1,0},{2,3},{3,2},{4,5},{5,4},{6,7},{7,6},{8,9},{9,8},{10,11... | collective-permute-start | bytes 3145736 | tf_op jit(solution)/shard_map/ppermute | solution.py:385
Sparse Core Ops, SparseCore 0:
  29.1 65.3 all-gather.2

commit v8 on v7

--- a/solution.py
+++ b/solution.py
@@ -30,7 +30,7 @@
     return pl.BlockSpec(memory_space=pltpu.VMEM)
 
 
-def known_kernel(section_ref, core_ref, top_ref, weight_ref, slab_ref, out_ref, one_ref, two_ref, three_ref, sent_ref, tops_ref, weights_ref, sems, *, slab, span, steps):
+def known_kernel(section_ref, core_ref, top_ref, weight_ref, slab_ref, share_a, share_b, share_c, share_d, out_ref, one_ref, two_ref, three_ref, sent_ref, state_ref, tops_ref, weights_ref, sems, *, slab, span, steps):
     rows, width = tops_ref.shape
     block, half = width // steps, width // 2
     section, core = section_ref[0], core_ref[0]
@@ -46,6 +46,8 @@
         for copy in copies(step):
             copy.start()
     sent_ref[:, half:] = slab_ref[...]
+    for i, share in enumerate((share_a, share_b, share_c, share_d) * 2):
+        state_ref[i] = share[...]
     for step in range(steps):
         for copy in copies(step):
             copy.wait()
@@ -77,7 +79,7 @@
         sent_ref[:, :half] = tops_ref[:, :half]
 
 
-def known_part(section, core, top_grad, weight, slab_own, span, steps):
+def known_part(section, core, top_grad, weight, slab_own, shares, span, steps):
     rows, width = top_grad.shape
     slab = slab_own.shape[1]
     widths = [slab, 4 * slab, 3 * slab, 2 * slab, width // 2 + slab]
@@ -89,10 +91,11 @@
             pl.BlockSpec(memory_space=pltpu.SMEM),
             pl.BlockSpec(memory_space=pltpu.HBM),
             pl.BlockSpec(memory_space=pltpu.HBM),
-            vmem_spec(),
-        ],
-        out_specs=[vmem_spec()] * 5,
-        out_shape=[jax.ShapeDtypeStruct((rows, w), t) for w, t in zip(widths, types)],
+        ]
+        + [vmem_spec()] * 5,
+        out_specs=[vmem_spec()] * 6,
+        out_shape=[jax.ShapeDtypeStruct((rows, w), t) for w, t in zip(widths, types)]
+        + [jax.ShapeDtypeStruct((8,) + shares[0].shape, f32)],
         scratch_shapes=[
             pltpu.VMEM((rows, width), bf16),
             pltpu.VMEM((slab, width), bf16),
@@ -100,7 +103,7 @@
         ],
         compiler_params=pltpu.CompilerParams(vmem_limit_bytes=56 * 2**20),
         name="known_part",
-    )(section, core, top_grad, weight, slab_own)
+    )(section, core, top_grad, weight, slab_own, *shares)
 
 
 def relay_kernel(section_ref, top_ref, own_ref, one_ref, two_ref, three_ref, w_own_ref, head_ref, grad_ref, *, slab):
@@ -284,29 +287,23 @@
     )(row, accum, parts)
 
 
-def total_kernel(count_ref, sums_ref, total_ref, square_ref, *, chunks, tokens):
-    rows, width = sums_ref.shape[1:]
+def square_kernel(count_ref, sums_ref, square_ref, *, tokens):
+    chunks, rows, width = sums_ref.shape
     square = jnp.zeros((rows, width), f32)
     for j in range(chunks):
-        cols = slice(j * width, (j + 1) * width)
         total = sums_ref[j].astype(f32) * (1.0 / tokens)
-        total_ref[:, cols] = total
         square = square + total * total
     square_ref[...] = jnp.full(square_ref.shape, jnp.sum(square) * count_ref[0].astype(f32), f32)
 
 
-def total_of(count, sums, tokens, peers):
-    chunks, rows, width = sums.shape
-    return pl.pallas_call(
-        functools.partial(total_kernel, chunks=sums.shape[0], tokens=tokens),
+def square_of(count, sums, tokens, peers):
+    return pl.pallas_call(
+        functools.partial(square_kernel, tokens=tokens),
         in_specs=[pl.BlockSpec(memory_space=pltpu.SMEM), vmem_spec()],
-        out_specs=[vmem_spec()] * 2,
-        out_shape=[
-            jax.ShapeDtypeStruct((rows, chunks * width), f32),
-            jax.ShapeDtypeStruct((peers, 1, 128), f32),
-        ],
-        compiler_params=pltpu.CompilerParams(vmem_limit_bytes=VMEM_BYTES),
-        name="total_of",
+        out_specs=vmem_spec(),
+        out_shape=jax.ShapeDtypeStruct((peers, 1, 128), f32),
+        compiler_params=pltpu.CompilerParams(vmem_limit_bytes=VMEM_BYTES),
+        name="square_of",
     )(count, sums)
 
 
@@ -318,32 +315,36 @@
     return step, master - learn_rate * step
 
 
-def fresh_kernel(squares_ref, total_ref, state_ref, out_ref, factor_ref):
+def fresh_kernel(squares_ref, sums_ref, state_ref, out_ref, factor_ref, *, tokens):
     square_norm = jnp.sum(squares_ref[...], axis=0)
     clip_factor = jnp.minimum(1.0, clip_norm / jnp.sqrt(square_norm))
     factor_ref[...] = jnp.broadcast_to(clip_factor, factor_ref.shape)
     lanes = factor_ref.shape[1]
-    for j in range(total_ref.shape[1] // lanes):
+    width = sums_ref.shape[2]
+    for j in range(out_ref.shape[2] // lanes):
         cols = slice(j * lanes, (j + 1) * lanes)
+        within = slice(j * lanes % width, j * lanes % width + lanes)
+        total = sums_ref[j * lanes // width, :, within].astype(f32) * (1.0 / tokens)
         fresh = adam(
-            total_ref[:, cols], state_ref[0, :, cols], state_ref[1, :, cols], state_ref[2, :, cols], clip_factor
+            total, state_ref[0, :, cols], state_ref[1, :, cols], state_ref[2, :, cols], clip_factor
         )[1].astype(bf16)
         for copy in range(out_ref.shape[0]):
             out_ref[copy, :, cols] = fresh
 
 
-def fresh_weights(squares, total_grad, state, copies):
-    return pl.pallas_call(
-        fresh_kernel,
+def fresh_weights(squares, sums, state, tokens, copies):
+    chunks, rows, width = sums.shape
+    return pl.pallas_call(
+        functools.partial(fresh_kernel, tokens=tokens),
         in_specs=[vmem_spec()] * 3,
         out_specs=[vmem_spec()] * 2,
         out_shape=[
-            jax.ShapeDtypeStruct((copies,) + total_grad.shape, bf16),
+            jax.ShapeDtypeStruct((copies, rows, chunks * width), bf16),
             jax.ShapeDtypeStruct((8, 128), f32),
         ],
         compiler_params=pltpu.CompilerParams(vmem_limit_bytes=VMEM_BYTES),
         name="fresh_weights",
-    )(squares, total_grad, state)
+    )(squares, sums, state)
 
 
 def place_kernel(side_ref, order_ref, half_ref, *refs):
@@ -398,12 +399,11 @@
     slab_own, weight = slab_inputs[0], weights[0]
     shard = master.shape[1:]
 
-    state = jnp.concatenate([master, moment1, moment2, grad_accum] * 2)
+    shares = [master[0], moment1[0], moment2[0], grad_accum[0]]
+    known, one, two, three, sent, state = known_part(
+        section[None], core[None], top_grad, weight, slab_own, shares, span, 4
+    )
     state = lax.all_gather(state, "z", axis=0, tiled=False)
-
-    known, one, two, three, sent = known_part(
-        section[None], core[None], top_grad, weight, slab_own, span, 4
-    )
     known_all = [known, down(one, 1), down(two, 2), down(three, 3)]
     other = swap(sent, "core")
     w_head = lax.optimization_barrier((weight, known))[0][:, :span]
@@ -430,13 +430,13 @@
 
     group = ("pipe", "y", "x", "core")
     count = lax.dynamic_slice(layer_counts, (section,), (1,))
-    total_grad, squares = total_of(count, sums, tokens, lax.axis_size(group))
+    squares = square_of(count, sums, tokens, lax.axis_size(group))
     squares = lax.all_to_all(squares, group, split_axis=0, concat_axis=0, tiled=True)
 
     state = state.transpose(1, 0, 2, 3).reshape(8, n_z, half)
-    fresh, factor = fresh_weights(squares, total_grad, state[:3], n_y * n_x)
+    fresh, factor = fresh_weights(squares, sums, state[:3], tokens, n_y * n_x)
     fresh = lax.all_to_all(fresh, ("y", "x"), split_axis=0, concat_axis=0, tiled=True)
-    own = lax.dynamic_slice(total_grad, (row, 0), (1, half)).reshape(shard)
+    own = lax.dynamic_slice(sums, (0, row, 0), (n_z, 1, half // n_z)).astype(f32).reshape(shard) / tokens
     adam_step, new_master = adam(own, master[0], moment1[0], moment2[0], factor[0, 0])
     fresh, adam_step, new_master = lax.optimization_barrier((fresh, adam_step, new_master))
     fresh = fresh.reshape(slab, half)

time: 167 us -> 167 us (level)
  blocking collectives: 25.8 us -> 22.8 us
  waiting for transfers between devices: 55.6 us -> 58.1 us
    all_to_all x1, blocking collectives: 25.8 us -> 22.8 us  [local(): parts = lax.all_to_all(parts, 'z', split_axis=0, concat_axis=0, tiled=True)]
    ppermute x3, waiting for transfers between devices: 8.2 us -> 10.7 us  [down(): return lax.ppermute(x, 'pipe', [(i, i - by) for i in range(by, 4)])]
  transfers between devices with their start and end apart: 11 -> 11, of which waited for: 7 -> 6; matrix products, arithmetic and copies ran while one was open for 3% -> 3% of each run, Pallas kernels for 5% -> 5%
where the time goes in v8:
time: 167 us; the launch traced here: 166 us
  waiting for transfers between devices  58.1 us (35%)
  starting transfers between devices  48.1 us (29%)
  blocking collectives  22.8 us (14%)
  Pallas kernels  15.3 us (9%)
  between operations  15 us (9%)
  local copies, waits for them, and re-layouts  5.87 us (4%)
    all_to_all x1, blocking collectives, local(): parts = lax.all_to_all(parts, 'z', split_axis=0, concat_axis=0, tiled=True)  22.8 us
    ppermute x3, starting transfers between devices, swap(): return lax.ppermute(x, axis, [(0, 1), (1, 0)])  21.1 us
    all_to_all x1, waiting for transfers between devices, local(): lax.all_to_all(product, ('y', 'x'), split_axis=0, concat_axis=0, tiled=True)  15.1 us
    all_to_all x1, waiting for transfers between devices, local(): lax.all_to_all(fresh, ('y', 'x'), split_axis=0, concat_axis=0, tiled=True)  13 us
    all_to_all x1, waiting for transfers between devices, local(): lax.all_to_all(fold(parts), 'z', split_axis=0, concat_axis=0, tiled=True)  11.4 us
    ppermute x3, waiting for transfers between devices, down(): return lax.ppermute(x, 'pipe', [(i, i - by) for i in range(by, 4)])  10.7 us
    all_to_all x1, starting transfers between devices, local(): lax.all_to_all(squares, group, split_axis=0, concat_axis=0, tiled=True)  8.28 us
    all_to_all x1, starting transfers between devices, local(): lax.all_to_all(fold(parts), 'z', split_axis=0, concat_axis=0, tiled=True)  7.53 us
  transfers between devices with their start and end apart: 11, of which 6 were waited for; matrix products, arithmetic and copies ran while one was open for 3% of the time, Pallas kernels for 5%

profile of v8, /device:TPU:1, one launch (start us, length us, event | category | flops | bytes accessed | tf_op | source)
XLA Modules:
  0.0 166.0 jit_solution(2793770145214408171)
XLA Ops:
  7.2 0.0 all-gather.3.cloned.1.call-start
  7.2 0.0 copy-start
  7.2 4.9 %known_part.1 = (f32[128,128]{1,0:T(8,128)}, bf16[128,512]{1,0:T(8,128)(2,1)}, bf16[128,384]{1,0:T(8,128)(2,1)}, bf16[128,256]{1,0:T(8,128)(2,1)}, bf16[128,4224]{1,0:T(8,128)(2,1)}, /*index=5*/f32[8,32,128]{2,1,0:T(8,128)}) custom-call(s32[1]{0:T(128)} %bitcast.4.section_ref, s32[1]{0:T(128)} %bitcast.core_ref.side_ref, bf16[128,8192]{1,0:T(8,128)(2,1)} %top_ref.7, ...), custom_call_target="tpu_custom_call" | custom-call | tf_op jit(solution)/shard_map/known_part/pallas_call | solution.py:87
  12.1 0.0 copy-start.2
  12.1 16.1 %collective-permute-start = (bf16[128,4224]{1,0:T(8,128)(2,1)}, bf16[128,4224]{1,0:T(8,128)(2,1)S(1)}, u32[]{:S(2)}, u32[]{:S(2)}) collective-permute-start(bf16[128,4224]{1,0:T(8,128)(2,1)} %get-tuple-element.21), channel_id=1, source_target_pairs={{0,1},{1,0},{2,3},{3,2},{4,5},{5,4},{6,7},{7,6},{8,9},{9,8},{10,11... | collective-permute-start | bytes 3244040 | tf_op jit(solution)/shard_map/ppermute | solution.py:386
  28.2 0.0 all-gather.3.cloned.1.call-update
  28.2 1.3 collective-permute-start.1
  29.5 1.3 collective-permute-start.2
  30.8 1.3 collective-permute-start.3
  32.1 0.9 slice.12.w_own_ref
  33.1 10.7 %collective-permute-done.3.three_ref = bf16[128,256]{1,0:T(8,128)(2,1)S(1)} collective-permute-done((bf16[128,256]{1,0:T(8,128)(2,1)}, bf16[128,256]{1,0:T(8,128)(2,1)S(1)}, u32[]{:S(2)}, u32[]{:S(2)}) %collective-permute-start.3) | collective-permute-done | bytes 65568 | tf_op jit(solution)/shard_map/ppermute | solution.py:382
  43.8 0.0 collective-permute-done.2.two_ref
  43.8 0.0 collective-permute-done.1.one_ref
  43.8 0.0 copy-done
  43.8 0.0 copy-start.4
  43.8 0.8 copy-done.4
  44.6 1.2 relay.1
  45.9 2.4 %collective-permute-start.4 = (bf16[128,512]{1,0:T(8,128)(2,1)S(1)}, bf16[128,512]{1,0:T(8,128)(2,1)S(1)}, u32[]{:S(2)}, u32[]{:S(2)}) collective-permute-start(bf16[128,512]{1,0:T(8,128)(2,1)S(1)} %get-tuple-element.29.head_a_ref), channel_id=1, source_target_pairs={{0,1},{1,0},{2,3},{3,2},{4,5},{5,4},{6,7},{7,6},{8,9},{9,8},{10,11... | collective-permute-start | bytes 393224 | tf_op jit(solution)/shard_map/ppermute | solution.py:386
  48.3 0.1 fusion.1.order_ref
  48.4 0.0 collective-permute-done.slab_b_ref.other_ref
  48.4 0.0 copy-done.2
  48.4 2.3 %tail_product.1 = (bf16[128,4096]{1,0:T(8,128)(2,1)S(1)}, bf16[128,128]{1,0:T(8,128)(2,1)S(1)}, bf16[128,128]{1,0:T(8,128)(2,1)S(1)}) custom-call(s32[1]{0:T(128)} %bitcast.core_ref.side_ref, bf16[128,128]{1,0:T(8,128)(2,1)S(1)} %fusion.1.order_ref, bf16[128,128]{1,0:T(8,128)(2,1)S(1)} %bitcast.35, ...), custom_call_target="tpu_custom_call" | custom-call | tf_op jit(solution)/shard_map/tail_product/pallas_call | solution.py:187
  50.7 0.0 collective-permute-done.4.head_b_ref
  50.7 0.2 head_product.1
  51.0 0.0 copy-start.1
  51.0 1.0 copy-done.1
  51.9 0.0 copy-start.3
  51.9 0.0 copy-start.8
  51.9 3.7 %all-to-all-start = ((bf16[8,16,4096]{2,1,0:T(8,128)(2,1)}), bf16[8,16,4096]{2,1,0:T(8,128)(2,1)S(1)}, u32[]{:S(2)}, u32[]{:S(2)}) async-start(bf16[8,16,4096]{2,1,0:T(8,128)(2,1)} %bitcast.33), calls=%async_computation | async-start | bytes 2097152 | tf_op jit(solution)/shard_map/all_to_all | solution.py:419
  55.7 15.1 %all-to-all-done.parts_ref = bf16[8,16,4096]{2,1,0:T(8,128)(2,1)S(1)} async-done(((bf16[8,16,4096]{2,1,0:T(8,128)(2,1)}), bf16[8,16,4096]{2,1,0:T(8,128)(2,1)S(1)}, u32[]{:S(2)}, u32[]{:S(2)}) %all-to-all-start) | async-done | bytes 1048608 | tf_op jit(solution)/shard_map/all_to_all | solution.py:419
  70.7 0.0 copy-done.3
  70.7 0.2 fold_chunks.1
  70.9 22.8 %all_to_all.29.parts_ref = bf16[16,16,256]{2,1,0:T(8,128)(2,1)S(1)} all-to-all(bf16[16,16,256]{2,1,0:T(8,128)(2,1)S(1)} %fold_chunks.1), channel_id=1, replica_groups=mesh['pipe'=4,'y'=2,'z'=16,'x'=4,'core'=2] {'z'}, dimensions={0} | all-to-all | bytes 262144 | tf_op jit(solution)/shard_map/all_to_all | solution.py:428
  93.7 0.7 fold.1
  94.4 7.5 %all-to-all-start.2 = ((bf16[16,16,256]{2,1,0:T(8,128)(2,1)}), bf16[16,16,256]{2,1,0:T(8,128)(2,1)S(1)}, u32[]{:S(2)}, u32[]{:S(2)}) async-start(bf16[16,16,256]{2,1,0:T(8,128)(2,1)} %fold.1), calls=%async_computation.2 | async-start | bytes 262144 | tf_op jit(solution)/shard_map/all_to_all | solution.py:429
  101.9 0.0 copy-done.8
  101.9 0.6 dynamic_slice.6.count_ref
  102.5 11.4 %all-to-all-done.2.sums_ref = bf16[16,16,256]{2,1,0:T(8,128)(2,1)S(1)} async-done(((bf16[16,16,256]{2,1,0:T(8,128)(2,1)}), bf16[16,16,256]{2,1,0:T(8,128)(2,1)S(1)}, u32[]{:S(2)}, u32[]{:S(2)}) %all-to-all-start.2) | async-done | bytes 131104 | tf_op jit(solution)/shard_map/all_to_all | solution.py:429
  113.9 1.4 square_of.1
  115.3 8.3 %all-to-all-start.3 = ((f32[64,1,128]{2,1,0:T(1,128)}), f32[64,1,128]{2,1,0:T(1,128)S(1)}, u32[]{:S(2)}, u32[]{:S(2)}) async-start(f32[64,1,128]{2,1,0:T(1,128)} %square_of.1), calls=%async_computation.3 | async-start | bytes 65536 | tf_op jit(solution)/shard_map/all_to_all | solution.py:434
  123.6 0.0 all-gather.3.cloned.1.call-done
  123.6 1.8 %copy.17 = f32[16,8,32,128]{3,2,0,1:T(8,128)S(1)} copy(f32[16,8,32,128]{3,2,1,0:T(8,128)} %bitcast.42) | data formatting | bytes 4194304 | tf_op jit(solution)/shard_map/all_gather | solution.py:406
  125.5 0.1 slice.16
  125.5 0.0 copy-start.5
  125.5 0.0 copy-start.6
  125.6 0.0 copy-start.7
  125.6 0.1 slice.14.state_ref
  125.7 7.2 %all-to-all-done.3.squares_ref = f32[64,1,128]{2,1,0:T(1,128)S(1)} async-done(((f32[64,1,128]{2,1,0:T(1,128)}), f32[64,1,128]{2,1,0:T(1,128)S(1)}, u32[]{:S(2)}, u32[]{:S(2)}) %all-to-all-start.3) | async-done | bytes 32800 | tf_op jit(solution)/shard_map/all_to_all | solution.py:434
  132.9 1.4 fresh_weights.1
  134.3 3.6 %all-to-all-start.4 = ((bf16[8,16,4096]{2,1,0:T(8,128)(2,1)}), bf16[8,16,4096]{2,1,0:T(8,128)(2,1)S(1)}, u32[]{:S(2)}, u32[]{:S(2)}) async-start(bf16[8,16,4096]{2,1,0:T(8,128)(2,1)} %get-tuple-element.32), calls=%async_computation.4 | async-start | bytes 2097152 | tf_op jit(solution)/shard_map/all_to_all | solution.py:438
  137.9 0.5 slice.15
  139.1 0.0 copy-done.5
  139.1 0.0 copy-done.6
  139.1 0.0 copy-done.7
  139.1 0.6 multiply_subtract_fusion
  139.7 13.0 %all-to-all-done.4 = bf16[8,16,4096]{2,1,0:T(8,128)(2,1)S(1)} async-done(((bf16[8,16,4096]{2,1,0:T(8,128)(2,1)}), bf16[8,16,4096]{2,1,0:T(8,128)(2,1)S(1)}, u32[]{:S(2)}, u32[]{:S(2)}) %all-to-all-start.4) | async-done | bytes 1048608 | tf_op jit(solution)/shard_map/all_to_all | solution.py:438
  152.7 2.7 %collective-permute-start.5 = (bf16[128,4096]{1,0:T(8,128)(2,1)S(1)}, bf16[128,4096]{1,0:T(8,128)(2,1)S(1)}, u32[]{:S(2)}, u32[]{:S(2)}) collective-permute-start(bf16[128,4096]{1,0:T(8,128)(2,1)S(1)} %bitcast.31), channel_id=1, source_target_pairs={{0,1},{1,0},{2,3},{3,2},{4,5},{5,4},{6,7},{7,6},{8,9},{9,8},{10,11... | collective-permute-start | bytes 3145736 | tf_op jit(solution)/shard_map/ppermute | solution.py:386
  155.4 0.1 fusion.order_ref
  155.5 1.5 place.2.refs_0_
  157.0 0.7 collective-permute-done.5.half_ref
  157.7 1.5 place.3
  (3 shorter events, 0.0 us)
Async XLA Ops:
  7.2 116.5 %all-gather.3.cloned.1.call-start = ((), (), s32[]{:S(2)}) async-start(), calls=%async_computation.5 | async-start | bytes 2228224 | tf_op jit(solution)/shard_map/all_gather | solution.py:406
  7.2 36.6 %copy-start = (bf16[128,8192]{1,0:T(8,128)(2,1)S(1)}, bf16[128,8192]{1,0:T(8,128)(2,1)}, u32[]{:S(2)}) copy-start(bf16[128,8192]{1,0:T(8,128)(2,1)} %top_ref.7) | copy-start | bytes 6291460
  12.1 36.2 %copy-start.2 = (bf16[1,128,128]{2,1,0:T(8,128)(2,1)S(1)}, bf16[1,128,128]{2,1,0:T(8,128)(2,1)}, u32[]{:S(2)}) copy-start(bf16[1,128,128]{2,1,0:T(8,128)(2,1)} %param.9) | copy-start | bytes 98308
  12.1 36.2 %collective-permute-start = (bf16[128,4224]{1,0:T(8,128)(2,1)}, bf16[128,4224]{1,0:T(8,128)(2,1)S(1)}, u32[]{:S(2)}, u32[]{:S(2)}) collective-permute-start(bf16[128,4224]{1,0:T(8,128)(2,1)} %get-tuple-element.21), channel_id=1, source_target_pairs={{0,1},{1,0},{2,3},{3,2},{4,5},{5,4},{6,7},{7,6},{8,9},{9,8},{10,11... | collective-permute-start | bytes 3244040 | tf_op jit(solution)/shard_map/ppermute | solution.py:386
  28.2 15.6 %collective-permute-start.1 = (bf16[128,512]{1,0:T(8,128)(2,1)}, bf16[128,512]{1,0:T(8,128)(2,1)S(1)}, u32[]{:S(2)}, u32[]{:S(2)}) collective-permute-start(bf16[128,512]{1,0:T(8,128)(2,1)} %get-tuple-element.25), channel_id=1, source_target_pairs={{256,0},{512,256},{768,512},{257,1},{513,257},{769,513},{258,2},{5... | collective-permute-start | bytes 393224 | tf_op jit(solution)/shard_map/ppermute | solution.py:382
  29.5 14.3 %collective-permute-start.2 = (bf16[128,384]{1,0:T(8,128)(2,1)}, bf16[128,384]{1,0:T(8,128)(2,1)S(1)}, u32[]{:S(2)}, u32[]{:S(2)}) collective-permute-start(bf16[128,384]{1,0:T(8,128)(2,1)} %get-tuple-element.26), channel_id=1, source_target_pairs={{512,0},{768,256},{513,1},{769,257},{514,2},{770,258},{515,3},{771... | collective-permute-start | bytes 294920 | tf_op jit(solution)/shard_map/ppermute | solution.py:382
  30.8 13.0 %collective-permute-start.3 = (bf16[128,256]{1,0:T(8,128)(2,1)}, bf16[128,256]{1,0:T(8,128)(2,1)S(1)}, u32[]{:S(2)}, u32[]{:S(2)}) collective-permute-start(bf16[128,256]{1,0:T(8,128)(2,1)} %get-tuple-element.27), channel_id=1, source_target_pairs={{768,0},{769,1},{770,2},{771,3},{772,4},{773,5},{774,6},{775,7},{7... | collective-permute-start | bytes 196616 | tf_op jit(solution)/shard_map/ppermute | solution.py:382
  43.8 0.8 copy-start.4
  45.9 4.8 %collective-permute-start.4 = (bf16[128,512]{1,0:T(8,128)(2,1)S(1)}, bf16[128,512]{1,0:T(8,128)(2,1)S(1)}, u32[]{:S(2)}, u32[]{:S(2)}) collective-permute-start(bf16[128,512]{1,0:T(8,128)(2,1)S(1)} %get-tuple-element.29.head_a_ref), channel_id=1, source_target_pairs={{0,1},{1,0},{2,3},{3,2},{4,5},{5,4},{6,7},{7,6},{8,9},{9,8},{10,11... | collective-permute-start | bytes 393224 | tf_op jit(solution)/shard_map/ppermute | solution.py:386
  51.0 1.0 copy-start.1
  51.9 18.8 %copy-start.3 = (f32[1,32,128]{2,1,0:T(8,128)S(1)}, f32[1,32,128]{2,1,0:T(8,128)}, u32[]{:S(2)}) copy-start(f32[1,32,128]{2,1,0:T(8,128)} %param.14) | copy-start | bytes 49156
  51.9 50.0 %copy-start.8 = (s32[4]{0:T(128)S(1)}, s32[4]{0:T(128)}, u32[]{:S(2)}) copy-start(s32[4]{0:T(128)} %param.15) | copy-start | bytes 52
  51.9 18.8 %all-to-all-start = ((bf16[8,16,4096]{2,1,0:T(8,128)(2,1)}), bf16[8,16,4096]{2,1,0:T(8,128)(2,1)S(1)}, u32[]{:S(2)}, u32[]{:S(2)}) async-start(bf16[8,16,4096]{2,1,0:T(8,128)(2,1)} %bitcast.33), calls=%async_computation | async-start | bytes 2097152 | tf_op jit(solution)/shard_map/all_to_all | solution.py:419
  94.4 19.5 %all-to-all-start.2 = ((bf16[16,16,256]{2,1,0:T(8,128)(2,1)}), bf16[16,16,256]{2,1,0:T(8,128)(2,1)S(1)}, u32[]{:S(2)}, u32[]{:S(2)}) async-start(bf16[16,16,256]{2,1,0:T(8,128)(2,1)} %fold.1), calls=%async_computation.2 | async-start | bytes 262144 | tf_op jit(solution)/shard_map/all_to_all | solution.py:429
  115.3 17.6 %all-to-all-start.3 = ((f32[64,1,128]{2,1,0:T(1,128)}), f32[64,1,128]{2,1,0:T(1,128)S(1)}, u32[]{:S(2)}, u32[]{:S(2)}) async-start(f32[64,1,128]{2,1,0:T(1,128)} %square_of.1), calls=%async_computation.3 | async-start | bytes 65536 | tf_op jit(solution)/shard_map/all_to_all | solution.py:434
  125.5 13.5 %copy-start.5 = (f32[1,32,128]{2,1,0:T(8,128)S(1)}, f32[1,32,128]{2,1,0:T(8,128)}, u32[]{:S(2)}) copy-start(f32[1,32,128]{2,1,0:T(8,128)} %param.11) | copy-start | bytes 49156
  125.5 13.5 %copy-start.6 = (f32[1,32,128]{2,1,0:T(8,128)S(1)}, f32[1,32,128]{2,1,0:T(8,128)}, u32[]{:S(2)}) copy-start(f32[1,32,128]{2,1,0:T(8,128)} %param.12) | copy-start | bytes 49156
  125.6 13.5 %copy-start.7 = (f32[1,32,128]{2,1,0:T(8,128)S(1)}, f32[1,32,128]{2,1,0:T(8,128)}, u32[]{:S(2)}) copy-start(f32[1,32,128]{2,1,0:T(8,128)} %param.13) | copy-start | bytes 49156
  134.3 18.4 %all-to-all-start.4 = ((bf16[8,16,4096]{2,1,0:T(8,128)(2,1)}), bf16[8,16,4096]{2,1,0:T(8,128)(2,1)S(1)}, u32[]{:S(2)}, u32[]{:S(2)}) async-start(bf16[8,16,4096]{2,1,0:T(8,128)(2,1)} %get-tuple-element.32), calls=%async_computation.4 | async-start | bytes 2097152 | tf_op jit(solution)/shard_map/all_to_all | solution.py:438
  152.7 5.0 %collective-permute-start.5 = (bf16[128,4096]{1,0:T(8,128)(2,1)S(1)}, bf16[128,4096]{1,0:T(8,128)(2,1)S(1)}, u32[]{:S(2)}, u32[]{:S(2)}) collective-permute-start(bf16[128,4096]{1,0:T(8,128)(2,1)S(1)} %bitcast.31), channel_id=1, source_target_pairs={{0,1},{1,0},{2,3},{3,2},{4,5},{5,4},{6,7},{7,6},{8,9},{9,8},{10,11... | collective-permute-start | bytes 3145736 | tf_op jit(solution)/shard_map/ppermute | solution.py:386
Sparse Core Ops, SparseCore 0:
  28.4 66.7 all-gather.2

commit v9 on v8

--- a/solution.py
+++ b/solution.py
@@ -404,7 +404,7 @@
         section[None], core[None], top_grad, weight, slab_own, shares, span, 4
     )
     state = lax.all_gather(state, "z", axis=0, tiled=False)
-    known_all = [known, down(one, 1), down(two, 2), down(three, 3)]
+    known_all = [known * (section >= 0).astype(f32), down(one, 1), down(two, 2), down(three, 3)]
     other = swap(sent, "core")
     w_head = lax.optimization_barrier((weight, known))[0][:, :span]
 

time: 167 us -> 166 us (level)
  no operation moved by 1% of the time
where the time goes in v9:
time: 166 us; the launch traced here: 165 us
  waiting for transfers between devices  57.1 us (34%)
  starting transfers between devices  47.4 us (29%)
  blocking collectives  23.4 us (14%)
  Pallas kernels  15.3 us (9%)
  between operations  15 us (9%)
  local copies, waits for them, and re-layouts  5.04 us (3%)
  other arithmetic  1.7 us (1%)
    all_to_all x1, blocking collectives, local(): parts = lax.all_to_all(parts, 'z', split_axis=0, concat_axis=0, tiled=True)  23.4 us
    ppermute x3, starting transfers between devices, swap(): return lax.ppermute(x, axis, [(0, 1), (1, 0)])  21.1 us
    all_to_all x1, waiting for transfers between devices, local(): lax.all_to_all(product, ('y', 'x'), split_axis=0, concat_axis=0, tiled=True)  14.9 us
    all_to_all x1, waiting for transfers between devices, local(): lax.all_to_all(fresh, ('y', 'x'), split_axis=0, concat_axis=0, tiled=True)  13 us
    all_to_all x1, waiting for transfers between devices, local(): lax.all_to_all(fold(parts), 'z', split_axis=0, concat_axis=0, tiled=True)  11.4 us
    ppermute x3, waiting for transfers between devices, down(): return lax.ppermute(x, 'pipe', [(i, i - by) for i in range(by, 4)])  9.9 us
    all_to_all x1, starting transfers between devices, local(): lax.all_to_all(squares, group, split_axis=0, concat_axis=0, tiled=True)  7.9 us
    all_to_all x1, waiting for transfers between devices, local(): lax.all_to_all(squares, group, split_axis=0, concat_axis=0, tiled=True)  7.19 us
  transfers between devices with their start and end apart: 11, of which 6 were waited for; matrix products, arithmetic and copies ran while one was open for 3% of the time, Pallas kernels for 5%

profile of v9, /device:TPU:1, one launch (start us, length us, event | category | flops | bytes accessed | tf_op | source)
XLA Modules:
  0.0 165.0 jit_solution(3373463724884093690)
XLA Ops:
  7.2 0.0 all-gather.3.cloned.1.call-start
  7.2 0.0 copy-start
  7.2 4.9 %known_part.1 = (f32[128,128]{1,0:T(8,128)}, bf16[128,512]{1,0:T(8,128)(2,1)}, bf16[128,384]{1,0:T(8,128)(2,1)}, bf16[128,256]{1,0:T(8,128)(2,1)}, bf16[128,4224]{1,0:T(8,128)(2,1)}, /*index=5*/f32[8,32,128]{2,1,0:T(8,128)}) custom-call(s32[1]{0:T(128)} %bitcast.4.section_ref, s32[1]{0:T(128)} %bitcast.core_ref.side_ref, bf16[128,8192]{1,0:T(8,128)(2,1)} %top_ref.7, ...), custom_call_target="tpu_custom_call" | custom-call | tf_op jit(solution)/shard_map/known_part/pallas_call | solution.py:87
  12.1 0.0 copy-start.2
  12.1 16.1 %collective-permute-start = (bf16[128,4224]{1,0:T(8,128)(2,1)}, bf16[128,4224]{1,0:T(8,128)(2,1)S(1)}, u32[]{:S(2)}, u32[]{:S(2)}) collective-permute-start(bf16[128,4224]{1,0:T(8,128)(2,1)} %get-tuple-element.21), channel_id=1, source_target_pairs={{0,1},{1,0},{2,3},{3,2},{4,5},{5,4},{6,7},{7,6},{8,9},{9,8},{10,11... | collective-permute-start | bytes 3244040 | tf_op jit(solution)/shard_map/ppermute | solution.py:386
  28.2 0.0 all-gather.3.cloned.1.call-update
  28.2 1.3 collective-permute-start.1
  29.5 1.3 collective-permute-start.2
  30.8 1.3 collective-permute-start.3
  32.1 0.8 broadcast_multiply_fusion.own_ref
  33.0 0.9 slice.12.w_own_ref
  33.9 9.9 %collective-permute-done.3.three_ref = bf16[128,256]{1,0:T(8,128)(2,1)S(1)} collective-permute-done((bf16[128,256]{1,0:T(8,128)(2,1)}, bf16[128,256]{1,0:T(8,128)(2,1)S(1)}, u32[]{:S(2)}, u32[]{:S(2)}) %collective-permute-start.3) | collective-permute-done | bytes 65568 | tf_op jit(solution)/shard_map/ppermute | solution.py:382
  43.8 0.0 collective-permute-done.2.two_ref
  43.8 0.0 collective-permute-done.1.one_ref
  43.8 0.0 copy-done
  43.8 1.3 relay.1
  45.0 2.4 %collective-permute-start.4 = (bf16[128,512]{1,0:T(8,128)(2,1)S(1)}, bf16[128,512]{1,0:T(8,128)(2,1)S(1)}, u32[]{:S(2)}, u32[]{:S(2)}) collective-permute-start(bf16[128,512]{1,0:T(8,128)(2,1)S(1)} %get-tuple-element.29.head_a_ref), channel_id=1, source_target_pairs={{0,1},{1,0},{2,3},{3,2},{4,5},{5,4},{6,7},{7,6},{8,9},{9,8},{10,11... | collective-permute-start | bytes 393224 | tf_op jit(solution)/shard_map/ppermute | solution.py:386
  47.4 0.1 fusion.1.order_ref
  47.5 0.0 collective-permute-done.slab_b_ref.other_ref
  47.5 0.0 copy-done.2
  47.5 2.3 %tail_product.1 = (bf16[128,4096]{1,0:T(8,128)(2,1)S(1)}, bf16[128,128]{1,0:T(8,128)(2,1)S(1)}, bf16[128,128]{1,0:T(8,128)(2,1)S(1)}) custom-call(s32[1]{0:T(128)} %bitcast.core_ref.side_ref, bf16[128,128]{1,0:T(8,128)(2,1)S(1)} %fusion.1.order_ref, bf16[128,128]{1,0:T(8,128)(2,1)S(1)} %bitcast.35, ...), custom_call_target="tpu_custom_call" | custom-call | tf_op jit(solution)/shard_map/tail_product/pallas_call | solution.py:187
  49.9 0.0 collective-permute-done.4.head_b_ref
  49.9 0.2 head_product.1
  50.1 0.0 copy-start.1
  50.1 1.0 copy-done.1
  51.1 0.0 copy-start.3
  51.1 0.0 copy-start.7
  51.1 3.7 %all-to-all-start = ((bf16[8,16,4096]{2,1,0:T(8,128)(2,1)}), bf16[8,16,4096]{2,1,0:T(8,128)(2,1)S(1)}, u32[]{:S(2)}, u32[]{:S(2)}) async-start(bf16[8,16,4096]{2,1,0:T(8,128)(2,1)} %bitcast.33), calls=%async_computation | async-start | bytes 2097152 | tf_op jit(solution)/shard_map/all_to_all | solution.py:419
  54.8 14.9 %all-to-all-done.parts_ref = bf16[8,16,4096]{2,1,0:T(8,128)(2,1)S(1)} async-done(((bf16[8,16,4096]{2,1,0:T(8,128)(2,1)}), bf16[8,16,4096]{2,1,0:T(8,128)(2,1)S(1)}, u32[]{:S(2)}, u32[]{:S(2)}) %all-to-all-start) | async-done | bytes 1048608 | tf_op jit(solution)/shard_map/all_to_all | solution.py:419
  69.8 0.0 copy-done.3
  69.8 0.2 fold_chunks.1
  69.9 23.4 %all_to_all.29.parts_ref = bf16[16,16,256]{2,1,0:T(8,128)(2,1)S(1)} all-to-all(bf16[16,16,256]{2,1,0:T(8,128)(2,1)S(1)} %fold_chunks.1), channel_id=1, replica_groups=mesh['pipe'=4,'y'=2,'z'=16,'x'=4,'core'=2] {'z'}, dimensions={0} | all-to-all | bytes 262144 | tf_op jit(solution)/shard_map/all_to_all | solution.py:428
  93.4 0.7 fold.1
  94.0 7.2 %all-to-all-start.2 = ((bf16[16,16,256]{2,1,0:T(8,128)(2,1)}), bf16[16,16,256]{2,1,0:T(8,128)(2,1)S(1)}, u32[]{:S(2)}, u32[]{:S(2)}) async-start(bf16[16,16,256]{2,1,0:T(8,128)(2,1)} %fold.1), calls=%async_computation.2 | async-start | bytes 262144 | tf_op jit(solution)/shard_map/all_to_all | solution.py:429
  101.2 0.0 copy-done.7
  101.2 0.6 dynamic_slice.6.count_ref
  101.8 11.4 %all-to-all-done.2.sums_ref = bf16[16,16,256]{2,1,0:T(8,128)(2,1)S(1)} async-done(((bf16[16,16,256]{2,1,0:T(8,128)(2,1)}), bf16[16,16,256]{2,1,0:T(8,128)(2,1)S(1)}, u32[]{:S(2)}, u32[]{:S(2)}) %all-to-all-start.2) | async-done | bytes 131104 | tf_op jit(solution)/shard_map/all_to_all | solution.py:429
  113.2 1.4 square_of.1
  114.7 7.9 %all-to-all-start.3 = ((f32[64,1,128]{2,1,0:T(1,128)}), f32[64,1,128]{2,1,0:T(1,128)S(1)}, u32[]{:S(2)}, u32[]{:S(2)}) async-start(f32[64,1,128]{2,1,0:T(1,128)} %square_of.1), calls=%async_computation.3 | async-start | bytes 65536 | tf_op jit(solution)/shard_map/all_to_all | solution.py:434
  122.6 0.0 all-gather.3.cloned.1.call-done
  122.6 1.8 %copy.17 = f32[16,8,32,128]{3,2,0,1:T(8,128)S(1)} copy(f32[16,8,32,128]{3,2,1,0:T(8,128)} %bitcast.42) | data formatting | bytes 4194304 | tf_op jit(solution)/shard_map/all_gather | solution.py:406
  124.4 0.1 slice.16
  124.5 0.0 copy-start.4
  124.5 0.0 copy-start.5
  124.5 0.0 copy-start.6
  124.5 0.1 slice.14.state_ref
  124.7 7.2 %all-to-all-done.3.squares_ref = f32[64,1,128]{2,1,0:T(1,128)S(1)} async-done(((f32[64,1,128]{2,1,0:T(1,128)}), f32[64,1,128]{2,1,0:T(1,128)S(1)}, u32[]{:S(2)}, u32[]{:S(2)}) %all-to-all-start.3) | async-done | bytes 32800 | tf_op jit(solution)/shard_map/all_to_all | solution.py:434
  131.9 1.4 fresh_weights.1
  133.2 3.6 %all-to-all-start.4 = ((bf16[8,16,4096]{2,1,0:T(8,128)(2,1)}), bf16[8,16,4096]{2,1,0:T(8,128)(2,1)S(1)}, u32[]{:S(2)}, u32[]{:S(2)}) async-start(bf16[8,16,4096]{2,1,0:T(8,128)(2,1)} %get-tuple-element.32), calls=%async_computation.4 | async-start | bytes 2097152 | tf_op jit(solution)/shard_map/all_to_all | solution.py:438
  136.8 0.5 slice.15
  138.0 0.0 copy-done.4
  138.0 0.0 copy-done.5
  138.0 0.0 copy-done.6
  138.0 0.6 multiply_subtract_fusion
  138.7 13.0 %all-to-all-done.4 = bf16[8,16,4096]{2,1,0:T(8,128)(2,1)S(1)} async-done(((bf16[8,16,4096]{2,1,0:T(8,128)(2,1)}), bf16[8,16,4096]{2,1,0:T(8,128)(2,1)S(1)}, u32[]{:S(2)}, u32[]{:S(2)}) %all-to-all-start.4) | async-done | bytes 1048608 | tf_op jit(solution)/shard_map/all_to_all | solution.py:438
  151.7 2.7 %collective-permute-start.5 = (bf16[128,4096]{1,0:T(8,128)(2,1)S(1)}, bf16[128,4096]{1,0:T(8,128)(2,1)S(1)}, u32[]{:S(2)}, u32[]{:S(2)}) collective-permute-start(bf16[128,4096]{1,0:T(8,128)(2,1)S(1)} %bitcast.31), channel_id=1, source_target_pairs={{0,1},{1,0},{2,3},{3,2},{4,5},{5,4},{6,7},{7,6},{8,9},{9,8},{10,11... | collective-permute-start | bytes 3145736 | tf_op jit(solution)/shard_map/ppermute | solution.py:386
  154.4 0.1 fusion.order_ref
  154.5 1.5 place.2.refs_0_
  156.0 0.7 collective-permute-done.5.half_ref
  156.7 1.5 place.3
  (3 shorter events, 0.0 us)
Async XLA Ops:
  7.2 115.4 %all-gather.3.cloned.1.call-start = ((), (), s32[]{:S(2)}) async-start(), calls=%async_computation.5 | async-start | bytes 2228224 | tf_op jit(solution)/shard_map/all_gather | solution.py:406
  7.2 36.6 %copy-start = (bf16[128,8192]{1,0:T(8,128)(2,1)S(1)}, bf16[128,8192]{1,0:T(8,128)(2,1)}, u32[]{:S(2)}) copy-start(bf16[128,8192]{1,0:T(8,128)(2,1)} %top_ref.7) | copy-start | bytes 6291460
  12.1 35.4 %copy-start.2 = (bf16[1,128,128]{2,1,0:T(8,128)(2,1)S(1)}, bf16[1,128,128]{2,1,0:T(8,128)(2,1)}, u32[]{:S(2)}) copy-start(bf16[1,128,128]{2,1,0:T(8,128)(2,1)} %param.9) | copy-start | bytes 98308
  12.1 35.4 %collective-permute-start = (bf16[128,4224]{1,0:T(8,128)(2,1)}, bf16[128,4224]{1,0:T(8,128)(2,1)S(1)}, u32[]{:S(2)}, u32[]{:S(2)}) collective-permute-start(bf16[128,4224]{1,0:T(8,128)(2,1)} %get-tuple-element.21), channel_id=1, source_target_pairs={{0,1},{1,0},{2,3},{3,2},{4,5},{5,4},{6,7},{7,6},{8,9},{9,8},{10,11... | collective-permute-start | bytes 3244040 | tf_op jit(solution)/shard_map/ppermute | solution.py:386
  28.2 15.6 %collective-permute-start.1 = (bf16[128,512]{1,0:T(8,128)(2,1)}, bf16[128,512]{1,0:T(8,128)(2,1)S(1)}, u32[]{:S(2)}, u32[]{:S(2)}) collective-permute-start(bf16[128,512]{1,0:T(8,128)(2,1)} %get-tuple-element.25), channel_id=1, source_target_pairs={{256,0},{512,256},{768,512},{257,1},{513,257},{769,513},{258,2},{5... | collective-permute-start | bytes 393224 | tf_op jit(solution)/shard_map/ppermute | solution.py:382
  29.5 14.3 %collective-permute-start.2 = (bf16[128,384]{1,0:T(8,128)(2,1)}, bf16[128,384]{1,0:T(8,128)(2,1)S(1)}, u32[]{:S(2)}, u32[]{:S(2)}) collective-permute-start(bf16[128,384]{1,0:T(8,128)(2,1)} %get-tuple-element.26), channel_id=1, source_target_pairs={{512,0},{768,256},{513,1},{769,257},{514,2},{770,258},{515,3},{771... | collective-permute-start | bytes 294920 | tf_op jit(solution)/shard_map/ppermute | solution.py:382
  30.8 13.0 %collective-permute-start.3 = (bf16[128,256]{1,0:T(8,128)(2,1)}, bf16[128,256]{1,0:T(8,128)(2,1)S(1)}, u32[]{:S(2)}, u32[]{:S(2)}) collective-permute-start(bf16[128,256]{1,0:T(8,128)(2,1)} %get-tuple-element.27), channel_id=1, source_target_pairs={{768,0},{769,1},{770,2},{771,3},{772,4},{773,5},{774,6},{775,7},{7... | collective-permute-start | bytes 196616 | tf_op jit(solution)/shard_map/ppermute | solution.py:382
  45.0 4.8 %collective-permute-start.4 = (bf16[128,512]{1,0:T(8,128)(2,1)S(1)}, bf16[128,512]{1,0:T(8,128)(2,1)S(1)}, u32[]{:S(2)}, u32[]{:S(2)}) collective-permute-start(bf16[128,512]{1,0:T(8,128)(2,1)S(1)} %get-tuple-element.29.head_a_ref), channel_id=1, source_target_pairs={{0,1},{1,0},{2,3},{3,2},{4,5},{5,4},{6,7},{7,6},{8,9},{9,8},{10,11... | collective-permute-start | bytes 393224 | tf_op jit(solution)/shard_map/ppermute | solution.py:386
  50.1 1.0 copy-start.1
  51.1 18.7 %copy-start.3 = (f32[1,32,128]{2,1,0:T(8,128)S(1)}, f32[1,32,128]{2,1,0:T(8,128)}, u32[]{:S(2)}) copy-start(f32[1,32,128]{2,1,0:T(8,128)} %param.14) | copy-start | bytes 49156
  51.1 50.1 %copy-start.7 = (s32[4]{0:T(128)S(1)}, s32[4]{0:T(128)}, u32[]{:S(2)}) copy-start(s32[4]{0:T(128)} %param.15) | copy-start | bytes 52
  51.1 18.7 %all-to-all-start = ((bf16[8,16,4096]{2,1,0:T(8,128)(2,1)}), bf16[8,16,4096]{2,1,0:T(8,128)(2,1)S(1)}, u32[]{:S(2)}, u32[]{:S(2)}) async-start(bf16[8,16,4096]{2,1,0:T(8,128)(2,1)} %bitcast.33), calls=%async_computation | async-start | bytes 2097152 | tf_op jit(solution)/shard_map/all_to_all | solution.py:419
  94.0 19.2 %all-to-all-start.2 = ((bf16[16,16,256]{2,1,0:T(8,128)(2,1)}), bf16[16,16,256]{2,1,0:T(8,128)(2,1)S(1)}, u32[]{:S(2)}, u32[]{:S(2)}) async-start(bf16[16,16,256]{2,1,0:T(8,128)(2,1)} %fold.1), calls=%async_computation.2 | async-start | bytes 262144 | tf_op jit(solution)/shard_map/all_to_all | solution.py:429
  114.7 17.2 %all-to-all-start.3 = ((f32[64,1,128]{2,1,0:T(1,128)}), f32[64,1,128]{2,1,0:T(1,128)S(1)}, u32[]{:S(2)}, u32[]{:S(2)}) async-start(f32[64,1,128]{2,1,0:T(1,128)} %square_of.1), calls=%async_computation.3 | async-start | bytes 65536 | tf_op jit(solution)/shard_map/all_to_all | solution.py:434
  124.5 13.5 %copy-start.4 = (f32[1,32,128]{2,1,0:T(8,128)S(1)}, f32[1,32,128]{2,1,0:T(8,128)}, u32[]{:S(2)}) copy-start(f32[1,32,128]{2,1,0:T(8,128)} %param.11) | copy-start | bytes 49156
  124.5 13.5 %copy-start.5 = (f32[1,32,128]{2,1,0:T(8,128)S(1)}, f32[1,32,128]{2,1,0:T(8,128)}, u32[]{:S(2)}) copy-start(f32[1,32,128]{2,1,0:T(8,128)} %param.12) | copy-start | bytes 49156
  124.5 13.5 %copy-start.6 = (f32[1,32,128]{2,1,0:T(8,128)S(1)}, f32[1,32,128]{2,1,0:T(8,128)}, u32[]{:S(2)}) copy-start(f32[1,32,128]{2,1,0:T(8,128)} %param.13) | copy-start | bytes 49156
  133.2 18.4 %all-to-all-start.4 = ((bf16[8,16,4096]{2,1,0:T(8,128)(2,1)}), bf16[8,16,4096]{2,1,0:T(8,128)(2,1)S(1)}, u32[]{:S(2)}, u32[]{:S(2)}) async-start(bf16[8,16,4096]{2,1,0:T(8,128)(2,1)} %get-tuple-element.32), calls=%async_computation.4 | async-start | bytes 2097152 | tf_op jit(solution)/shard_map/all_to_all | solution.py:438
  151.7 5.0 %collective-permute-start.5 = (bf16[128,4096]{1,0:T(8,128)(2,1)S(1)}, bf16[128,4096]{1,0:T(8,128)(2,1)S(1)}, u32[]{:S(2)}, u32[]{:S(2)}) collective-permute-start(bf16[128,4096]{1,0:T(8,128)(2,1)S(1)} %bitcast.31), channel_id=1, source_target_pairs={{0,1},{1,0},{2,3},{3,2},{4,5},{5,4},{6,7},{7,6},{8,9},{9,8},{10,11... | collective-permute-start | bytes 3145736 | tf_op jit(solution)/shard_map/ppermute | solution.py:386
Sparse Core Ops, SparseCore 0:
  28.3 66.0 all-gather.2
